TPU v7x, 32 devices: a whole 2x2x4 slice. The times are simulated.
32 devices in a mesh: seq: 8 (over y, x, core), head: 4 (over z).
Axes of the slice: x: 2, y: 2, z: 4, core: 2. Of those that a mesh axis runs over, the one named last changes fastest.
Arguments:
- queries: bfloat16 [2048, 2560], P('seq', 'head'), may hold values from -16 to 16
- keys: bfloat16 [2048, 2560], P('seq', 'head'), may hold values from -16 to 16
- values: bfloat16 [2048, 2560], P('seq', 'head'), may hold values from -6 to 6
- grad_out: bfloat16 [2048, 2560], P(('seq', 'head')), may hold values from -6 to 6
Outputs:
- grad_queries: bfloat16 [2048, 2560], P('seq', 'head')
- grad_keys: bfloat16 [2048, 2560], P('seq', 'head')
- grad_values: bfloat16 [2048, 2560], P('seq', 'head')
All inputs are finite; a program needn't handle non-finite values.
Results may differ from a plain program's by a relative error of at most 0.0079.
Values may be sent and summed in bfloat16 or wider, within the bound.
No kernel may reach another device: no remote copies, remote signals or barrier semaphores. Data moves between devices by JAX's collectives and lax.ppermute only.
A program may use at most 64 MiB of HBM per device.

v0:
```python
import jax
import jax.numpy as jnp
from jax import lax
from jax.sharding import PartitionSpec as P

HD = 80
LEVEL1_SPAN = 4
LEVEL1_DILATION = 4


def from_partner(block, axis, apart):
    count = lax.axis_size(axis)
    route = []
    for low in range(count):
        high = low | 1 << apart
        if high != low and high < count:
            route += [(low, high), (high, low)]
    return lax.ppermute(block, axis, route)


def lane_mask(heads_local, stride):
    first_head = lax.axis_index("head") * heads_local
    labels = first_head + jnp.arange(heads_local, dtype=jnp.int32)
    lanes = jnp.arange(stride, dtype=jnp.int32)
    return lanes[:, None] == (labels % stride)[None, :]


def pick_level(field, stride, chosen):
    if stride == 1:
        return field
    shaped = field.reshape((field.shape[0] // stride, stride) + field.shape[1:])
    kept = jnp.where(chosen[None, :, :, None], shaped, jnp.zeros((), field.dtype))
    return jnp.sum(kept, axis=1, dtype=field.dtype)


def spread_level(sparse, stride, chosen, fill):
    if stride == 1:
        return sparse
    widened = jnp.where(chosen[None, :, :, None], sparse[:, None], fill)
    return widened.reshape((sparse.shape[0] * stride,) + sparse.shape[1:])


def masked_scores(query_rows, key_rows, first_query, scale):
    scores = (
        jnp.einsum("ihd,jhd->hij", query_rows, key_rows, preferred_element_type=jnp.float32) * scale
    )
    query_index = first_query + jnp.arange(query_rows.shape[0], dtype=jnp.int32)
    key_index = jnp.arange(key_rows.shape[0], dtype=jnp.int32)
    later = query_index[:, None] >= key_index[None, :]
    return jnp.where(later[None], scores, -jnp.inf)


def swap_pairs(blocks, bit_index):
    return (from_partner(blocks[0], "seq", bit_index),)


def swap_grads(block, bit_index):
    return from_partner(block, "seq", bit_index)


def group_gather(pieces, group_size, sender):
    position = lax.axis_index("seq") % group_size
    section_count = group_size.bit_length() - 1
    sequence = list(range(section_count))
    blocks = tuple((piece[None] for piece in pieces))
    for bit_index in sequence:
        arrived = sender(blocks, bit_index)
        upper = position // 2**bit_index % 2 == 1
        joined = []
        for own_block, other_block in zip(blocks, arrived):
            lower_half = jnp.where(upper, other_block, own_block)
            upper_half = jnp.where(upper, own_block, other_block)
            stacked = jnp.stack((lower_half, upper_half), axis=0)
            joined.append(stacked.reshape((-1,) + own_block.shape[1:]))
        blocks = tuple(joined)
    return tuple((block.reshape((-1,) + block.shape[2:]) for block in blocks))


def group_reduce(term, group_size, sender):
    position = lax.axis_index("seq") % group_size
    section_count = group_size.bit_length() - 1
    sequence = list(range(section_count))
    blocks = term.reshape((group_size, -1) + term.shape[1:])
    for bit_index in sequence:
        upper = position // 2**bit_index % 2 == 1
        block_count = blocks.shape[0]
        halves = blocks.reshape((block_count // 2, 2) + blocks.shape[1:])
        lower_blocks, upper_blocks = (halves[:, 0], halves[:, 1])
        kept = jnp.where(upper, upper_blocks, lower_blocks)
        given = jnp.where(upper, lower_blocks, upper_blocks)
        blocks = kept + sender(given, bit_index)
    return blocks[0]


def body(queries, keys, values, grad_out):
    heads_local = queries.shape[1] // HD
    tokens_here = queries.shape[0]
    broadest_level = min(32, lax.axis_size("seq"))
    scale = HD ** (-0.5)
    grads_here = lax.all_to_all(grad_out, "head", split_axis=1, concat_axis=0, tiled=True)
    fields = [
        field.reshape(tokens_here, heads_local, HD) for field in (queries, keys, values, grads_here)
    ]
    layout_recipe = ((1, 1), (LEVEL1_SPAN, LEVEL1_DILATION), (broadest_level, broadest_level))
    levels = []
    lse_rows = []
    for group_size, stride in layout_recipe:
        chosen = lane_mask(heads_local, stride)
        picks = [pick_level(field, stride, chosen) for field in fields]
        row_count = picks[0].shape[0]
        first_row = lax.axis_index("seq") % group_size * row_count
        if group_size > 1:
            pair = jnp.stack((picks[1], picks[2]), axis=1).reshape(row_count, 2, heads_local * HD)
            gathered = group_gather((pair,), group_size, swap_pairs)[0]
            gathered = gathered.reshape(group_size * row_count, 2, heads_local, HD)
            key_rows, value_rows = (gathered[:, 0], gathered[:, 1])
        else:
            key_rows, value_rows = (picks[1], picks[2])
        scores = masked_scores(picks[0], key_rows, first_row, scale)
        top = jnp.max(scores, axis=2)
        lse = top + jnp.log(jnp.sum(jnp.exp(scores - top[:, :, None]), axis=2))
        lse_rows.append(spread_level(lse.T[:, :, None], stride, chosen, -jnp.inf)[:, :, 0])
        levels.append((group_size, stride, chosen, picks, key_rows, value_rows, first_row, scores))
    stacked = jnp.stack(lse_rows)
    peak = jnp.max(stacked, axis=0)
    total = peak + jnp.log(jnp.sum(jnp.exp(stacked - peak[None]), axis=0))
    merged = jnp.zeros((tokens_here, heads_local, HD), jnp.float32)
    level_probs = []
    for group_size, stride, chosen, picks, key_rows, value_rows, first_row, scores in levels:
        level_total = pick_level(total[:, :, None], stride, chosen)[:, :, 0]
        prob = jnp.exp(scores - level_total.T[:, :, None])
        weight = prob.astype(jnp.bfloat16)
        partial_out = jnp.einsum(
            "hij,jhd->ihd", weight, value_rows, preferred_element_type=jnp.float32
        )
        merged = merged + spread_level(partial_out, stride, chosen, 0.0)
        level_probs.append((level_total, prob, weight))
    delta = jnp.sum(fields[3].astype(jnp.float32) * merged, axis=2)
    grad_q = jnp.zeros((tokens_here, heads_local, HD), jnp.float32)
    grad_k = jnp.zeros((tokens_here, heads_local, HD), jnp.float32)
    grad_v = jnp.zeros((tokens_here, heads_local, HD), jnp.float32)
    for level_info, prob_info in zip(levels, level_probs):
        group_size, stride, chosen, picks, key_rows, value_rows, first_row, scores = level_info
        level_total, prob, weight = prob_info
        level_delta = pick_level(delta[:, :, None], stride, chosen)[:, :, 0]
        dprob = jnp.einsum("ihd,jhd->hij", picks[3], value_rows, preferred_element_type=jnp.float32)
        dscore = (prob * (dprob - level_delta.T[:, :, None]) * scale).astype(jnp.bfloat16)
        query_grad = jnp.einsum(
            "hij,jhd->ihd", dscore, key_rows, preferred_element_type=jnp.float32
        )
        grad_q = grad_q + spread_level(query_grad, stride, chosen, 0.0)
        if group_size == 1:
            grad_k = jnp.einsum(
                "hij,ihd->jhd", dscore, picks[0], preferred_element_type=jnp.float32
            )
            grad_v = jnp.einsum(
                "hij,ihd->jhd", weight, picks[3], preferred_element_type=jnp.float32
            )
        else:
            key_part = jnp.einsum(
                "hij,ihd->jhd", dscore, picks[0], preferred_element_type=jnp.float32
            )
            value_part = jnp.einsum(
                "hij,ihd->jhd", weight, picks[3], preferred_element_type=jnp.float32
            )
            term = jnp.stack((key_part, value_part), axis=1).reshape(
                key_part.shape[0], 2, heads_local * HD
            )
            owned = group_reduce(term, group_size, swap_grads).reshape(-1, 2, heads_local, HD)
            grad_k = grad_k + spread_level(owned[:, 0], stride, chosen, 0.0)
            grad_v = grad_v + spread_level(owned[:, 1], stride, chosen, 0.0)
    width_here = heads_local * HD
    return (
        grad_q.astype(jnp.bfloat16).reshape(tokens_here, width_here),
        grad_k.astype(jnp.bfloat16).reshape(tokens_here, width_here),
        grad_v.astype(jnp.bfloat16).reshape(tokens_here, width_here),
    )


def solution(mesh):
    return jax.shard_map(
        body,
        mesh=mesh,
        in_specs=(P("seq", "head"), P("seq", "head"), P("seq", "head"), P(("seq", "head"), None)),
        out_specs=(P("seq", "head"), P("seq", "head"), P("seq", "head")),
        check_vma=False,
    )
```

profile of v0, /device:TPU:0, one launch (start us, length us, event | category | flops | bytes accessed | tf_op | source)
XLA Modules:
  0.0 203.6 jit_solution(2434175722664797837)
XLA Ops:
  2.4 6.3 %all-to-all-start = ((bf16[64,4,640]{2,0,1:T(8,128)(2,1)}), bf16[64,4,640]{2,0,1:T(8,128)(2,1)S(1)}, u32[]{:S(2)}, u32[]{:S(2)}) async-start(bf16[64,4,640]{2,0,1:T(8,128)(2,1)} %bitcast.304), calls=%async_computation | async-start | bytes 655360 | tf_op jit(solution)/shard_map/all_to_all | solution.py:100
  16.6 2.4 %reshape_reshape.27 = bf16[32,8,8,80]{3,2,1,0:T(8,128)(2,1)} reshape(bf16[256,640]{1,0:T(8,128)(2,1)} %param.4) | data formatting | bytes 655360 | tf_op jit(solution)/shard_map/reshape;reshape | solution.py:31
  21.7 2.3 %reshape_reshape.24 = bf16[64,4,8,80]{3,2,1,0:T(8,128)(2,1)} reshape(bf16[256,640]{1,0:T(8,128)(2,1)} %param.4) | data formatting | bytes 655360 | tf_op jit(solution)/shard_map/reshape;reshape | solution.py:31
  30.4 3.1 %select_reduce_fusion = (bf16[32,8,80]{2,1,0:T(8,128)(2,1)}, bf16[32,8,80]{2,1,0:T(8,128)(2,1)S(1)}, bf16[32,8,80]{2,1,0:T(8,128)(2,1)S(1)}, bf16[32,8,80]{2,1,0:T(8,128)(2,1)}) fusion(bf16[32,8,8,80]{3,2,1,0:T(8,128)(2,1)} %reshape_reshape.31, pred[8,8]{1,0:T(8,128)(4,1)S(1)} %copy-done.38, bf16[32,8,8,80]{3,2,1,0:T(8,128)(2,1)} %reshape_reshape.28, ...), kind=kLoop, calls=%fused_computation.53 | loop fusion | flops 1228800 | bytes 1474624 | tf_op jit(solution)/shard_map/reduce_sum | solution.py:33
  35.0 2.8 %select_reduce_fusion.1 = (bf16[64,8,80]{2,1,0:T(8,128)(2,1)}, bf16[64,8,80]{2,1,0:T(8,128)(2,1)S(1)}, bf16[64,8,80]{2,1,0:T(8,128)(2,1)S(1)}, bf16[64,8,80]{2,1,0:T(8,128)(2,1)}) fusion(bf16[64,4,8,80]{3,2,1,0:T(8,128)(2,1)} %reshape_reshape.30, pred[4,8]{1,0:T(4,128)(4,1)S(1)} %copy-done.41, bf16[64,4,8,80]{3,2,1,0:T(8,128)(2,1)S(1)} %copy-done.19, ...), kind=kLoop, calls=%fused_computation.54 | loop fusion | flops 1146880 | bytes 1638432 | tf_op jit(solution)/shard_map/reduce_sum | solution.py:33
  41.9 4.9 %collective-permute-done.3 = bf16[2,32,2,640]{3,1,2,0:T(8,128)(2,1)S(1)} collective-permute-done((bf16[2,32,2,640]{3,1,2,0:T(8,128)(2,1)S(1)}, bf16[2,32,2,640]{3,1,2,0:T(8,128)(2,1)S(1)}, u32[]{:S(2)}, u32[]{:S(2)}) %collective-permute-start.3) | collective-permute-done | bytes 163872 | tf_op jit(solution)/shard_map/ppermute | solution.py:18
  49.3 3.6 %collective-permute-done.1 = bf16[2,64,2,640]{3,1,2,0:T(8,128)(2,1)S(1)} collective-permute-done((bf16[2,64,2,640]{3,1,2,0:T(8,128)(2,1)S(1)}, bf16[2,64,2,640]{3,1,2,0:T(8,128)(2,1)S(1)}, u32[]{:S(2)}, u32[]{:S(2)}) %collective-permute-start.1) | collective-permute-done | bytes 327712 | tf_op jit(solution)/shard_map/ppermute | solution.py:18
  53.9 3.8 %copy.231 = bf16[2,2,64,2,640]{2,1,0,4,3:T(2,128)(2,1)} copy(bf16[2,2,64,2,640]{4,2,3,1,0:T(8,128)(2,1)} %pad_maximum_fusion) | data formatting | bytes 1310720 | tf_op jit(solution)/shard_map/reshape;reshape;reshape | solution.py:115
  57.7 3.9 %reshape.592 = bf16[256,2,8,80]{0,3,2,1:T(8,128)(2,1)} reshape(bf16[2,2,64,2,640]{2,1,0,4,3:T(2,128)(2,1)} %copy.231) | data formatting | bytes 1310720 | tf_op jit(solution)/shard_map/reshape;reshape;reshape | solution.py:115
  67.5 3.0 %reshape_reshape_reshape.9 = bf16[256,2,8,80]{3,2,0,1:T(8,128)(2,1)} reshape(bf16[2,4,32,2,640]{4,2,1,0,3:T(8,128)(2,1)} %pad_maximum_fusion.1) | data formatting | bytes 1310720 | tf_op jit(solution)/shard_map/reshape;reshape;reshape | solution.py:115
  70.5 2.3 %fusion.59 = (bf16[256,1,8,80]{3,2,0,1:T(8,128)(2,1)}, bf16[256,1,8,80]{3,2,0,1:T(8,128)(2,1)}) fusion(bf16[256,2,8,80]{3,2,0,1:T(8,128)(2,1)} %reshape_reshape_reshape.9), kind=kLoop, calls=%fused_computation.151 | loop fusion | bytes 1310720 | tf_op jit(solution)/shard_map/slice | solution.py:116
  72.8 2.0 %copy.233 = bf16[256,1,8,80]{0,3,2,1:T(8,128)(2,1)} copy(bf16[256,1,8,80]{3,2,0,1:T(8,128)(2,1)} %get-tuple-element.22) | data formatting | bytes 655360
  90.7 2.0 %copy.234 = bf16[256,1,8,80]{0,3,2,1:T(8,128)(2,1)} copy(bf16[256,1,8,80]{3,2,0,1:T(8,128)(2,1)} %get-tuple-element.23) | data formatting | bytes 655360
  97.0 2.4 %copy.174 = f32[256,8,80]{0,2,1:T(8,128)} copy(f32[256,8,80]{2,1,0:T(8,128)} %bitcast.310) | data formatting | bytes 1310720 | tf_op jit(solution)/shard_map/jit(_where)/broadcast_in_dim | solution.py:39
  105.2 2.4 %copy.170 = f32[256,8,80]{0,2,1:T(8,128)} copy(f32[256,8,80]{2,1,0:T(8,128)} %bitcast.311) | data formatting | bytes 1310720 | tf_op jit(solution)/shard_map/jit(_where)/broadcast_in_dim | solution.py:39
  111.7 2.0 convolution_bitcast_fusion.8
  122.6 2.4 %copy.202 = f32[256,8,80]{2,1,0:T(8,128)} copy(f32[256,8,80]{0,2,1:T(8,128)} %convolution_bitcast_fusion.4) | data formatting | bytes 1310720 | tf_op jit(solution)/shard_map/hij,ihd->jhd/transpose | solution.py:163
  125.0 2.4 %stack.110 = f32[4,2,32,1,640]{4,2,1,0,3:T(8,128)} reshape(f32[256,8,80]{2,1,0:T(8,128)} %copy.202) | data formatting | bytes 1310720 | tf_op jit(solution)/shard_map/stack | solution.py:166
  129.5 2.4 %copy.187 = f32[256,8,80]{2,1,0:T(8,128)} copy(f32[256,8,80]{0,2,1:T(8,128)} %convolution_bitcast_fusion.7) | data formatting | bytes 1310720 | tf_op jit(solution)/shard_map/hij,ihd->jhd/transpose | solution.py:160
  131.9 2.4 %stack.106 = f32[2,2,64,1,640]{4,2,1,0,3:T(8,128)} reshape(f32[256,8,80]{2,1,0:T(8,128)} %copy.187) | data formatting | bytes 1310720 | tf_op jit(solution)/shard_map/stack | solution.py:166
  134.3 2.0 constant_dynamic-update-slice_fusion.5
  136.3 2.5 %copy.189 = f32[256,8,80]{2,1,0:T(8,128)} copy(f32[256,8,80]{0,2,1:T(8,128)} %convolution_bitcast_fusion.6) | data formatting | bytes 1310720 | tf_op jit(solution)/shard_map/hij,ihd->jhd/transpose | solution.py:163
  138.8 2.4 %stack.107 = f32[2,2,64,1,640]{4,2,1,0,3:T(8,128)} reshape(f32[256,8,80]{2,1,0:T(8,128)} %copy.189) | data formatting | bytes 1310720 | tf_op jit(solution)/shard_map/stack | solution.py:166
  144.7 2.4 %copy.184 = f32[256,8,80]{0,2,1:T(8,128)} copy(f32[256,8,80]{2,1,0:T(8,128)} %bitcast.312) | data formatting | bytes 1310720 | tf_op jit(solution)/shard_map/jit(_where)/broadcast_in_dim | solution.py:39
  159.9 7.2 %collective-permute-done.8 = f32[2,32,2,640]{3,1,0,2:T(8,128)S(1)} collective-permute-done((f32[2,32,2,640]{3,1,0,2:T(8,128)S(1)}, f32[2,32,2,640]{3,1,0,2:T(8,128)S(1)}, u32[]{:S(2)}, u32[]{:S(2)}) %collective-permute-start.8) | collective-permute-done | bytes 327712 | tf_op jit(solution)/shard_map/ppermute | solution.py:18
  170.1 3.2 %collective-permute-done.6 = f32[1,64,2,640]{3,1,2,0:T(8,128)S(1)} collective-permute-done((f32[1,64,2,640]{3,1,2,0:T(8,128)S(1)}, f32[1,64,2,640]{3,1,2,0:T(8,128)S(1)}, u32[]{:S(2)}, u32[]{:S(2)}) %collective-permute-start.6) | collective-permute-done | bytes 327712 | tf_op jit(solution)/shard_map/ppermute | solution.py:18
  174.1 2.0 reshape_squeeze.6
  178.9 2.4 %copy.198 = f32[256,8,80]{0,2,1:T(8,128)} copy(f32[256,8,80]{2,1,0:T(8,128)} %bitcast.314) | data formatting | bytes 1310720 | tf_op jit(solution)/shard_map/jit(_where)/broadcast_in_dim | solution.py:39
  181.3 2.0 broadcast_in_dim.398
  183.3 2.4 %copy.218 = f32[256,8,80]{0,2,1:T(8,128)} copy(f32[256,8,80]{2,1,0:T(8,128)} %bitcast.315) | data formatting | bytes 1310720 | tf_op jit(solution)/shard_map/jit(_where)/broadcast_in_dim | solution.py:39
  191.9 2.4 %copy.215 = f32[256,8,80]{0,2,1:T(8,128)} copy(f32[256,8,80]{2,1,0:T(8,128)} %bitcast.316) | data formatting | bytes 1310720 | tf_op jit(solution)/shard_map/jit(_where)/broadcast_in_dim | solution.py:39
  194.3 2.6 %fusion.15 = bf16[256,8,80]{0,2,1:T(8,128)(2,1)} fusion(bf16[8,256,256]{1,2,0:T(8,128)(2,1)S(1)} %multiply_convert_fusion, bf16[256,8,80]{0,2,1:T(8,128)(2,1)} %bitcast.322, f32[256,8,80]{0,2,1:T(8,128)} %copy.215, f32[256,8,80]{0,2,1:T(8,128)} %copy.198, pred[256,8]{0,1:T(8,128)(4,1)S(1)} %copy-done.30, pred[256,8]{0,1:T(8,128)(4,1)S(1)} %copy-done.31), kind=kOutput, calls=%fused_computation.29 | convolution fusion | flops 84705280 | bytes 3018752 | tf_op jit(solution)/shard_map/hij,ihd->jhd/dot_general | solution.py:153
  (235 shorter events, 109.9 us)
Async XLA Ops:
  0.6 9.3 %copy-start.9 = (bf16[256,640]{1,0:T(8,128)(2,1)S(1)}, bf16[256,640]{1,0:T(8,128)(2,1)}, u32[]{:S(2)}) copy-start(bf16[256,640]{1,0:T(8,128)(2,1)} %param.4) | copy-start | bytes 983044
  2.4 24.3 %all-to-all-start = ((bf16[64,4,640]{2,0,1:T(8,128)(2,1)}), bf16[64,4,640]{2,0,1:T(8,128)(2,1)S(1)}, u32[]{:S(2)}, u32[]{:S(2)}) async-start(bf16[64,4,640]{2,0,1:T(8,128)(2,1)} %bitcast.304), calls=%async_computation | async-start | bytes 655360 | tf_op jit(solution)/shard_map/all_to_all | solution.py:100
  12.7 13.4 %copy-start.27 = (f32[8,256]{1,0:T(8,128)}, f32[8,256]{1,0:T(8,128)S(1)}, u32[]{:S(2)}) copy-start(f32[8,256]{1,0:T(8,128)S(1)} %get-tuple-element.46) | copy-start | bytes 24580
  13.0 13.1 %copy-start.29 = (f32[8,256]{1,0:T(8,128)}, f32[8,256]{1,0:T(8,128)S(1)}, u32[]{:S(2)}) copy-start(f32[8,256]{1,0:T(8,128)S(1)} %exponential_reduce_fusion) | copy-start | bytes 24580
  15.2 92.4 %copy-start.6 = (bf16[256,640]{0,1:T(8,128)(2,1)}, bf16[256,640]{0,1:T(8,128)(2,1)S(1)}, u32[]{:S(2)}) copy-start(bf16[256,640]{0,1:T(8,128)(2,1)S(1)} %copy.158) | copy-start | bytes 983044
  15.2 8.9 %copy-start.28 = (pred[256,8]{1,0:T(8,128)(4,1)S(1)}, pred[256,8]{1,0:T(8,128)(4,1)}, u32[]{:S(2)}) copy-start(pred[256,8]{1,0:T(8,128)(4,1)} %broadcast_bitcast_fusion.1) | copy-start | bytes 6148
  15.2 9.5 %copy-start.40 = (pred[4,8]{1,0:T(4,128)(4,1)S(1)}, pred[4,8]{1,0:T(4,128)(4,1)}, u32[]{:S(2)}) copy-start(pred[4,8]{1,0:T(4,128)(4,1)} %iota_compare_fusion.4) | copy-start | bytes 100
  15.2 10.2 %copy-start.44 = (s32[64]{0:T(128)S(1)}, s32[64]{0:T(128)}, u32[]{:S(2)}) copy-start(s32[64]{0:T(128)} %iota_add_fusion.1) | copy-start | bytes 772
  21.7 8.7 %copy-start.38 = (pred[8,8]{1,0:T(8,128)(4,1)S(1)}, pred[8,8]{1,0:T(8,128)(4,1)}, u32[]{:S(2)}) copy-start(pred[8,8]{1,0:T(8,128)(4,1)} %copy-done.37) | copy-start | bytes 196
  28.7 6.3 %copy-start.41 = (pred[4,8]{1,0:T(4,128)(4,1)S(1)}, pred[4,8]{1,0:T(4,128)(4,1)}, u32[]{:S(2)}) copy-start(pred[4,8]{1,0:T(4,128)(4,1)} %iota_compare_fusion.4) | copy-start | bytes 100
  30.4 77.2 %copy-start.4 = (bf16[256,8,80]{0,2,1:T(8,128)(2,1)}, bf16[256,8,80]{0,2,1:T(8,128)(2,1)S(1)}, u32[]{:S(2)}) copy-start(bf16[256,8,80]{0,2,1:T(8,128)(2,1)S(1)} %copy.159) | copy-start | bytes 983044
  35.0 3.7 %collective-permute-start.2 = (bf16[1,32,2,640]{3,1,2,0:T(8,128)(2,1)}, bf16[1,32,2,640]{3,1,2,0:T(8,128)(2,1)}, u32[]{:S(2)}, u32[]{:S(2)}) collective-permute-start(bf16[1,32,2,640]{3,1,2,0:T(8,128)(2,1)} %constant_dynamic-update-slice_fusion.2), channel_id=1, source_target_pairs={{0,4},{4,0},{8,12},{12,8},{16,20},{20,16},{24,28},{28,24},{1,5},{5... | collective-permute-start | bytes 245768 | tf_op jit(solution)/shard_map/ppermute | solution.py:18
  38.1 3.1 %collective-permute-start = (bf16[1,64,2,640]{3,1,2,0:T(8,128)(2,1)S(1)}, bf16[1,64,2,640]{3,1,2,0:T(8,128)(2,1)S(1)}, u32[]{:S(2)}, u32[]{:S(2)}) collective-permute-start(bf16[1,64,2,640]{3,1,2,0:T(8,128)(2,1)S(1)} %constant_dynamic-update-slice_fusion), channel_id=1, source_target_pairs={{0,4},{4,0},{8,12},{12,8},{16,20},{20,16},{24,28},{28,24},{1,5},{5... | collective-permute-start | bytes 491528 | tf_op jit(solution)/shard_map/ppermute | solution.py:18
  39.7 7.1 %collective-permute-start.3 = (bf16[2,32,2,640]{3,1,2,0:T(8,128)(2,1)S(1)}, bf16[2,32,2,640]{3,1,2,0:T(8,128)(2,1)S(1)}, u32[]{:S(2)}, u32[]{:S(2)}) collective-permute-start(bf16[2,32,2,640]{3,1,2,0:T(8,128)(2,1)S(1)} %maximum_bitcast_fusion.1), channel_id=1, source_target_pairs={{0,8},{8,0},{4,12},{12,4},{16,24},{24,16},{20,28},{28,20},{1,9},{9... | collective-permute-start | bytes 491528 | tf_op jit(solution)/shard_map/ppermute | solution.py:18
  41.3 11.6 %collective-permute-start.1 = (bf16[2,64,2,640]{3,1,2,0:T(8,128)(2,1)S(1)}, bf16[2,64,2,640]{3,1,2,0:T(8,128)(2,1)S(1)}, u32[]{:S(2)}, u32[]{:S(2)}) collective-permute-start(bf16[2,64,2,640]{3,1,2,0:T(8,128)(2,1)S(1)} %maximum_bitcast_fusion), channel_id=1, source_target_pairs={{0,8},{8,0},{4,12},{12,4},{16,24},{24,16},{20,28},{28,20},{1,9},{9... | collective-permute-start | bytes 983048 | tf_op jit(solution)/shard_map/ppermute | solution.py:18
  46.9 10.8 %copy-start.12 = (bf16[2,2,32,2,640]{4,2,3,1,0:T(8,128)(2,1)}, bf16[2,2,32,2,640]{4,2,3,1,0:T(8,128)(2,1)S(1)}, u32[]{:S(2)}) copy-start(bf16[2,2,32,2,640]{4,2,3,1,0:T(8,128)(2,1)S(1)} %pad_maximum_fusion.2) | copy-start | bytes 983044
  47.8 17.7 %collective-permute-start.4 = (bf16[4,32,2,640]{3,1,0,2:T(8,128)(2,1)}, bf16[4,32,2,640]{3,1,0,2:T(8,128)(2,1)}, u32[]{:S(2)}, u32[]{:S(2)}) collective-permute-start(bf16[4,32,2,640]{3,1,0,2:T(8,128)(2,1)} %copy.147), channel_id=1, source_target_pairs={{0,16},{16,0},{4,20},{20,4},{8,24},{24,8},{12,28},{28,12},{1,17},{... | collective-permute-start | bytes 983048 | tf_op jit(solution)/shard_map/ppermute | solution.py:18
  53.9 7.7 %copy-start.24 = (bf16[64,8,80]{2,1,0:T(8,128)(2,1)S(1)}, bf16[64,8,80]{2,1,0:T(8,128)(2,1)}, u32[]{:S(2)}) copy-start(bf16[64,8,80]{2,1,0:T(8,128)(2,1)} %get-tuple-element.19) | copy-start | bytes 245764
  53.9 7.7 %copy-start.39 = (pred[64,256]{1,0:T(8,128)(4,1)S(1)}, pred[64,256]{1,0:T(8,128)(4,1)}, u32[]{:S(2)}) copy-start(pred[64,256]{1,0:T(8,128)(4,1)} %iota_compare_fusion.1) | copy-start | bytes 49156
  63.3 7.3 %copy-start.23 = (f32[64,8]{1,0:T(8,128)}, f32[64,8]{1,0:T(8,128)S(1)}, u32[]{:S(2)}) copy-start(f32[64,8]{1,0:T(8,128)S(1)} %copy.141) | copy-start | bytes 6148
  67.5 7.3 %copy-start.36 = (pred[32,256]{1,0:T(8,128)(4,1)S(1)}, pred[32,256]{1,0:T(8,128)(4,1)}, u32[]{:S(2)}) copy-start(pred[32,256]{1,0:T(8,128)(4,1)} %iota_compare_fusion.2) | copy-start | bytes 24580
  109.4 5.4 %copy-start.20 = (bf16[64,8,80]{2,1,0:T(8,128)(2,1)S(1)}, bf16[64,8,80]{2,1,0:T(8,128)(2,1)}, u32[]{:S(2)}) copy-start(bf16[64,8,80]{2,1,0:T(8,128)(2,1)} %get-tuple-element.16) | copy-start | bytes 245764
  110.4 5.6 %copy-start.43 = (pred[8,8]{0,1:T(8,128)(4,1)S(1)}, pred[8,8]{0,1:T(8,128)(4,1)}, u32[]{:S(2)}) copy-start(pred[8,8]{0,1:T(8,128)(4,1)} %copy-done.42) | copy-start | bytes 196
  110.4 5.8 %copy-start.22 = (bf16[32,8,80]{2,1,0:T(8,128)(2,1)S(1)}, bf16[32,8,80]{2,1,0:T(8,128)(2,1)}, u32[]{:S(2)}) copy-start(bf16[32,8,80]{2,1,0:T(8,128)(2,1)} %get-tuple-element.12) | copy-start | bytes 122884
  110.4 5.8 %copy-start.33 = (f32[32,8]{0,1:T(8,128)S(1)}, f32[32,8]{0,1:T(8,128)}, u32[]{:S(2)}) copy-start(f32[32,8]{0,1:T(8,128)} %copy-done.32) | copy-start | bytes 3076
  111.7 5.7 %copy-start.11 = (bf16[256,1,8,80]{0,3,2,1:T(8,128)(2,1)S(1)}, bf16[256,1,8,80]{0,3,2,1:T(8,128)(2,1)}, u32[]{:S(2)}) copy-start(bf16[256,1,8,80]{0,3,2,1:T(8,128)(2,1)} %copy.234) | copy-start | bytes 983044
  128.5 5.8 %copy-start = (f32[4,2,32,2,640]{4,2,1,0,3:T(8,128)}, f32[4,2,32,2,640]{4,2,1,0,3:T(8,128)S(1)}, u32[]{:S(2)}) copy-start(f32[4,2,32,2,640]{4,2,1,0,3:T(8,128)S(1)} %constant_dynamic-update-slice_fusion.6) | copy-start | bytes 3932164
  129.5 25.2 %collective-permute-start.7 = (f32[4,32,2,640]{3,1,0,2:T(8,128)}, f32[4,32,2,640]{3,1,0,2:T(8,128)}, u32[]{:S(2)}, u32[]{:S(2)}) collective-permute-start(f32[4,32,2,640]{3,1,0,2:T(8,128)} %select_bitcast_fusion), channel_id=1, source_target_pairs={{0,4},{4,0},{8,12},{12,8},{16,20},{20,16},{24,28},{28,24},{1,5},{5... | collective-permute-start | bytes 1966088 | tf_op jit(solution)/shard_map/ppermute | solution.py:18
  149.6 8.5 %collective-permute-start.5 = (f32[2,64,2,640]{3,1,0,2:T(8,128)}, f32[2,64,2,640]{3,1,0,2:T(8,128)}, u32[]{:S(2)}, u32[]{:S(2)}) collective-permute-start(f32[2,64,2,640]{3,1,0,2:T(8,128)} %select_bitcast_fusion.1), channel_id=1, source_target_pairs={{0,4},{4,0},{8,12},{12,8},{16,20},{20,16},{24,28},{28,24},{1,5},{5... | collective-permute-start | bytes 1966088 | tf_op jit(solution)/shard_map/ppermute | solution.py:18
  156.5 10.6 %collective-permute-start.8 = (f32[2,32,2,640]{3,1,0,2:T(8,128)S(1)}, f32[2,32,2,640]{3,1,0,2:T(8,128)S(1)}, u32[]{:S(2)}, u32[]{:S(2)}) collective-permute-start(f32[2,32,2,640]{3,1,0,2:T(8,128)S(1)} %select_bitcast_fusion.2), channel_id=1, source_target_pairs={{0,8},{8,0},{4,12},{12,4},{16,24},{24,16},{20,28},{28,20},{1,9},{9... | collective-permute-start | bytes 983048 | tf_op jit(solution)/shard_map/ppermute | solution.py:18
  159.3 14.0 %collective-permute-start.6 = (f32[1,64,2,640]{3,1,2,0:T(8,128)S(1)}, f32[1,64,2,640]{3,1,2,0:T(8,128)S(1)}, u32[]{:S(2)}, u32[]{:S(2)}) collective-permute-start(f32[1,64,2,640]{3,1,2,0:T(8,128)S(1)} %select_bitcast_fusion.3), channel_id=1, source_target_pairs={{0,8},{8,0},{4,12},{12,4},{16,24},{24,16},{20,28},{28,20},{1,9},{9... | collective-permute-start | bytes 983048 | tf_op jit(solution)/shard_map/ppermute | solution.py:18
  168.6 17.1 %collective-permute-start.9 = (f32[1,32,2,640]{3,1,2,0:T(8,128)}, f32[1,32,2,640]{3,1,2,0:T(8,128)}, u32[]{:S(2)}, u32[]{:S(2)}) collective-permute-start(f32[1,32,2,640]{3,1,2,0:T(8,128)} %select_bitcast_fusion.8), channel_id=1, source_target_pairs={{0,16},{16,0},{4,20},{20,4},{8,24},{24,8},{12,28},{28,12},{1,17},{... | collective-permute-start | bytes 491528 | tf_op jit(solution)/shard_map/ppermute | solution.py:18
  (24 other events, 70.2 us)
where the time goes:
time: 206 us; the launch traced here: 204 us
  local copies, waits for them, and re-layouts  115 us (56%)
  other arithmetic  30.8 us (15%)
  matrix products  22.7 us (11%)
  waiting for transfers between devices  19 us (9%)
  starting transfers between devices  14.8 us (7%)
    broadcast_in_dim x27, local copies, waits for them, and re-layouts, spread_level(): widened = jnp.where(chosen[None, :, :, None], sparse[:, None], fill)  33.4 us
    ppermute x10, waiting for transfers between devices, from_partner(): return lax.ppermute(block, axis, route)  19 us
    unnamed x102, local copies, waits for them, and re-layouts  15.4 us
    another operation x9, local copies, waits for them, and re-layouts, pick_level(): shaped = field.reshape((field.shape[0] // stride, stride) + field.shape[1:])  13.1 us
    another operation x6, local copies, waits for them, and re-layouts, body(): jnp.stack((key_part, value_part), axis=1)  10.7 us
    another operation x3, local copies, waits for them, and re-layouts, body(): gathered = gathered.reshape(group_size * row_count, 2, heads_local, HD)  10.7 us
    reduce_sum x6, other arithmetic, pick_level(): return jnp.sum(kept, axis=1, dtype=field.dtype)  9.68 us
    ppermute x10, starting transfers between devices, from_partner(): return lax.ppermute(block, axis, route)  8.49 us
  transfers between devices with their start and end apart: 11, of which 4 were waited for; matrix products, arithmetic and copies ran while one was open for 37% of the time, Pallas kernels for 0%

commit v1 on v0

v1 whole, which is shorter than its diff:
```python
import functools
import math

import jax
import jax.numpy as jnp
from jax import lax
from jax.experimental import pallas as pl
from jax.experimental.pallas import tpu as pltpu
from jax.sharding import PartitionSpec as P

HD = 80
SPAN1 = 4
DIL1 = 4
WIDEST = 32
LANES = 128
BF16 = jnp.bfloat16
F32 = jnp.float32
SCALE = HD**-0.5
SCALE2 = SCALE * math.log2(math.e)
VMEM_BYTES = 48 * 2**20


class Plan:
    def __init__(self, tokens, width, seq_count, head_count):
        self.tokens = tokens
        self.width = width
        self.heads = width // HD
        self.g1 = SPAN1
        self.g2 = min(WIDEST, seq_count)
        self.r2 = self.g2
        self.n1 = tokens // DIL1
        self.n2 = tokens // self.r2
        self.turns = self.r2 // DIL1
        self.zcount = head_count
        self.rows = [2 * (self.n1 if b < self.g1 else self.n2) for b in range(self.g2)]


def nt(a, b):
    return lax.dot_general(a, b, (((1,), (1,)), ((), ())), preferred_element_type=F32)


def nn(a, b):
    return lax.dot_general(a, b, (((1,), (0,)), ((), ())), preferred_element_type=F32)


def tn(a, b):
    return lax.dot_general(a, b, (((0,), (0,)), ((), ())), preferred_element_type=F32)


def iota(shape, dim):
    return lax.broadcasted_iota(jnp.int32, shape, dim)


def phase_order(p, inverse=False):
    shape = (p.tokens, p.tokens)
    row, col = (iota(shape, 1), iota(shape, 0)) if inverse else (iota(shape, 0), iota(shape, 1))
    return jnp.where(col == p.r2 * (row % p.n2) + row // p.n2, 1.0, 0.0).astype(BF16)


def first_head(p):
    return lax.axis_index("head") * p.heads


def column_class(p):
    return (first_head(p) + iota((1, p.width), 1) // HD) % p.r2


def lane_class(p):
    return (first_head(p) + iota((1, LANES), 1)) % p.r2


def pick(p, whole, label):
    parts = []
    for t in range(p.turns):
        want = (label + DIL1 * t) % p.r2
        part = jnp.zeros((p.n2, whole.shape[1]), F32)
        for c in range(p.r2):
            part = jnp.where(want == c, whole[c * p.n2 : (c + 1) * p.n2], part)
        parts.append(part)
    return jnp.concatenate(parts, axis=0)


def spread(p, kept, label, base):
    parts = []
    for c in range(p.r2):
        part = base[c * p.n2 : (c + 1) * p.n2]
        for t in range(p.turns):
            hit = (label + DIL1 * t) % p.r2 == c
            part = jnp.where(hit, kept[t * p.n2 : (t + 1) * p.n2], part)
        parts.append(part)
    return jnp.concatenate(parts, axis=0)


def window(h):
    low = h * HD // LANES * LANES
    high = -(-(h + 1) * HD // LANES) * LANES
    return low, high


def window_mask(h, low, high):
    lane = low + iota((1, high - low), 1)
    return (lane >= h * HD) & (lane < (h + 1) * HD)


def head_mask(p, h):
    lane = iota((1, p.width), 1)
    return (lane >= h * HD) & (lane < (h + 1) * HD)


def own_bias(p):
    shape = (p.tokens, p.tokens)
    row, col = iota(shape, 0), iota(shape, 1)
    qpos = p.r2 * (row % p.n2) + row // p.n2
    kpos = p.r2 * (col % p.n2) + col // p.n2
    return jnp.where(qpos >= kpos, 0.0, -jnp.inf)


def call(kernel, outs, scratch=(), flops=0):
    return pl.pallas_call(
        kernel,
        out_shape=[jax.ShapeDtypeStruct(s, d) for s, d in outs],
        scratch_shapes=[pltpu.VMEM(s, d) for s, d in scratch],
        compiler_params=pltpu.CompilerParams(vmem_limit_bytes=VMEM_BYTES),
        cost_estimate=pl.CostEstimate(flops=flops, bytes_accessed=2**20, transcendentals=0),
    )


def pack_kernel(p, q_ref, k_ref, v_ref, g_ref, qp, kp, vp, q1, kv1, kv2, *gz):
    z = lax.axis_index("head")
    for b in range(p.zcount):
        start = pl.multiple_of(jnp.bitwise_xor(z, b) * p.width, LANES)
        gz[b][...] = g_ref[:, pl.ds(start, p.width)]
    order = phase_order(p)
    label = column_class(p)
    k = nn(order, k_ref[...])
    kp[...] = k.astype(BF16)
    k_kept = pick(p, k, label)
    v = nn(order, v_ref[...])
    vp[...] = v.astype(BF16)
    v_kept = pick(p, v, label)
    kv1[...] = jnp.concatenate([k_kept, v_kept], axis=0).astype(BF16)
    kv2[...] = jnp.concatenate([k_kept[: p.n2], v_kept[: p.n2]], axis=0).astype(BF16)
    q = nn(order, q_ref[...])
    qp[...] = q.astype(BF16)
    q1[...] = pick(p, q, label).astype(BF16)


def own_kernel(p, qp, kp, vp, *refs):
    gz, (gp, g1, lse0, d0, lse01, d01, natural) = refs[: p.zcount], refs[p.zcount :]
    z = lax.axis_index("head")
    share = p.tokens // p.zcount
    for b in range(p.zcount):
        start = pl.multiple_of(jnp.bitwise_xor(z, b) * share, share)
        natural[pl.ds(start, share), :] = gz[b][...]
    g = nn(phase_order(p), natural[...])
    gp[...] = g.astype(BF16)
    g1[...] = pick(p, g, column_class(p)).astype(BF16)
    bias = own_bias(p)
    lane = iota((1, LANES), 1)
    lse_all = jnp.zeros((p.tokens, LANES), F32)
    d_all = jnp.zeros((p.tokens, LANES), F32)
    for h in range(p.heads):
        low, high = window(h)
        mask = jnp.where(window_mask(h, low, high), 1.0, 0.0).astype(BF16)
        s = nt(qp[:, low:high] * mask, kp[:, low:high]) * SCALE2 + bias
        top = jnp.max(s, axis=1, keepdims=True)
        e = jnp.exp2(s - top)
        denom = jnp.sum(e, axis=1, keepdims=True)
        dp = nt(gp[:, low:high] * mask, vp[:, low:high])
        d = jnp.sum(e * dp, axis=1, keepdims=True) / denom
        lse_all = jnp.where(lane == h, top + jnp.log2(denom), lse_all)
        d_all = jnp.where(lane == h, d, d_all)
    lse0[...] = lse_all
    d0[...] = d_all
    label = lane_class(p)
    lse01[...] = pick(p, lse_all, label)
    d01[...] = pick(p, d_all, label)


def columns(p, stat):
    return jnp.concatenate([stat[:, h : h + 1] for h in range(p.heads)], axis=0)


def to_lanes(p, column):
    lane = iota((1, LANES), 1)
    out = jnp.zeros((p.n1, LANES), F32)
    for h in range(p.heads):
        out = jnp.where(lane == h, column[h * p.n1 : (h + 1) * p.n1], out)
    return out


def wide_rows(p, column):
    return jnp.concatenate([column[h * p.n1 : h * p.n1 + p.n2] for h in range(p.heads)], axis=0)


def widen(p, column, fill):
    rest = jnp.full((p.n1 - p.n2, column.shape[1]), fill, F32)
    parts = []
    for h in range(p.heads):
        parts += [column[h * p.n2 : (h + 1) * p.n2], rest]
    return jnp.concatenate(parts, axis=0)


def by_head(p, rows):
    parts = [jnp.where(head_mask(p, h), rows, 0.0) for h in range(p.heads)]
    return jnp.concatenate(parts, axis=0).astype(BF16)


def merge_heads(p, rows, count):
    out = jnp.zeros((count, p.width), F32)
    for h in range(p.heads):
        out = jnp.where(head_mask(p, h), rows[h * count : (h + 1) * count], out)
    return out


def levels_kernel(p, q1, g1, lse01, d01, *refs):
    kv = refs[: p.g2]
    dq1, total1, delta1, keep, send = refs[p.g2 :]
    d = lax.axis_index("seq")
    n1, n2 = p.n1, p.n2
    blocks = [ref[...].astype(F32) for ref in kv]
    k1 = jnp.concatenate([blocks[b][:n1] for b in range(p.g1)], axis=0).astype(BF16)
    v1 = jnp.concatenate([blocks[b][n1:] for b in range(p.g1)], axis=0).astype(BF16)
    k2 = jnp.concatenate([block[:n2] for block in blocks], axis=0).astype(BF16)
    v2 = jnp.concatenate(
        [block[half : half + n2] for block, half in zip(blocks, [r // 2 for r in p.rows])], axis=0
    ).astype(BF16)
    q_rows, g_rows = q1[...].astype(F32), g1[...].astype(F32)
    q1b, g1b = by_head(p, q_rows), by_head(p, g_rows)
    q2b, g2b = by_head(p, q_rows[:n2]), by_head(p, g_rows[:n2])

    shape1 = (p.heads * n1, p.g1 * n1)
    row = iota((shape1[0], 1), 0)
    col = iota((1, shape1[1]), 1)
    head = first_head(p) + row // n1
    own = row % n1
    qpos = p.tokens * d + p.r2 * (own % n2) + (head + DIL1 * (own // n2)) % p.r2
    other = col % n1
    kbase = p.tokens * jnp.bitwise_xor(d, col // n1) + p.r2 * (other % n2)
    kpos = kbase + jnp.bitwise_and(head + DIL1 * (other // n2), p.r2 - 1)
    s1 = jnp.where(kpos <= qpos, nt(q1b, k1) * SCALE2, -jnp.inf)
    top1 = jnp.max(s1, axis=1, keepdims=True)
    lse1 = top1 + jnp.log2(jnp.sum(jnp.exp2(s1 - top1), axis=1, keepdims=True))

    row2 = d * n2 + iota((p.heads * n2, 1), 0) % n2
    col2 = iota((1, p.g2 * n2), 1)
    col2 = jnp.bitwise_xor(d, col2 // n2) * n2 + col2 % n2
    s2 = jnp.where(col2 <= row2, nt(q2b, k2) * SCALE2, -jnp.inf)
    top2 = jnp.max(s2, axis=1, keepdims=True)
    lse2 = top2 + jnp.log2(jnp.sum(jnp.exp2(s2 - top2), axis=1, keepdims=True))

    lse0 = columns(p, lse01[...])
    lse2 = widen(p, lse2, -jnp.inf)
    peak = jnp.maximum(jnp.maximum(lse0, lse1), lse2)
    share0 = jnp.exp2(lse0 - peak)
    total = peak + jnp.log2(share0 + jnp.exp2(lse1 - peak) + jnp.exp2(lse2 - peak))
    p1 = jnp.exp2(s1 - total)
    p2 = jnp.exp2(s2 - wide_rows(p, total))
    dp1 = nt(g1b, v1)
    dp2 = nt(g2b, v2)
    delta = jnp.exp2(lse0 - total) * columns(p, d01[...])
    delta += jnp.sum(p1 * dp1, axis=1, keepdims=True)
    delta += widen(p, jnp.sum(p2 * dp2, axis=1, keepdims=True), 0.0)
    ds1 = (p1 * (dp1 - delta) * SCALE).astype(BF16)
    ds2 = (p2 * (dp2 - wide_rows(p, delta)) * SCALE).astype(BF16)
    p1, p2 = p1.astype(BF16), p2.astype(BF16)

    dk1, dk2 = tn(ds1, q1b), tn(ds2, q2b)
    dv1, dv2 = tn(p1, g1b), tn(p2, g2b)
    at = [0, 0]
    for b in range(p.g2):
        rows = slice(b * n2, (b + 1) * n2)
        if b < p.g1:
            first = slice(b * n1, b * n1 + n2)
            rest = slice(b * n1 + n2, (b + 1) * n1)
            part = [dk1[first] + dk2[rows], dk1[rest], dv1[first] + dv2[rows], dv1[rest]]
        else:
            part = [dk2[rows], dv2[rows]]
        part = jnp.concatenate(part, axis=0)
        odd = b % 2
        ref = send if odd else keep
        ref[at[odd] : at[odd] + p.rows[b], :] = part.astype(ref.dtype)
        at[odd] += p.rows[b]
    dq = merge_heads(p, nn(ds1, k1), n1)
    wide = merge_heads(p, nn(ds2, k2), n2)
    dq1[...] = jnp.concatenate([dq[:n2] + wide, dq[n2:]], axis=0)
    total1[...] = to_lanes(p, total)
    delta1[...] = to_lanes(p, delta)


def chip_kernel(p, keep, came, own, *outs):
    at = 0
    for index, b in enumerate(range(0, p.g2, 2)):
        rows = slice(at, at + p.rows[b])
        block = keep[rows, :] + came[rows, :].astype(F32)
        if b == 0:
            own[...] = block
        else:
            outs[index - 1][...] = block.astype(BF16)
        at += p.rows[b]


def own_grad_kernel(p, qp, kp, vp, gp, lse0, d0, total1, delta1, dq1, grad_q, dk0, dv0, dq):
    label = lane_class(p)
    total = spread(p, total1[...], label, lse0[...])
    delta = spread(p, delta1[...], label, d0[...])
    bias = own_bias(p)
    for ref in (dq, dk0, dv0):
        ref[...] = jnp.zeros_like(ref)
    for h in range(p.heads):
        low, high = window(h)
        hit = window_mask(h, low, high)
        mask = jnp.where(hit, 1.0, 0.0).astype(BF16)
        q = qp[:, low:high] * mask
        g = gp[:, low:high] * mask
        k = kp[:, low:high]
        prob = jnp.exp2(nt(q, k) * SCALE2 + bias - total[:, h : h + 1])
        dp = nt(g, vp[:, low:high])
        ds = (prob * (dp - delta[:, h : h + 1]) * SCALE).astype(BF16)
        dq[:, low:high] = jnp.where(hit, nn(ds, k), dq[:, low:high])
        dk0[:, low:high] += tn(ds, q)
        dv0[:, low:high] += tn(prob.astype(BF16), g)
    zero = jnp.zeros((p.tokens, p.width), F32)
    all_q = dq[...] + spread(p, dq1[...], column_class(p), zero)
    grad_q[...] = nn(phase_order(p, True), all_q.astype(BF16)).astype(BF16)


def last_kernel(p, dk0, dv0, own, *refs):
    came, (grad_k, grad_v) = refs[:-2], refs[-2:]
    order = phase_order(p, True)
    label = column_class(p)
    zero = jnp.zeros((p.tokens, p.width), F32)
    sums = own[...]
    wide = []
    for ref, b in zip(came, range(2, p.g2, 2)):
        block = ref[...].astype(F32)
        if b < p.g1:
            sums = sums + block
        else:
            wide.append(block)
    for index, (base, grad) in enumerate(((dk0, grad_k), (dv0, grad_v))):
        kept = sums[index * p.n1 : (index + 1) * p.n1]
        if wide:
            first = kept[: p.n2]
            for block in wide:
                first = first + block[index * p.n2 : (index + 1) * p.n2]
            kept = jnp.concatenate([first, kept[p.n2 :]], axis=0)
        whole = base[...] + spread(p, kept, label, zero)
        grad[...] = nn(order, whole.astype(BF16)).astype(BF16)


def swap(block, axis, bits):
    count = lax.axis_size(axis)
    return lax.ppermute(block, axis, [(i, i ^ bits) for i in range(count)])


def body(queries, keys, values, grad_out):
    tokens, width = queries.shape
    p = Plan(tokens, width, lax.axis_size("seq"), lax.axis_size("head"))
    n1, n2 = p.n1, p.n2
    run = lambda kernel: functools.partial(kernel, p)
    row, kept = (tokens, width), (n1, width)
    share = (tokens // p.zcount, width)

    outs = call(
        run(pack_kernel),
        [(row, BF16)] * 3
        + [(kept, BF16), ((2 * n1, width), BF16), ((2 * n2, width), BF16)]
        + [(share, BF16)] * p.zcount,
    )(queries, keys, values, grad_out)
    qp, kp, vp, q1, kv1, kv2 = outs[:6]
    gz = outs[6:]
    gz = [gz[0]] + [swap(gz[b], "head", b) for b in range(1, p.zcount)]

    kv = {0: kv1}
    for b in range(2, p.g2, 2):
        kv[b] = swap(kv1 if b < p.g1 else kv2, "seq", b)
    for b in range(0, p.g2, 2):
        kv[b + 1] = swap(kv[b], "seq", 1)

    stat, stat1 = (tokens, LANES), (n1, LANES)
    gp, g1, lse0, d0, lse01, d01 = call(
        run(own_kernel),
        [(row, BF16), (kept, BF16), (stat, F32), (stat, F32), (stat1, F32), (stat1, F32)],
        [(row, BF16)],
    )(qp, kp, vp, *gz)
    half_rows = sum(p.rows[::2])
    dq1, total1, delta1, keep, send = call(
        run(levels_kernel),
        [
            (kept, F32),
            (stat1, F32),
            (stat1, F32),
            ((half_rows, width), F32),
            ((half_rows, width), BF16),
        ],
    )(q1, g1, lse01, d01, *[kv[b] for b in range(p.g2)])
    came = swap(send, "seq", 1)
    grad_q, dk0, dv0 = call(
        run(own_grad_kernel), [(row, BF16), (row, F32), (row, F32)], [(row, F32)]
    )(qp, kp, vp, gp, lse0, d0, total1, delta1, dq1)
    sums = call(
        run(chip_kernel),
        [((p.rows[0], width), F32)] + [((p.rows[b], width), BF16) for b in range(2, p.g2, 2)],
    )(keep, came)
    parts = [swap(s, "seq", b) for s, b in zip(sums[1:], range(2, p.g2, 2))]
    grad_k, grad_v = call(run(last_kernel), [(row, BF16)] * 2)(dk0, dv0, sums[0], *parts)
    return grad_q, grad_k, grad_v


def solution(mesh):
    return jax.shard_map(
        body,
        mesh=mesh,
        in_specs=(P("seq", "head"), P("seq", "head"), P("seq", "head"), P(("seq", "head"), None)),
        out_specs=(P("seq", "head"), P("seq", "head"), P("seq", "head")),
        check_vma=False,
    )
```

time: 206 us -> 39.8 us (0.19); the launches traced: 204 us -> 39.5 us
  local copies, waits for them, and re-layouts: 115 us -> 3.88 us
  other arithmetic: 30.8 us -> 0 us
  matrix products: 22.7 us -> 0 us
  Pallas kernels: 0 us -> 10.6 us
  waiting for transfers between devices: 19 us -> 9.36 us
    another operation x26 -> x0, local copies, waits for them, and re-layouts: 39.3 us -> none  [the longest x9 13.1 us: pick_level(): shaped = field.reshape((field.shape[0] // stride, stride) + field.shape[1:])]
    broadcast_in_dim x27 -> x0, local copies, waits for them, and re-layouts: 33.4 us -> none  [spread_level(): widened = jnp.where(chosen[None, :, :, None], sparse[:, None], fill)]
    dot_general x18 -> x0, matrix products: 22.7 us -> none  [the longest x3 4.83 us: body(): jnp.einsum('hij,ihd->jhd', dscore, picks[0], preferred_element_type=jnp.f...]
    unnamed x102 -> x8, local copies, waits for them, and re-layouts: 15.4 us -> 3.88 us
    transpose x10 -> x0, local copies, waits for them, and re-layouts: 11.2 us -> none  [the longest x2 4.93 us: body(): jnp.einsum('hij,ihd->jhd', weight, picks[3], preferred_element_type=jnp.f...]
    reduce_sum x10 -> x0, other arithmetic: 11.2 us -> none  [the longest x6 9.68 us: pick_level(): return jnp.sum(kept, axis=1, dtype=field.dtype)]
    pallas_call x0 -> x6, Pallas kernels: none -> 10.6 us  [the longest x1 3.7 us: body(): call(run(own_grad_kernel), [(row, BF16), (row, F32), (row, F32)], [(row,...]
    ppermute x10 -> x14, waiting for transfers between devices: 19 us -> 9.36 us  [swap(): return lax.ppermute(block, axis, [(i, i ^ bits) for i in range(count)])]
  transfers between devices with their start and end apart: 11 -> 14, of which waited for: 4 -> 5; matrix products, arithmetic and copies ran while one was open for 37% -> 0% of each run, Pallas kernels for 0% -> 13%
where the time goes in v1:
time: 39.8 us; the launch traced here: 39.5 us
  starting transfers between devices  15 us (38%)
  Pallas kernels  10.6 us (27%)
  waiting for transfers between devices  9.36 us (24%)
  local copies, waits for them, and re-layouts  3.88 us (10%)
  between operations  0.72 us (2%)
    ppermute x14, starting transfers between devices, swap(): return lax.ppermute(block, axis, [(i, i ^ bits) for i in range(count)])  15 us
    ppermute x14, waiting for transfers between devices, swap(): return lax.ppermute(block, axis, [(i, i ^ bits) for i in range(count)])  9.36 us
    unnamed x8, local copies, waits for them, and re-layouts  3.88 us
    pallas_call x1, Pallas kernels, body(): call(run(own_grad_kernel), [(row, BF16), (row, F32), (row, F32)], [(row,...  3.7 us
    pallas_call x1, Pallas kernels, body(): call(run(levels_kernel), [(kept, F32), (stat1, F32), (stat1, F32), ((half...  3.57 us
    pallas_call x1, Pallas kernels, body(): call(run(own_kernel), [(row, BF16), (kept, BF16), (stat, F32), (stat, F32...  1.37 us
    pallas_call x1, Pallas kernels, body(): call(run(last_kernel), [(row, BF16)] * 2)(dk0, dv0, sums[0], *parts)  1.27 us
  transfers between devices with their start and end apart: 14, of which 5 were waited for; matrix products, arithmetic and copies ran while one was open for 0% of the time, Pallas kernels for 13%

profile of v1, /device:TPU:0, one launch (start us, length us, event | category | flops | bytes accessed | tf_op | source)
XLA Modules:
  0.0 39.5 jit_solution(9555249040490780994)
XLA Ops:
  0.6 1.0 %copy-done = bf16[256,640]{1,0:T(8,128)(2,1)S(1)} copy-done((bf16[256,640]{1,0:T(8,128)(2,1)S(1)}, bf16[256,640]{1,0:T(8,128)(2,1)}, u32[]{:S(2)}) %copy-start) | copy-done | bytes 327704
  1.6 1.0 %copy-done.1 = bf16[256,640]{1,0:T(8,128)(2,1)S(1)} copy-done((bf16[256,640]{1,0:T(8,128)(2,1)S(1)}, bf16[256,640]{1,0:T(8,128)(2,1)}, u32[]{:S(2)}) %copy-start.1) | copy-done | bytes 327704
  2.6 1.0 %copy-done.2 = bf16[256,640]{1,0:T(8,128)(2,1)S(1)} copy-done((bf16[256,640]{1,0:T(8,128)(2,1)S(1)}, bf16[256,640]{1,0:T(8,128)(2,1)}, u32[]{:S(2)}) %copy-start.2) | copy-done | bytes 327704
  3.6 1.0 %copy-done.3 = bf16[64,2560]{1,0:T(8,128)(2,1)S(1)} copy-done((bf16[64,2560]{1,0:T(8,128)(2,1)S(1)}, bf16[64,2560]{1,0:T(8,128)(2,1)}, u32[]{:S(2)}) %copy-start.3) | copy-done | bytes 327704
  4.5 0.6 %shard_map.67 = (bf16[256,640]{1,0:T(8,128)(2,1)S(1)}, bf16[256,640]{1,0:T(8,128)(2,1)S(1)}, bf16[256,640]{1,0:T(8,128)(2,1)S(1)}, bf16[64,640]{1,0:T(8,128)(2,1...) custom-call(bf16[256,640]{1,0:T(8,128)(2,1)S(1)} %copy-done, ...), custom_call_target="tpu_custom_call" | custom-call | bytes 1048576 | tf_op jit(solution)/shard_map/pallas_call | solution.py:365
  5.1 3.0 %collective-permute-start.4 = (bf16[128,640]{1,0:T(8,128)(2,1)S(1)}, bf16[128,640]{1,0:T(8,128)(2,1)S(1)}, u32[]{:S(2)}, u32[]{:S(2)}) collective-permute-start(bf16[128,640]{1,0:T(8,128)(2,1)S(1)} %get-tuple-element.47.refs_0_), channel_id=1, source_target_pairs={{0,8},{4,12},{8,0},{12,4},{16,24},{20,28},{24,16},{28,20},{1,9},{5... | collective-permute-start | bytes 491528 | tf_op jit(solution)/shard_map/ppermute | solution.py:354
  8.1 1.6 %collective-permute-start = (bf16[64,640]{1,0:T(8,128)(2,1)S(1)}, bf16[64,640]{1,0:T(8,128)(2,1)S(1)}, u32[]{:S(2)}, u32[]{:S(2)}) collective-permute-start(bf16[64,640]{1,0:T(8,128)(2,1)S(1)} %get-tuple-element.37), channel_id=1, source_target_pairs={{0,1},{1,0},{2,3},{3,2},{4,5},{5,4},{6,7},{7,6},{8,9},{9,8},{10,11... | collective-permute-start | bytes 245768 | tf_op jit(solution)/shard_map/ppermute | solution.py:354
  9.7 2.6 %collective-permute-start.1 = (bf16[64,640]{1,0:T(8,128)(2,1)S(1)}, bf16[64,640]{1,0:T(8,128)(2,1)S(1)}, u32[]{:S(2)}, u32[]{:S(2)}) collective-permute-start(bf16[64,640]{1,0:T(8,128)(2,1)S(1)} %get-tuple-element.38), channel_id=1, source_target_pairs={{0,2},{1,3},{2,0},{3,1},{4,6},{5,7},{6,4},{7,5},{8,10},{9,11},{10,... | collective-permute-start | bytes 245768 | tf_op jit(solution)/shard_map/ppermute | solution.py:354
  12.3 1.5 %collective-permute-start.6 = (bf16[64,640]{1,0:T(8,128)(2,1)S(1)}, bf16[64,640]{1,0:T(8,128)(2,1)S(1)}, u32[]{:S(2)}, u32[]{:S(2)}) collective-permute-start(bf16[64,640]{1,0:T(8,128)(2,1)S(1)} %get-tuple-element.48), channel_id=1, source_target_pairs={{0,16},{4,20},{8,24},{12,28},{16,0},{20,4},{24,8},{28,12},{1,17},{... | collective-permute-start | bytes 245768 | tf_op jit(solution)/shard_map/ppermute | solution.py:354
  13.8 0.5 %collective-permute-start.8 = (bf16[64,640]{1,0:T(8,128)(2,1)S(1)}, bf16[64,640]{1,0:T(8,128)(2,1)S(1)}, u32[]{:S(2)}, u32[]{:S(2)}) collective-permute-start(bf16[64,640]{1,0:T(8,128)(2,1)S(1)} %get-tuple-element.48), channel_id=1, source_target_pairs={{0,24},{4,28},{8,16},{12,20},{16,8},{20,12},{24,0},{28,4},{1,25},{... | collective-permute-start | bytes 245768 | tf_op jit(solution)/shard_map/ppermute | solution.py:354
  14.3 0.0 collective-permute-done.refs_1_
  14.3 0.0 collective-permute-start.3
  14.3 0.0 collective-permute-done.4.refs_2_
  14.3 0.5 %collective-permute-start.5 = (bf16[128,640]{1,0:T(8,128)(2,1)S(1)}, bf16[128,640]{1,0:T(8,128)(2,1)S(1)}, u32[]{:S(2)}, u32[]{:S(2)}) collective-permute-start(bf16[128,640]{1,0:T(8,128)(2,1)S(1)} %collective-permute-done.4.refs_2_), channel_id=1, source_target_pairs={{0,4},{4,0},{8,12},{12,8},{16,20},{20,16},{24,28},{28,24},{1,5},{5... | collective-permute-start | bytes 491528 | tf_op jit(solution)/shard_map/ppermute | solution.py:354
  14.8 1.2 %collective-permute-done.1.refs_2_ = bf16[64,640]{1,0:T(8,128)(2,1)S(1)} collective-permute-done((bf16[64,640]{1,0:T(8,128)(2,1)S(1)}, bf16[64,640]{1,0:T(8,128)(2,1)S(1)}, u32[]{:S(2)}, u32[]{:S(2)}) %collective-permute-start.1) | collective-permute-done | bytes 81952 | tf_op jit(solution)/shard_map/ppermute | solution.py:354
  16.0 1.7 %collective-permute-start.2 = (bf16[64,640]{1,0:T(8,128)(2,1)S(1)}, bf16[64,640]{1,0:T(8,128)(2,1)S(1)}, u32[]{:S(2)}, u32[]{:S(2)}) collective-permute-start(bf16[64,640]{1,0:T(8,128)(2,1)S(1)} %get-tuple-element.39), channel_id=1, source_target_pairs={{0,3},{1,2},{2,1},{3,0},{4,7},{5,6},{6,5},{7,4},{8,11},{9,10},{10,... | collective-permute-start | bytes 245768 | tf_op jit(solution)/shard_map/ppermute | solution.py:354
  17.7 0.0 collective-permute-done.6.refs_4_
  17.7 0.0 collective-permute-start.7
  17.7 1.4 %collective-permute-done.8.refs_6_ = bf16[64,640]{1,0:T(8,128)(2,1)S(1)} collective-permute-done((bf16[64,640]{1,0:T(8,128)(2,1)S(1)}, bf16[64,640]{1,0:T(8,128)(2,1)S(1)}, u32[]{:S(2)}, u32[]{:S(2)}) %collective-permute-start.8) | collective-permute-done | bytes 81952 | tf_op jit(solution)/shard_map/ppermute | solution.py:354
  19.1 0.0 collective-permute-start.9
  19.1 3.1 %collective-permute-done.2.refs_3_ = bf16[64,640]{1,0:T(8,128)(2,1)S(1)} collective-permute-done((bf16[64,640]{1,0:T(8,128)(2,1)S(1)}, bf16[64,640]{1,0:T(8,128)(2,1)S(1)}, u32[]{:S(2)}, u32[]{:S(2)}) %collective-permute-start.2) | collective-permute-done | bytes 81952 | tf_op jit(solution)/shard_map/ppermute | solution.py:354
  22.2 1.4 %shard_map.68 = (bf16[256,640]{1,0:T(8,128)(2,1)S(1)}, bf16[64,640]{1,0:T(8,128)(2,1)S(1)}, f32[256,128]{1,0:T(8,128)S(1)}, f32[256,128]{1,0:T(8,128)S(1)}, f32[...) custom-call(bf16[256,640]{1,0:T(8,128)(2,1)S(1)} %get-tuple-element.33.qp, bf16[256,640]{1,0:T(8,128)(2,1)S(1)} %get-tuple-element.34.kp, ...), custom_call_target="tpu_custom_call" | custom-call | bytes 1048576 | tf_op jit(solution)/shard_map/pallas_call | solution.py:382
  23.7 3.6 %shard_map.69 = (f32[64,640]{1,0:T(8,128)S(1)}, f32[64,128]{1,0:T(8,128)S(1)}, f32[64,128]{1,0:T(8,128)S(1)}, f32[384,640]{1,0:T(8,128)S(1)}, bf16[384,640]{1,0:T(8,128)(2,1)S(1)}) custom-call(bf16[64,640]{1,0:T(8,128)(2,1)S(1)} %get-tuple-element.43.q1, bf16[64,640]{1,0:T(8,128)(2,1)S(1)} %get-tuple-element.44.g1, f32[64,128]{1,0:T(8,128)S(1)} %get-tuple-element.45.lse01, ...), custom_call_target="tpu_custom_call" | custom-call | bytes 1048576 | tf_op jit(solution)/shard_map/pallas_call | solution.py:388
  27.2 0.1 collective-permute-start.10
  27.3 1.9 %collective-permute-done.10.came = bf16[384,640]{1,0:T(8,128)(2,1)S(1)} collective-permute-done((bf16[384,640]{1,0:T(8,128)(2,1)S(1)}, bf16[384,640]{1,0:T(8,128)(2,1)S(1)}, u32[]{:S(2)}, u32[]{:S(2)}) %collective-permute-start.10) | collective-permute-done | bytes 491552 | tf_op jit(solution)/shard_map/ppermute | solution.py:354
  29.2 0.1 shard_map.71
  29.3 0.6 %collective-permute-start.11 = (bf16[128,640]{1,0:T(8,128)(2,1)S(1)}, bf16[128,640]{1,0:T(8,128)(2,1)S(1)}, u32[]{:S(2)}, u32[]{:S(2)}) collective-permute-start(bf16[128,640]{1,0:T(8,128)(2,1)S(1)} %get-tuple-element.58), channel_id=1, source_target_pairs={{0,8},{4,12},{8,0},{12,4},{16,24},{20,28},{24,16},{28,20},{1,9},{5... | collective-permute-start | bytes 491528 | tf_op jit(solution)/shard_map/ppermute | solution.py:354
  29.9 1.5 %collective-permute-start.12 = (bf16[64,640]{1,0:T(8,128)(2,1)S(1)}, bf16[64,640]{1,0:T(8,128)(2,1)S(1)}, u32[]{:S(2)}, u32[]{:S(2)}) collective-permute-start(bf16[64,640]{1,0:T(8,128)(2,1)S(1)} %get-tuple-element.59), channel_id=1, source_target_pairs={{0,16},{4,20},{8,24},{12,28},{16,0},{20,4},{24,8},{28,12},{1,17},{... | collective-permute-start | bytes 245768 | tf_op jit(solution)/shard_map/ppermute | solution.py:354
  31.4 1.4 %collective-permute-start.13 = (bf16[64,640]{1,0:T(8,128)(2,1)S(1)}, bf16[64,640]{1,0:T(8,128)(2,1)S(1)}, u32[]{:S(2)}, u32[]{:S(2)}) collective-permute-start(bf16[64,640]{1,0:T(8,128)(2,1)S(1)} %get-tuple-element.60), channel_id=1, source_target_pairs={{0,24},{4,28},{8,16},{12,20},{16,8},{20,12},{24,0},{28,4},{1,25},{... | collective-permute-start | bytes 245768 | tf_op jit(solution)/shard_map/ppermute | solution.py:354
  32.8 3.7 %shard_map.70 = (bf16[256,640]{1,0:T(8,128)(2,1)}, f32[256,640]{1,0:T(8,128)S(1)}, f32[256,640]{1,0:T(8,128)S(1)}) custom-call(bf16[256,640]{1,0:T(8,128)(2,1)S(1)} %get-tuple-element.33.qp, bf16[256,640]{1,0:T(8,128)(2,1)S(1)} %get-tuple-element.34.kp, bf16[256,640]{1,0:T(8,128)(2,1)S(1)} %get-tuple-element.35.vp, ...), custom_call_target="tpu_custom_call" | custom-call | bytes 1048576 | tf_op jit(solution)/shard_map/pallas_call | solution.py:399
  36.5 1.7 %collective-permute-done.13.refs_2_ = bf16[64,640]{1,0:T(8,128)(2,1)S(1)} collective-permute-done((bf16[64,640]{1,0:T(8,128)(2,1)S(1)}, bf16[64,640]{1,0:T(8,128)(2,1)S(1)}, u32[]{:S(2)}, u32[]{:S(2)}) %collective-permute-start.13) | collective-permute-done | bytes 81952 | tf_op jit(solution)/shard_map/ppermute | solution.py:354
  38.3 1.3 %shard_map.72 = (bf16[256,640]{1,0:T(8,128)(2,1)}, bf16[256,640]{1,0:T(8,128)(2,1)}) custom-call(f32[256,640]{1,0:T(8,128)S(1)} %get-tuple-element.53.dk0, f32[256,640]{1,0:T(8,128)S(1)} %get-tuple-element.54.dv0, f32[128,640]{1,0:T(8,128)S(1)} %get-tuple-element.57.own, bf16[128,640]{1,0:T(8,128)(2,1)S(1)} %collective-permute-done.11.refs_0_, ...), custom_call_target="tpu_custom_call" | custom-call | bytes 1048576 | tf_op jit(solution)/shard_map/pallas_call | solution.py:407
  (10 shorter events, 0.0 us)
Async XLA Ops:
  0.6 1.0 %copy-start = (bf16[256,640]{1,0:T(8,128)(2,1)S(1)}, bf16[256,640]{1,0:T(8,128)(2,1)}, u32[]{:S(2)}) copy-start(bf16[256,640]{1,0:T(8,128)(2,1)} %q_ref.1) | copy-start | bytes 983044
  1.6 1.0 %copy-start.1 = (bf16[256,640]{1,0:T(8,128)(2,1)S(1)}, bf16[256,640]{1,0:T(8,128)(2,1)}, u32[]{:S(2)}) copy-start(bf16[256,640]{1,0:T(8,128)(2,1)} %k_ref.1) | copy-start | bytes 983044
  2.6 1.0 %copy-start.2 = (bf16[256,640]{1,0:T(8,128)(2,1)S(1)}, bf16[256,640]{1,0:T(8,128)(2,1)}, u32[]{:S(2)}) copy-start(bf16[256,640]{1,0:T(8,128)(2,1)} %v_ref.1) | copy-start | bytes 983044
  3.6 1.0 %copy-start.3 = (bf16[64,2560]{1,0:T(8,128)(2,1)S(1)}, bf16[64,2560]{1,0:T(8,128)(2,1)}, u32[]{:S(2)}) copy-start(bf16[64,2560]{1,0:T(8,128)(2,1)} %g_ref.1) | copy-start | bytes 983044
  5.1 9.2 %collective-permute-start.4 = (bf16[128,640]{1,0:T(8,128)(2,1)S(1)}, bf16[128,640]{1,0:T(8,128)(2,1)S(1)}, u32[]{:S(2)}, u32[]{:S(2)}) collective-permute-start(bf16[128,640]{1,0:T(8,128)(2,1)S(1)} %get-tuple-element.47.refs_0_), channel_id=1, source_target_pairs={{0,8},{4,12},{8,0},{12,4},{16,24},{20,28},{24,16},{28,20},{1,9},{5... | collective-permute-start | bytes 491528 | tf_op jit(solution)/shard_map/ppermute | solution.py:354
  8.1 6.2 %collective-permute-start = (bf16[64,640]{1,0:T(8,128)(2,1)S(1)}, bf16[64,640]{1,0:T(8,128)(2,1)S(1)}, u32[]{:S(2)}, u32[]{:S(2)}) collective-permute-start(bf16[64,640]{1,0:T(8,128)(2,1)S(1)} %get-tuple-element.37), channel_id=1, source_target_pairs={{0,1},{1,0},{2,3},{3,2},{4,5},{5,4},{6,7},{7,6},{8,9},{9,8},{10,11... | collective-permute-start | bytes 245768 | tf_op jit(solution)/shard_map/ppermute | solution.py:354
  9.7 6.3 %collective-permute-start.1 = (bf16[64,640]{1,0:T(8,128)(2,1)S(1)}, bf16[64,640]{1,0:T(8,128)(2,1)S(1)}, u32[]{:S(2)}, u32[]{:S(2)}) collective-permute-start(bf16[64,640]{1,0:T(8,128)(2,1)S(1)} %get-tuple-element.38), channel_id=1, source_target_pairs={{0,2},{1,3},{2,0},{3,1},{4,6},{5,7},{6,4},{7,5},{8,10},{9,11},{10,... | collective-permute-start | bytes 245768 | tf_op jit(solution)/shard_map/ppermute | solution.py:354
  12.3 5.4 %collective-permute-start.6 = (bf16[64,640]{1,0:T(8,128)(2,1)S(1)}, bf16[64,640]{1,0:T(8,128)(2,1)S(1)}, u32[]{:S(2)}, u32[]{:S(2)}) collective-permute-start(bf16[64,640]{1,0:T(8,128)(2,1)S(1)} %get-tuple-element.48), channel_id=1, source_target_pairs={{0,16},{4,20},{8,24},{12,28},{16,0},{20,4},{24,8},{28,12},{1,17},{... | collective-permute-start | bytes 245768 | tf_op jit(solution)/shard_map/ppermute | solution.py:354
  13.8 5.3 %collective-permute-start.8 = (bf16[64,640]{1,0:T(8,128)(2,1)S(1)}, bf16[64,640]{1,0:T(8,128)(2,1)S(1)}, u32[]{:S(2)}, u32[]{:S(2)}) collective-permute-start(bf16[64,640]{1,0:T(8,128)(2,1)S(1)} %get-tuple-element.48), channel_id=1, source_target_pairs={{0,24},{4,28},{8,16},{12,20},{16,8},{20,12},{24,0},{28,4},{1,25},{... | collective-permute-start | bytes 245768 | tf_op jit(solution)/shard_map/ppermute | solution.py:354
  14.3 9.4 %collective-permute-start.3 = (bf16[128,640]{1,0:T(8,128)(2,1)S(1)}, bf16[128,640]{1,0:T(8,128)(2,1)S(1)}, u32[]{:S(2)}, u32[]{:S(2)}) collective-permute-start(bf16[128,640]{1,0:T(8,128)(2,1)S(1)} %get-tuple-element.47.refs_0_), channel_id=1, source_target_pairs={{0,4},{4,0},{8,12},{12,8},{16,20},{20,16},{24,28},{28,24},{1,5},{5... | collective-permute-start | bytes 491528 | tf_op jit(solution)/shard_map/ppermute | solution.py:354
  14.3 9.4 %collective-permute-start.5 = (bf16[128,640]{1,0:T(8,128)(2,1)S(1)}, bf16[128,640]{1,0:T(8,128)(2,1)S(1)}, u32[]{:S(2)}, u32[]{:S(2)}) collective-permute-start(bf16[128,640]{1,0:T(8,128)(2,1)S(1)} %collective-permute-done.4.refs_2_), channel_id=1, source_target_pairs={{0,4},{4,0},{8,12},{12,8},{16,20},{20,16},{24,28},{28,24},{1,5},{5... | collective-permute-start | bytes 491528 | tf_op jit(solution)/shard_map/ppermute | solution.py:354
  16.0 6.2 %collective-permute-start.2 = (bf16[64,640]{1,0:T(8,128)(2,1)S(1)}, bf16[64,640]{1,0:T(8,128)(2,1)S(1)}, u32[]{:S(2)}, u32[]{:S(2)}) collective-permute-start(bf16[64,640]{1,0:T(8,128)(2,1)S(1)} %get-tuple-element.39), channel_id=1, source_target_pairs={{0,3},{1,2},{2,1},{3,0},{4,7},{5,6},{6,5},{7,4},{8,11},{9,10},{10,... | collective-permute-start | bytes 245768 | tf_op jit(solution)/shard_map/ppermute | solution.py:354
  17.7 5.9 %collective-permute-start.7 = (bf16[64,640]{1,0:T(8,128)(2,1)S(1)}, bf16[64,640]{1,0:T(8,128)(2,1)S(1)}, u32[]{:S(2)}, u32[]{:S(2)}) collective-permute-start(bf16[64,640]{1,0:T(8,128)(2,1)S(1)} %collective-permute-done.6.refs_4_), channel_id=1, source_target_pairs={{0,4},{4,0},{8,12},{12,8},{16,20},{20,16},{24,28},{28,24},{1,5},{5... | collective-permute-start | bytes 245768 | tf_op jit(solution)/shard_map/ppermute | solution.py:354
  19.1 4.5 %collective-permute-start.9 = (bf16[64,640]{1,0:T(8,128)(2,1)S(1)}, bf16[64,640]{1,0:T(8,128)(2,1)S(1)}, u32[]{:S(2)}, u32[]{:S(2)}) collective-permute-start(bf16[64,640]{1,0:T(8,128)(2,1)S(1)} %collective-permute-done.8.refs_6_), channel_id=1, source_target_pairs={{0,4},{4,0},{8,12},{12,8},{16,20},{20,16},{24,28},{28,24},{1,5},{5... | collective-permute-start | bytes 245768 | tf_op jit(solution)/shard_map/ppermute | solution.py:354
  27.2 1.9 %collective-permute-start.10 = (bf16[384,640]{1,0:T(8,128)(2,1)S(1)}, bf16[384,640]{1,0:T(8,128)(2,1)S(1)}, u32[]{:S(2)}, u32[]{:S(2)}) collective-permute-start(bf16[384,640]{1,0:T(8,128)(2,1)S(1)} %get-tuple-element.56), channel_id=1, source_target_pairs={{0,4},{4,0},{8,12},{12,8},{16,20},{20,16},{24,28},{28,24},{1,5},{5... | collective-permute-start | bytes 1474568 | tf_op jit(solution)/shard_map/ppermute | solution.py:354
  29.3 9.0 %collective-permute-start.11 = (bf16[128,640]{1,0:T(8,128)(2,1)S(1)}, bf16[128,640]{1,0:T(8,128)(2,1)S(1)}, u32[]{:S(2)}, u32[]{:S(2)}) collective-permute-start(bf16[128,640]{1,0:T(8,128)(2,1)S(1)} %get-tuple-element.58), channel_id=1, source_target_pairs={{0,8},{4,12},{8,0},{12,4},{16,24},{20,28},{24,16},{28,20},{1,9},{5... | collective-permute-start | bytes 491528 | tf_op jit(solution)/shard_map/ppermute | solution.py:354
  29.9 6.7 %collective-permute-start.12 = (bf16[64,640]{1,0:T(8,128)(2,1)S(1)}, bf16[64,640]{1,0:T(8,128)(2,1)S(1)}, u32[]{:S(2)}, u32[]{:S(2)}) collective-permute-start(bf16[64,640]{1,0:T(8,128)(2,1)S(1)} %get-tuple-element.59), channel_id=1, source_target_pairs={{0,16},{4,20},{8,24},{12,28},{16,0},{20,4},{24,8},{28,12},{1,17},{... | collective-permute-start | bytes 245768 | tf_op jit(solution)/shard_map/ppermute | solution.py:354
  31.4 6.9 %collective-permute-start.13 = (bf16[64,640]{1,0:T(8,128)(2,1)S(1)}, bf16[64,640]{1,0:T(8,128)(2,1)S(1)}, u32[]{:S(2)}, u32[]{:S(2)}) collective-permute-start(bf16[64,640]{1,0:T(8,128)(2,1)S(1)} %get-tuple-element.60), channel_id=1, source_target_pairs={{0,24},{4,28},{8,16},{12,20},{16,8},{20,12},{24,0},{28,4},{1,25},{... | collective-permute-start | bytes 245768 | tf_op jit(solution)/shard_map/ppermute | solution.py:354

commit v2 on v1

--- a/solution.py
+++ b/solution.py
@@ -17,7 +17,7 @@
 F32 = jnp.float32
 SCALE = HD**-0.5
 SCALE2 = SCALE * math.log2(math.e)
-VMEM_BYTES = 48 * 2**20
+VMEM_BYTES = 28 * 2**20
 
 
 class Plan:
@@ -115,38 +115,74 @@
     return jnp.where(qpos >= kpos, 0.0, -jnp.inf)
 
 
-def call(kernel, outs, scratch=(), flops=0):
+def call(kernel, outs, scratch=(), flops=0, specs=None):
     return pl.pallas_call(
         kernel,
         out_shape=[jax.ShapeDtypeStruct(s, d) for s, d in outs],
-        scratch_shapes=[pltpu.VMEM(s, d) for s, d in scratch],
+        **({} if specs is None else {"in_specs": specs}),
+        scratch_shapes=[pltpu.VMEM(*s) if isinstance(s, tuple) else s for s in scratch],
         compiler_params=pltpu.CompilerParams(vmem_limit_bytes=VMEM_BYTES),
         cost_estimate=pl.CostEstimate(flops=flops, bytes_accessed=2**20, transcendentals=0),
     )
 
 
-def pack_kernel(p, q_ref, k_ref, v_ref, g_ref, qp, kp, vp, q1, kv1, kv2, *gz):
-    z = lax.axis_index("head")
-    for b in range(p.zcount):
-        start = pl.multiple_of(jnp.bitwise_xor(z, b) * p.width, LANES)
-        gz[b][...] = g_ref[:, pl.ds(start, p.width)]
+def slab(p, g_ref, b):
+    start = pl.multiple_of(jnp.bitwise_xor(lax.axis_index("head"), b) * p.width, LANES)
+    return g_ref.at[:, pl.ds(start, p.width)]
+
+
+def far_kernel(p, g_ref, out, sem):
+    copy = pltpu.make_async_copy(slab(p, g_ref, p.zcount - 1), out, sem)
+    copy.start()
+    copy.wait()
+
+
+def pack_kernel(p, q_ref, k_ref, v_ref, g_ref, qp, kp, vp, q1, kv1, kv2, *refs):
+    gz, (q_in, k_in, v_in, sems) = refs[: p.zcount - 1], refs[p.zcount - 1 :]
+    loads = [(k_ref, k_in), (v_ref, v_in), (q_ref, q_in)]
+    loads += [(slab(p, g_ref, b), gz[b]) for b in range(p.zcount - 1)]
+    copies = [pltpu.make_async_copy(src, dst, sems.at[i]) for i, (src, dst) in enumerate(loads)]
+    for copy in copies:
+        copy.start()
     order = phase_order(p)
     label = column_class(p)
-    k = nn(order, k_ref[...])
+    copies[0].wait()
+    k = nn(order, k_in[...])
     kp[...] = k.astype(BF16)
     k_kept = pick(p, k, label)
-    v = nn(order, v_ref[...])
+    copies[1].wait()
+    v = nn(order, v_in[...])
     vp[...] = v.astype(BF16)
     v_kept = pick(p, v, label)
     kv1[...] = jnp.concatenate([k_kept, v_kept], axis=0).astype(BF16)
     kv2[...] = jnp.concatenate([k_kept[: p.n2], v_kept[: p.n2]], axis=0).astype(BF16)
-    q = nn(order, q_ref[...])
+    copies[2].wait()
+    q = nn(order, q_in[...])
     qp[...] = q.astype(BF16)
     q1[...] = pick(p, q, label).astype(BF16)
-
-
-def own_kernel(p, qp, kp, vp, *refs):
-    gz, (gp, g1, lse0, d0, lse01, d01, natural) = refs[: p.zcount], refs[p.zcount :]
+    for copy in copies[3:]:
+        copy.wait()
+
+
+def own_scores_kernel(p, qp, kp, weight, lse0, lse01):
+    bias = own_bias(p)
+    lane = iota((1, LANES), 1)
+    lse_all = jnp.zeros((p.tokens, LANES), F32)
+    for h in range(p.heads):
+        low, high = window(h)
+        mask = jnp.where(window_mask(h, low, high), 1.0, 0.0).astype(BF16)
+        s = nt(qp[:, low:high] * mask, kp[:, low:high]) * SCALE2 + bias
+        top = jnp.max(s, axis=1, keepdims=True)
+        e = jnp.exp2(s - top)
+        denom = jnp.sum(e, axis=1, keepdims=True)
+        weight[h * p.tokens : (h + 1) * p.tokens, :] = e * (1.0 / denom)
+        lse_all = jnp.where(lane == h, top + jnp.log2(denom), lse_all)
+    lse0[...] = lse_all
+    lse01[...] = pick(p, lse_all, lane_class(p))
+
+
+def own_delta_kernel(p, vp, weight, *refs):
+    gz, (gp, g1, dprob, d0, d01, natural) = refs[: p.zcount], refs[p.zcount :]
     z = lax.axis_index("head")
     share = p.tokens // p.zcount
     for b in range(p.zcount):
@@ -155,26 +191,26 @@
     g = nn(phase_order(p), natural[...])
     gp[...] = g.astype(BF16)
     g1[...] = pick(p, g, column_class(p)).astype(BF16)
-    bias = own_bias(p)
     lane = iota((1, LANES), 1)
-    lse_all = jnp.zeros((p.tokens, LANES), F32)
     d_all = jnp.zeros((p.tokens, LANES), F32)
     for h in range(p.heads):
         low, high = window(h)
+        rows = slice(h * p.tokens, (h + 1) * p.tokens)
         mask = jnp.where(window_mask(h, low, high), 1.0, 0.0).astype(BF16)
-        s = nt(qp[:, low:high] * mask, kp[:, low:high]) * SCALE2 + bias
-        top = jnp.max(s, axis=1, keepdims=True)
-        e = jnp.exp2(s - top)
-        denom = jnp.sum(e, axis=1, keepdims=True)
         dp = nt(gp[:, low:high] * mask, vp[:, low:high])
-        d = jnp.sum(e * dp, axis=1, keepdims=True) / denom
-        lse_all = jnp.where(lane == h, top + jnp.log2(denom), lse_all)
+        dprob[rows, :] = dp
+        d = jnp.sum(weight[rows, :] * dp, axis=1, keepdims=True)
         d_all = jnp.where(lane == h, d, d_all)
-    lse0[...] = lse_all
     d0[...] = d_all
-    label = lane_class(p)
-    lse01[...] = pick(p, lse_all, label)
-    d01[...] = pick(p, d_all, label)
+    d01[...] = pick(p, d_all, lane_class(p))
+
+
+def merge_kernel(p, *refs):
+    out = refs[-1]
+    at = 0
+    for ref in refs[:-1]:
+        out[at : at + ref.shape[0], :] = ref[...]
+        at += ref.shape[0]
 
 
 def columns(p, stat):
@@ -202,8 +238,19 @@
 
 
 def by_head(p, rows):
-    parts = [jnp.where(head_mask(p, h), rows, 0.0) for h in range(p.heads)]
+    if rows.shape[0] % 16:
+        rows = rows.astype(F32)
+    parts = []
+    for h in range(p.heads):
+        mask = jnp.where(head_mask(p, h), 1.0, 0.0).astype(rows.dtype)
+        parts.append(rows * mask)
     return jnp.concatenate(parts, axis=0).astype(BF16)
+
+
+def cut(p, block, start, count):
+    if start % 16 or count % 16:
+        block = block.astype(F32)
+    return block[start : start + count]
 
 
 def merge_heads(p, rows, count):
@@ -213,21 +260,25 @@
     return out
 
 
-def levels_kernel(p, q1, g1, lse01, d01, *refs):
-    kv = refs[: p.g2]
-    dq1, total1, delta1, keep, send = refs[p.g2 :]
+def scores_kernel(p, q1, lse01, came, *refs):
+    even = refs[: p.g2 // 2]
+    k1, v1, k2, v2, p1, p2, total1, share1 = refs[p.g2 // 2 :]
     d = lax.axis_index("seq")
     n1, n2 = p.n1, p.n2
-    blocks = [ref[...].astype(F32) for ref in kv]
-    k1 = jnp.concatenate([blocks[b][:n1] for b in range(p.g1)], axis=0).astype(BF16)
-    v1 = jnp.concatenate([blocks[b][n1:] for b in range(p.g1)], axis=0).astype(BF16)
-    k2 = jnp.concatenate([block[:n2] for block in blocks], axis=0).astype(BF16)
-    v2 = jnp.concatenate(
-        [block[half : half + n2] for block, half in zip(blocks, [r // 2 for r in p.rows])], axis=0
-    ).astype(BF16)
-    q_rows, g_rows = q1[...].astype(F32), g1[...].astype(F32)
-    q1b, g1b = by_head(p, q_rows), by_head(p, g_rows)
-    q2b, g2b = by_head(p, q_rows[:n2]), by_head(p, g_rows[:n2])
+    blocks, at = [], 0
+    for b in range(p.g2):
+        if b % 2 == 0:
+            blocks.append(even[b // 2][...])
+        else:
+            blocks.append(came[at : at + p.rows[b], :])
+            at += p.rows[b]
+    for half, (out1, out2) in enumerate(((k1, k2), (v1, v2))):
+        parts = [cut(p, blocks[b], half * n1, n1) for b in range(p.g1)]
+        out1[...] = jnp.concatenate(parts, axis=0).astype(BF16)
+        parts = [cut(p, blocks[b], half * p.rows[b] // 2, n2) for b in range(p.g2)]
+        out2[...] = jnp.concatenate(parts, axis=0).astype(BF16)
+    q_rows = q1[...]
+    q1b, q2b = by_head(p, q_rows), by_head(p, cut(p, q_rows, 0, n2))
 
     shape1 = (p.heads * n1, p.g1 * n1)
     row = iota((shape1[0], 1), 0)
@@ -238,35 +289,45 @@
     other = col % n1
     kbase = p.tokens * jnp.bitwise_xor(d, col // n1) + p.r2 * (other % n2)
     kpos = kbase + jnp.bitwise_and(head + DIL1 * (other // n2), p.r2 - 1)
-    s1 = jnp.where(kpos <= qpos, nt(q1b, k1) * SCALE2, -jnp.inf)
+    s1 = jnp.where(kpos <= qpos, nt(q1b, k1[...]) * SCALE2, -jnp.inf)
     top1 = jnp.max(s1, axis=1, keepdims=True)
-    lse1 = top1 + jnp.log2(jnp.sum(jnp.exp2(s1 - top1), axis=1, keepdims=True))
+    e1 = jnp.exp2(s1 - top1)
+    lse1 = top1 + jnp.log2(jnp.sum(e1, axis=1, keepdims=True))
 
     row2 = d * n2 + iota((p.heads * n2, 1), 0) % n2
     col2 = iota((1, p.g2 * n2), 1)
     col2 = jnp.bitwise_xor(d, col2 // n2) * n2 + col2 % n2
-    s2 = jnp.where(col2 <= row2, nt(q2b, k2) * SCALE2, -jnp.inf)
+    s2 = jnp.where(col2 <= row2, nt(q2b, k2[...]) * SCALE2, -jnp.inf)
     top2 = jnp.max(s2, axis=1, keepdims=True)
-    lse2 = top2 + jnp.log2(jnp.sum(jnp.exp2(s2 - top2), axis=1, keepdims=True))
+    e2 = jnp.exp2(s2 - top2)
+    lse2 = top2 + jnp.log2(jnp.sum(e2, axis=1, keepdims=True))
 
     lse0 = columns(p, lse01[...])
     lse2 = widen(p, lse2, -jnp.inf)
     peak = jnp.maximum(jnp.maximum(lse0, lse1), lse2)
-    share0 = jnp.exp2(lse0 - peak)
-    total = peak + jnp.log2(share0 + jnp.exp2(lse1 - peak) + jnp.exp2(lse2 - peak))
-    p1 = jnp.exp2(s1 - total)
-    p2 = jnp.exp2(s2 - wide_rows(p, total))
-    dp1 = nt(g1b, v1)
-    dp2 = nt(g2b, v2)
-    delta = jnp.exp2(lse0 - total) * columns(p, d01[...])
-    delta += jnp.sum(p1 * dp1, axis=1, keepdims=True)
-    delta += widen(p, jnp.sum(p2 * dp2, axis=1, keepdims=True), 0.0)
-    ds1 = (p1 * (dp1 - delta) * SCALE).astype(BF16)
-    ds2 = (p2 * (dp2 - wide_rows(p, delta)) * SCALE).astype(BF16)
-    p1, p2 = p1.astype(BF16), p2.astype(BF16)
+    total = peak + jnp.log2(jnp.exp2(lse0 - peak) + jnp.exp2(lse1 - peak) + jnp.exp2(lse2 - peak))
+    p1[...] = e1 * jnp.exp2(top1 - total)
+    p2[...] = e2 * jnp.exp2(top2 - wide_rows(p, total))
+    total1[...] = to_lanes(p, total)
+    share1[...] = to_lanes(p, jnp.exp2(lse0 - total))
+
+
+def levels_kernel(p, q1, g1, k1, v1, k2, v2, p1, p2, share1, d01, dq1, delta1, keep, send):
+    n1, n2 = p.n1, p.n2
+    q_rows, g_rows = q1[...], g1[...]
+    q1b, g1b = by_head(p, q_rows), by_head(p, g_rows)
+    q2b, g2b = by_head(p, cut(p, q_rows, 0, n2)), by_head(p, cut(p, g_rows, 0, n2))
+    prob1, prob2 = p1[...], p2[...]
+    dp1 = nt(g1b, v1[...])
+    dp2 = nt(g2b, v2[...])
+    delta = columns(p, share1[...] * d01[...])
+    delta += jnp.sum(prob1 * dp1, axis=1, keepdims=True)
+    delta += widen(p, jnp.sum(prob2 * dp2, axis=1, keepdims=True), 0.0)
+    ds1 = (prob1 * (dp1 - delta) * SCALE).astype(BF16)
+    ds2 = (prob2 * (dp2 - wide_rows(p, delta)) * SCALE).astype(BF16)
 
     dk1, dk2 = tn(ds1, q1b), tn(ds2, q2b)
-    dv1, dv2 = tn(p1, g1b), tn(p2, g2b)
+    dv1, dv2 = tn(prob1.astype(BF16), g1b), tn(prob2.astype(BF16), g2b)
     at = [0, 0]
     for b in range(p.g2):
         rows = slice(b * n2, (b + 1) * n2)
@@ -281,10 +342,9 @@
         ref = send if odd else keep
         ref[at[odd] : at[odd] + p.rows[b], :] = part.astype(ref.dtype)
         at[odd] += p.rows[b]
-    dq = merge_heads(p, nn(ds1, k1), n1)
-    wide = merge_heads(p, nn(ds2, k2), n2)
+    dq = merge_heads(p, nn(ds1, k1[...]), n1)
+    wide = merge_heads(p, nn(ds2, k2[...]), n2)
     dq1[...] = jnp.concatenate([dq[:n2] + wide, dq[n2:]], axis=0)
-    total1[...] = to_lanes(p, total)
     delta1[...] = to_lanes(p, delta)
 
 
@@ -300,26 +360,25 @@
         at += p.rows[b]
 
 
-def own_grad_kernel(p, qp, kp, vp, gp, lse0, d0, total1, delta1, dq1, grad_q, dk0, dv0, dq):
+def own_grad_kernel(
+    p, qp, kp, gp, weight, dprob, lse0, d0, total1, delta1, dq1, grad_q, dk0, dv0, dq
+):
     label = lane_class(p)
-    total = spread(p, total1[...], label, lse0[...])
+    lse = lse0[...]
+    share = jnp.exp2(lse - spread(p, total1[...], label, lse))
     delta = spread(p, delta1[...], label, d0[...])
-    bias = own_bias(p)
-    for ref in (dq, dk0, dv0):
+    for ref in (dk0, dv0):
         ref[...] = jnp.zeros_like(ref)
     for h in range(p.heads):
         low, high = window(h)
+        rows = slice(h * p.tokens, (h + 1) * p.tokens)
         hit = window_mask(h, low, high)
         mask = jnp.where(hit, 1.0, 0.0).astype(BF16)
-        q = qp[:, low:high] * mask
-        g = gp[:, low:high] * mask
-        k = kp[:, low:high]
-        prob = jnp.exp2(nt(q, k) * SCALE2 + bias - total[:, h : h + 1])
-        dp = nt(g, vp[:, low:high])
-        ds = (prob * (dp - delta[:, h : h + 1]) * SCALE).astype(BF16)
-        dq[:, low:high] = jnp.where(hit, nn(ds, k), dq[:, low:high])
-        dk0[:, low:high] += tn(ds, q)
-        dv0[:, low:high] += tn(prob.astype(BF16), g)
+        prob = weight[rows, :] * share[:, h : h + 1]
+        ds = (prob * (dprob[rows, :] - delta[:, h : h + 1]) * SCALE).astype(BF16)
+        dq[:, low:high] = jnp.where(hit, nn(ds, kp[:, low:high]), dq[:, low:high])
+        dk0[:, low:high] += tn(ds, qp[:, low:high] * mask)
+        dv0[:, low:high] += tn(prob.astype(BF16), gp[:, low:high] * mask)
     zero = jnp.zeros((p.tokens, p.width), F32)
     all_q = dq[...] + spread(p, dq1[...], column_class(p), zero)
     grad_q[...] = nn(phase_order(p, True), all_q.astype(BF16)).astype(BF16)
@@ -356,54 +415,70 @@
 
 def body(queries, keys, values, grad_out):
     tokens, width = queries.shape
+    queries, keys, values, grad_out = (
+        pltpu.with_memory_space_constraint(field, pltpu.HBM)
+        for field in (queries, keys, values, grad_out)
+    )
     p = Plan(tokens, width, lax.axis_size("seq"), lax.axis_size("head"))
     n1, n2 = p.n1, p.n2
     run = lambda kernel: functools.partial(kernel, p)
     row, kept = (tokens, width), (n1, width)
     share = (tokens // p.zcount, width)
-
+    stat, stat1 = (tokens, LANES), (n1, LANES)
+    flat = lambda count: (count, tokens)
+    even = range(0, p.g2, 2)
+    half_rows = sum(p.rows[::2])
+    hbm = pl.BlockSpec(memory_space=pltpu.HBM)
+
+    (far,) = call(run(far_kernel), [(share, BF16)], [pltpu.SemaphoreType.DMA], specs=[hbm])(grad_out)
     outs = call(
         run(pack_kernel),
         [(row, BF16)] * 3
         + [(kept, BF16), ((2 * n1, width), BF16), ((2 * n2, width), BF16)]
-        + [(share, BF16)] * p.zcount,
+        + [(share, BF16)] * (p.zcount - 1),
+        [(row, BF16)] * 3 + [pltpu.SemaphoreType.DMA((p.zcount + 2,))],
+        specs=[hbm] * 4,
     )(queries, keys, values, grad_out)
     qp, kp, vp, q1, kv1, kv2 = outs[:6]
-    gz = outs[6:]
+    gz = [*outs[6:], far]
     gz = [gz[0]] + [swap(gz[b], "head", b) for b in range(1, p.zcount)]
 
-    kv = {0: kv1}
-    for b in range(2, p.g2, 2):
-        kv[b] = swap(kv1 if b < p.g1 else kv2, "seq", b)
-    for b in range(0, p.g2, 2):
-        kv[b + 1] = swap(kv[b], "seq", 1)
-
-    stat, stat1 = (tokens, LANES), (n1, LANES)
-    gp, g1, lse0, d0, lse01, d01 = call(
-        run(own_kernel),
-        [(row, BF16), (kept, BF16), (stat, F32), (stat, F32), (stat1, F32), (stat1, F32)],
+    kv = [kv1] + [swap(kv1 if b < p.g1 else kv2, "seq", b) for b in even[1:]]
+    (sent,) = call(run(merge_kernel), [((half_rows, width), BF16)])(*kv)
+    came = swap(sent, "seq", 1)
+
+    weight, lse0, lse01 = call(
+        run(own_scores_kernel), [(flat(p.heads * tokens), F32), (stat, F32), (stat1, F32)]
+    )(qp, kp)
+    k1, v1, k2, v2, p1, p2, total1, share1 = call(
+        run(scores_kernel),
+        [(row, BF16)] * 4
+        + [(flat(p.heads * n1), F32), (flat(p.heads * n2), F32), (stat1, F32), (stat1, F32)],
+    )(q1, lse01, came, *kv)
+    gp, g1, dprob, d0, d01 = call(
+        run(own_delta_kernel),
+        [(row, BF16), (kept, BF16), (flat(p.heads * tokens), F32), (stat, F32), (stat1, F32)],
         [(row, BF16)],
-    )(qp, kp, vp, *gz)
-    half_rows = sum(p.rows[::2])
-    dq1, total1, delta1, keep, send = call(
+        flops=2 * 10**10,
+    )(vp, weight, *gz)
+    dq1, delta1, keep, send = call(
         run(levels_kernel),
         [
             (kept, F32),
             (stat1, F32),
-            (stat1, F32),
             ((half_rows, width), F32),
             ((half_rows, width), BF16),
         ],
-    )(q1, g1, lse01, d01, *[kv[b] for b in range(p.g2)])
-    came = swap(send, "seq", 1)
+    )(q1, g1, k1, v1, k2, v2, p1, p2, share1, d01)
+    returned = swap(send, "seq", 1)
     grad_q, dk0, dv0 = call(
         run(own_grad_kernel), [(row, BF16), (row, F32), (row, F32)], [(row, F32)]
-    )(qp, kp, vp, gp, lse0, d0, total1, delta1, dq1)
+    )(qp, kp, gp, weight, dprob, lse0, d0, total1, delta1, dq1)
     sums = call(
         run(chip_kernel),
-        [((p.rows[0], width), F32)] + [((p.rows[b], width), BF16) for b in range(2, p.g2, 2)],
-    )(keep, came)
-    parts = [swap(s, "seq", b) for s, b in zip(sums[1:], range(2, p.g2, 2))]
+        [((p.rows[0], width), F32)] + [((p.rows[b], width), BF16) for b in even[1:]],
+    )(keep, returned)
+    parts = [swap(s, "seq", b) for s, b in zip(sums[1:], even[1:])]
     grad_k, grad_v = call(run(last_kernel), [(row, BF16)] * 2)(dk0, dv0, sums[0], *parts)
     return grad_q, grad_k, grad_v
 

time: 39.8 us -> 35.6 us (0.89)
  local copies, waits for them, and re-layouts: 3.88 us -> 0 us
  Pallas kernels: 10.6 us -> 11.9 us
  starting transfers between devices: 15 us -> 13.9 us
  waiting for transfers between devices: 9.36 us -> 8.84 us
    unnamed x8 -> x0, local copies, waits for them, and re-layouts: 3.88 us -> none
    pallas_call x1, Pallas kernels: 0.57 us -> 1.91 us  [body(): call(run(pack_kernel), [(row, BF16)] * 3 + [(kept, BF16), ((2 * n1, width...]
    pallas_call x2 -> x6, Pallas kernels: 4.94 us -> 6.08 us  [the longest x1 2.2 us: body(): call(run(levels_kernel), [(kept, F32), (stat1, F32), ((half_rows, width),...]
    pallas_call x1, Pallas kernels: 3.7 us -> 2.6 us  [body(): call(run(own_grad_kernel), [(row, BF16), (row, F32), (row, F32)], [(row,...]
    ppermute x14 -> x11, starting transfers between devices: 15 us -> 13.9 us  [swap(): return lax.ppermute(block, axis, [(i, i ^ bits) for i in range(count)])]
    ppermute x14 -> x11, waiting for transfers between devices: 9.36 us -> 8.84 us  [swap(): return lax.ppermute(block, axis, [(i, i ^ bits) for i in range(count)])]
  transfers between devices with their start and end apart: 14 -> 11, of which waited for: 5 -> 4; matrix products, arithmetic and copies ran while one was open for 0% -> 0% of each run, Pallas kernels for 13% -> 15%
where the time goes in v2:
time: 35.6 us; the launch traced here: 35.5 us
  starting transfers between devices  13.9 us (39%)
  Pallas kernels  11.9 us (33%)
  waiting for transfers between devices  8.84 us (25%)
  between operations  0.75 us (2%)
    ppermute x11, starting transfers between devices, swap(): return lax.ppermute(block, axis, [(i, i ^ bits) for i in range(count)])  13.9 us
    ppermute x11, waiting for transfers between devices, swap(): return lax.ppermute(block, axis, [(i, i ^ bits) for i in range(count)])  8.84 us
    pallas_call x1, Pallas kernels, body(): call(run(own_grad_kernel), [(row, BF16), (row, F32), (row, F32)], [(row,...  2.6 us
    pallas_call x1, Pallas kernels, body(): call(run(levels_kernel), [(kept, F32), (stat1, F32), ((half_rows, width),...  2.2 us
    pallas_call x1, Pallas kernels, body(): call(run(pack_kernel), [(row, BF16)] * 3 + [(kept, BF16), ((2 * n1, width...  1.91 us
    pallas_call x1, Pallas kernels, body(): call(run(scores_kernel), [(row, BF16)] * 4 + [(flat(p.heads * n1), F32),...  1.29 us
    pallas_call x1, Pallas kernels, body(): call(run(last_kernel), [(row, BF16)] * 2)(dk0, dv0, sums[0], *parts)  1.27 us
    pallas_call x1, Pallas kernels, body(): call(run(own_scores_kernel), [(flat(p.heads * tokens), F32), (stat, F32),...  0.94 us
  transfers between devices with their start and end apart: 11, of which 4 were waited for; matrix products, arithmetic and copies ran while one was open for 0% of the time, Pallas kernels for 15%

profile of v2, /device:TPU:0, one launch (start us, length us, event | category | flops | bytes accessed | tf_op | source)
XLA Modules:
  0.0 35.5 jit_solution(16623013021668340227)
XLA Ops:
  0.6 1.9 %shard_map.67 = (bf16[256,640]{1,0:T(8,128)(2,1)S(1)}, bf16[256,640]{1,0:T(8,128)(2,1)S(1)}, bf16[256,640]{1,0:T(8,128)(2,1)S(1)}, bf16[64,640]{1,0:T(8,128)(2,1...) custom-call(bf16[256,640]{1,0:T(8,128)(2,1)} %q_ref.1, ...), custom_call_target="tpu_custom_call" | custom-call | bytes 1048576 | tf_op jit(solution)/shard_map/pallas_call | solution.py:434
  2.5 3.0 %collective-permute-start.3 = (bf16[128,640]{1,0:T(8,128)(2,1)S(1)}, bf16[128,640]{1,0:T(8,128)(2,1)S(1)}, u32[]{:S(2)}, u32[]{:S(2)}) collective-permute-start(bf16[128,640]{1,0:T(8,128)(2,1)S(1)} %get-tuple-element.54.refs_0_), channel_id=1, source_target_pairs={{0,8},{4,12},{8,0},{12,4},{16,24},{20,28},{24,16},{28,20},{1,9},{5... | collective-permute-start | bytes 491528 | tf_op jit(solution)/shard_map/ppermute | solution.py:413
  5.5 1.5 %collective-permute-start.4 = (bf16[64,640]{1,0:T(8,128)(2,1)S(1)}, bf16[64,640]{1,0:T(8,128)(2,1)S(1)}, u32[]{:S(2)}, u32[]{:S(2)}) collective-permute-start(bf16[64,640]{1,0:T(8,128)(2,1)S(1)} %get-tuple-element.55), channel_id=1, source_target_pairs={{0,16},{4,20},{8,24},{12,28},{16,0},{20,4},{24,8},{28,12},{1,17},{... | collective-permute-start | bytes 245768 | tf_op jit(solution)/shard_map/ppermute | solution.py:413
  7.1 0.0 collective-permute-start.5
  7.1 2.0 %collective-permute-start = (bf16[64,640]{1,0:T(8,128)(2,1)S(1)}, bf16[64,640]{1,0:T(8,128)(2,1)S(1)}, u32[]{:S(2)}, u32[]{:S(2)}) collective-permute-start(bf16[64,640]{1,0:T(8,128)(2,1)S(1)} %get-tuple-element.46), channel_id=1, source_target_pairs={{0,1},{1,0},{2,3},{3,2},{4,5},{5,4},{6,7},{7,6},{8,9},{9,8},{10,11... | collective-permute-start | bytes 245768 | tf_op jit(solution)/shard_map/ppermute | solution.py:413
  9.1 2.6 %collective-permute-start.1 = (bf16[64,640]{1,0:T(8,128)(2,1)S(1)}, bf16[64,640]{1,0:T(8,128)(2,1)S(1)}, u32[]{:S(2)}, u32[]{:S(2)}) collective-permute-start(bf16[64,640]{1,0:T(8,128)(2,1)S(1)} %get-tuple-element.47), channel_id=1, source_target_pairs={{0,2},{1,3},{2,0},{3,1},{4,6},{5,7},{6,4},{7,5},{8,10},{9,11},{10,... | collective-permute-start | bytes 245768 | tf_op jit(solution)/shard_map/ppermute | solution.py:413
  11.7 0.9 %shard_map.69 = bf16[64,640]{1,0:T(8,128)(2,1)S(1)} custom-call(bf16[64,2560]{1,0:T(8,128)(2,1)} %g_ref.3), custom_call_target="tpu_custom_call" | custom-call | bytes 1048576 | tf_op jit(solution)/shard_map/pallas_call | solution.py:433
  12.6 0.0 collective-permute-done.4.refs_2_
  12.6 1.1 %collective-permute-start.2 = (bf16[64,640]{1,0:T(8,128)(2,1)S(1)}, bf16[64,640]{1,0:T(8,128)(2,1)S(1)}, u32[]{:S(2)}, u32[]{:S(2)}) collective-permute-start(bf16[64,640]{1,0:T(8,128)(2,1)S(1)} %shard_map.69), channel_id=1, source_target_pairs={{0,3},{1,2},{2,1},{3,0},{4,7},{5,6},{6,5},{7,4},{8,11},{9,10},{10,... | collective-permute-start | bytes 245768 | tf_op jit(solution)/shard_map/ppermute | solution.py:413
  13.7 0.9 %shard_map.68 = (f32[2048,256]{1,0:T(8,128)S(1)}, f32[256,128]{1,0:T(8,128)S(1)}, f32[64,128]{1,0:T(8,128)S(1)}) custom-call(bf16[256,640]{1,0:T(8,128)(2,1)S(1)} %get-tuple-element.41.qp, bf16[256,640]{1,0:T(8,128)(2,1)S(1)} %get-tuple-element.42.kp), custom_call_target="tpu_custom_call" | custom-call | bytes 1048576 | tf_op jit(solution)/shard_map/pallas_call | solution.py:450
  14.7 0.0 collective-permute-done.5.refs_3_
  14.7 0.0 collective-permute-done.3.refs_1_
  14.7 0.1 collective-permute-start.6
  14.8 0.0 collective-permute-done.refs_1_
  14.8 2.3 %collective-permute-done.1.refs_2_ = bf16[64,640]{1,0:T(8,128)(2,1)S(1)} collective-permute-done((bf16[64,640]{1,0:T(8,128)(2,1)S(1)}, bf16[64,640]{1,0:T(8,128)(2,1)S(1)}, u32[]{:S(2)}, u32[]{:S(2)}) %collective-permute-start.1) | collective-permute-done | bytes 81952 | tf_op jit(solution)/shard_map/ppermute | solution.py:413
  17.1 1.9 %collective-permute-done.2.refs_3_ = bf16[64,640]{1,0:T(8,128)(2,1)S(1)} collective-permute-done((bf16[64,640]{1,0:T(8,128)(2,1)S(1)}, bf16[64,640]{1,0:T(8,128)(2,1)S(1)}, u32[]{:S(2)}, u32[]{:S(2)}) %collective-permute-start.2) | collective-permute-done | bytes 81952 | tf_op jit(solution)/shard_map/ppermute | solution.py:413
  18.9 0.7 %shard_map.70 = (bf16[256,640]{1,0:T(8,128)(2,1)S(1)}, bf16[64,640]{1,0:T(8,128)(2,1)S(1)}, f32[2048,256]{1,0:T(8,128)S(1)}, f32[256,128]{1,0:T(8,128)S(1)}, f32[64,128]{1,0:T(8,128)S(1)}) custom-call(bf16[256,640]{1,0:T(8,128)(2,1)S(1)} %get-tuple-element.43.vp, f32[2048,256]{1,0:T(8,128)S(1)} %get-tuple-element.44.weight, ...), custom_call_target="tpu_custom_call" | custom-call | flops 20000000000 | bytes 1048576 | tf_op jit(solution)/shard_map/pallas_call | solution.py:458
  19.7 0.0 collective-permute-done.6.came
  19.7 1.3 %shard_map.72 = (bf16[256,640]{1,0:T(8,128)(2,1)S(1)}, bf16[256,640]{1,0:T(8,128)(2,1)S(1)}, bf16[256,640]{1,0:T(8,128)(2,1)S(1)}, bf16[256,640]{1,0:T(8,128)(2,...) custom-call(bf16[64,640]{1,0:T(8,128)(2,1)S(1)} %get-tuple-element.52.q, ...), custom_call_target="tpu_custom_call" | custom-call | bytes 1048576 | tf_op jit(solution)/shard_map/pallas_call | solution.py:453
  21.0 2.2 %shard_map.73 = (f32[64,640]{1,0:T(8,128)S(1)}, f32[64,128]{1,0:T(8,128)S(1)}, f32[384,640]{1,0:T(8,128)S(1)}, bf16[384,640]{1,0:T(8,128)(2,1)S(1)}) custom-call(bf16[64,640]{1,0:T(8,128)(2,1)S(1)} %get-tuple-element.52.q1, bf16[64,640]{1,0:T(8,128)(2,1)S(1)} %get-tuple-element.57.g1, bf16[256,640]{1,0:T(8,128)(2,1)S(1)} %get-tuple-element.58.k1, ...), custom_call_target="tpu_custom_call" | custom-call | bytes 1048576 | tf_op jit(solution)/shard_map/pallas_call | solution.py:464
  23.2 0.1 collective-permute-start.7
  23.3 1.9 %collective-permute-done.7.came = bf16[384,640]{1,0:T(8,128)(2,1)S(1)} collective-permute-done((bf16[384,640]{1,0:T(8,128)(2,1)S(1)}, bf16[384,640]{1,0:T(8,128)(2,1)S(1)}, u32[]{:S(2)}, u32[]{:S(2)}) %collective-permute-start.7) | collective-permute-done | bytes 491552 | tf_op jit(solution)/shard_map/ppermute | solution.py:413
  25.1 0.1 shard_map.75
  25.2 1.5 %collective-permute-start.8 = (bf16[128,640]{1,0:T(8,128)(2,1)S(1)}, bf16[128,640]{1,0:T(8,128)(2,1)S(1)}, u32[]{:S(2)}, u32[]{:S(2)}) collective-permute-start(bf16[128,640]{1,0:T(8,128)(2,1)S(1)} %get-tuple-element.74), channel_id=1, source_target_pairs={{0,8},{4,12},{8,0},{12,4},{16,24},{20,28},{24,16},{28,20},{1,9},{5... | collective-permute-start | bytes 491528 | tf_op jit(solution)/shard_map/ppermute | solution.py:413
  26.7 1.5 %collective-permute-start.9 = (bf16[64,640]{1,0:T(8,128)(2,1)S(1)}, bf16[64,640]{1,0:T(8,128)(2,1)S(1)}, u32[]{:S(2)}, u32[]{:S(2)}) collective-permute-start(bf16[64,640]{1,0:T(8,128)(2,1)S(1)} %get-tuple-element.75), channel_id=1, source_target_pairs={{0,16},{4,20},{8,24},{12,28},{16,0},{20,4},{24,8},{28,12},{1,17},{... | collective-permute-start | bytes 245768 | tf_op jit(solution)/shard_map/ppermute | solution.py:413
  28.3 0.5 %collective-permute-start.10 = (bf16[64,640]{1,0:T(8,128)(2,1)S(1)}, bf16[64,640]{1,0:T(8,128)(2,1)S(1)}, u32[]{:S(2)}, u32[]{:S(2)}) collective-permute-start(bf16[64,640]{1,0:T(8,128)(2,1)S(1)} %get-tuple-element.76), channel_id=1, source_target_pairs={{0,24},{4,28},{8,16},{12,20},{16,8},{20,12},{24,0},{28,4},{1,25},{... | collective-permute-start | bytes 245768 | tf_op jit(solution)/shard_map/ppermute | solution.py:413
  28.7 2.6 %shard_map.74 = (bf16[256,640]{1,0:T(8,128)(2,1)}, f32[256,640]{1,0:T(8,128)S(1)}, f32[256,640]{1,0:T(8,128)S(1)}) custom-call(bf16[256,640]{1,0:T(8,128)(2,1)S(1)} %get-tuple-element.41.qp, bf16[256,640]{1,0:T(8,128)(2,1)S(1)} %get-tuple-element.42.kp, bf16[256,640]{1,0:T(8,128)(2,1)S(1)} %get-tuple-element.48.gp, ...), custom_call_target="tpu_custom_call" | custom-call | bytes 1048576 | tf_op jit(solution)/shard_map/pallas_call | solution.py:474
  31.3 0.0 collective-permute-done.9.refs_1_
  31.3 2.9 %collective-permute-done.10.refs_2_ = bf16[64,640]{1,0:T(8,128)(2,1)S(1)} collective-permute-done((bf16[64,640]{1,0:T(8,128)(2,1)S(1)}, bf16[64,640]{1,0:T(8,128)(2,1)S(1)}, u32[]{:S(2)}, u32[]{:S(2)}) %collective-permute-start.10) | collective-permute-done | bytes 81952 | tf_op jit(solution)/shard_map/ppermute | solution.py:413
  34.2 0.0 collective-permute-done.8.refs_0_
  34.2 1.3 %shard_map.76 = (bf16[256,640]{1,0:T(8,128)(2,1)}, bf16[256,640]{1,0:T(8,128)(2,1)}) custom-call(f32[256,640]{1,0:T(8,128)S(1)} %get-tuple-element.69.dk0, f32[256,640]{1,0:T(8,128)S(1)} %get-tuple-element.70.dv0, f32[128,640]{1,0:T(8,128)S(1)} %get-tuple-element.73.own, bf16[128,640]{1,0:T(8,128)(2,1)S(1)} %collective-permute-done.8.refs_0_, ...), custom_call_target="tpu_custom_call" | custom-call | bytes 1048576 | tf_op jit(solution)/shard_map/pallas_call | solution.py:482
  (1 shorter events, 0.0 us)
Async XLA Ops:
  2.5 12.1 %collective-permute-start.3 = (bf16[128,640]{1,0:T(8,128)(2,1)S(1)}, bf16[128,640]{1,0:T(8,128)(2,1)S(1)}, u32[]{:S(2)}, u32[]{:S(2)}) collective-permute-start(bf16[128,640]{1,0:T(8,128)(2,1)S(1)} %get-tuple-element.54.refs_0_), channel_id=1, source_target_pairs={{0,8},{4,12},{8,0},{12,4},{16,24},{20,28},{24,16},{28,20},{1,9},{5... | collective-permute-start | bytes 491528 | tf_op jit(solution)/shard_map/ppermute | solution.py:413
  5.5 7.1 %collective-permute-start.4 = (bf16[64,640]{1,0:T(8,128)(2,1)S(1)}, bf16[64,640]{1,0:T(8,128)(2,1)S(1)}, u32[]{:S(2)}, u32[]{:S(2)}) collective-permute-start(bf16[64,640]{1,0:T(8,128)(2,1)S(1)} %get-tuple-element.55), channel_id=1, source_target_pairs={{0,16},{4,20},{8,24},{12,28},{16,0},{20,4},{24,8},{28,12},{1,17},{... | collective-permute-start | bytes 245768 | tf_op jit(solution)/shard_map/ppermute | solution.py:413
  7.1 7.6 %collective-permute-start.5 = (bf16[64,640]{1,0:T(8,128)(2,1)S(1)}, bf16[64,640]{1,0:T(8,128)(2,1)S(1)}, u32[]{:S(2)}, u32[]{:S(2)}) collective-permute-start(bf16[64,640]{1,0:T(8,128)(2,1)S(1)} %get-tuple-element.55), channel_id=1, source_target_pairs={{0,24},{4,28},{8,16},{12,20},{16,8},{20,12},{24,0},{28,4},{1,25},{... | collective-permute-start | bytes 245768 | tf_op jit(solution)/shard_map/ppermute | solution.py:413
  7.1 7.7 %collective-permute-start = (bf16[64,640]{1,0:T(8,128)(2,1)S(1)}, bf16[64,640]{1,0:T(8,128)(2,1)S(1)}, u32[]{:S(2)}, u32[]{:S(2)}) collective-permute-start(bf16[64,640]{1,0:T(8,128)(2,1)S(1)} %get-tuple-element.46), channel_id=1, source_target_pairs={{0,1},{1,0},{2,3},{3,2},{4,5},{5,4},{6,7},{7,6},{8,9},{9,8},{10,11... | collective-permute-start | bytes 245768 | tf_op jit(solution)/shard_map/ppermute | solution.py:413
  9.1 8.0 %collective-permute-start.1 = (bf16[64,640]{1,0:T(8,128)(2,1)S(1)}, bf16[64,640]{1,0:T(8,128)(2,1)S(1)}, u32[]{:S(2)}, u32[]{:S(2)}) collective-permute-start(bf16[64,640]{1,0:T(8,128)(2,1)S(1)} %get-tuple-element.47), channel_id=1, source_target_pairs={{0,2},{1,3},{2,0},{3,1},{4,6},{5,7},{6,4},{7,5},{8,10},{9,11},{10,... | collective-permute-start | bytes 245768 | tf_op jit(solution)/shard_map/ppermute | solution.py:413
  12.6 6.3 %collective-permute-start.2 = (bf16[64,640]{1,0:T(8,128)(2,1)S(1)}, bf16[64,640]{1,0:T(8,128)(2,1)S(1)}, u32[]{:S(2)}, u32[]{:S(2)}) collective-permute-start(bf16[64,640]{1,0:T(8,128)(2,1)S(1)} %shard_map.69), channel_id=1, source_target_pairs={{0,3},{1,2},{2,1},{3,0},{4,7},{5,6},{6,5},{7,4},{8,11},{9,10},{10,... | collective-permute-start | bytes 245768 | tf_op jit(solution)/shard_map/ppermute | solution.py:413
  14.7 4.9 %collective-permute-start.6 = (bf16[384,640]{1,0:T(8,128)(2,1)S(1)}, bf16[384,640]{1,0:T(8,128)(2,1)S(1)}, u32[]{:S(2)}, u32[]{:S(2)}) collective-permute-start(bf16[384,640]{1,0:T(8,128)(2,1)S(1)} %shard_map.71), channel_id=1, source_target_pairs={{0,4},{4,0},{8,12},{12,8},{16,20},{20,16},{24,28},{28,24},{1,5},{5... | collective-permute-start | bytes 1474568 | tf_op jit(solution)/shard_map/ppermute | solution.py:413
  23.2 1.9 %collective-permute-start.7 = (bf16[384,640]{1,0:T(8,128)(2,1)S(1)}, bf16[384,640]{1,0:T(8,128)(2,1)S(1)}, u32[]{:S(2)}, u32[]{:S(2)}) collective-permute-start(bf16[384,640]{1,0:T(8,128)(2,1)S(1)} %get-tuple-element.72), channel_id=1, source_target_pairs={{0,4},{4,0},{8,12},{12,8},{16,20},{20,16},{24,28},{28,24},{1,5},{5... | collective-permute-start | bytes 1474568 | tf_op jit(solution)/shard_map/ppermute | solution.py:413
  25.2 9.0 %collective-permute-start.8 = (bf16[128,640]{1,0:T(8,128)(2,1)S(1)}, bf16[128,640]{1,0:T(8,128)(2,1)S(1)}, u32[]{:S(2)}, u32[]{:S(2)}) collective-permute-start(bf16[128,640]{1,0:T(8,128)(2,1)S(1)} %get-tuple-element.74), channel_id=1, source_target_pairs={{0,8},{4,12},{8,0},{12,4},{16,24},{20,28},{24,16},{28,20},{1,9},{5... | collective-permute-start | bytes 491528 | tf_op jit(solution)/shard_map/ppermute | solution.py:413
  26.7 4.6 %collective-permute-start.9 = (bf16[64,640]{1,0:T(8,128)(2,1)S(1)}, bf16[64,640]{1,0:T(8,128)(2,1)S(1)}, u32[]{:S(2)}, u32[]{:S(2)}) collective-permute-start(bf16[64,640]{1,0:T(8,128)(2,1)S(1)} %get-tuple-element.75), channel_id=1, source_target_pairs={{0,16},{4,20},{8,24},{12,28},{16,0},{20,4},{24,8},{28,12},{1,17},{... | collective-permute-start | bytes 245768 | tf_op jit(solution)/shard_map/ppermute | solution.py:413
  28.3 5.9 %collective-permute-start.10 = (bf16[64,640]{1,0:T(8,128)(2,1)S(1)}, bf16[64,640]{1,0:T(8,128)(2,1)S(1)}, u32[]{:S(2)}, u32[]{:S(2)}) collective-permute-start(bf16[64,640]{1,0:T(8,128)(2,1)S(1)} %get-tuple-element.76), channel_id=1, source_target_pairs={{0,24},{4,28},{8,16},{12,20},{16,8},{20,12},{24,0},{28,4},{1,25},{... | collective-permute-start | bytes 245768 | tf_op jit(solution)/shard_map/ppermute | solution.py:413

commit v3 on v2

--- a/solution.py
+++ b/solution.py
@@ -18,6 +18,8 @@
 SCALE = HD**-0.5
 SCALE2 = SCALE * math.log2(math.e)
 VMEM_BYTES = 28 * 2**20
+LOWEST = -1e30
+TINY = 1e-30
 
 
 class Plan:
@@ -102,6 +104,19 @@
     return (lane >= h * HD) & (lane < (h + 1) * HD)
 
 
+def head_groups(p):
+    groups, h = [], 0
+    while h < p.heads:
+        low, high = window(h)
+        end = h + 1
+        while end < p.heads and window(end)[1] - low <= 2 * LANES:
+            high = window(end)[1]
+            end += 1
+        groups.append((h, end, low, high))
+        h = end
+    return groups
+
+
 def head_mask(p, h):
     lane = iota((1, p.width), 1)
     return (lane >= h * HD) & (lane < (h + 1) * HD)
@@ -131,16 +146,10 @@
     return g_ref.at[:, pl.ds(start, p.width)]
 
 
-def far_kernel(p, g_ref, out, sem):
-    copy = pltpu.make_async_copy(slab(p, g_ref, p.zcount - 1), out, sem)
-    copy.start()
-    copy.wait()
-
-
 def pack_kernel(p, q_ref, k_ref, v_ref, g_ref, qp, kp, vp, q1, kv1, kv2, *refs):
-    gz, (q_in, k_in, v_in, sems) = refs[: p.zcount - 1], refs[p.zcount - 1 :]
+    gz, (q_in, k_in, v_in, sems) = refs[: p.zcount], refs[p.zcount :]
     loads = [(k_ref, k_in), (v_ref, v_in), (q_ref, q_in)]
-    loads += [(slab(p, g_ref, b), gz[b]) for b in range(p.zcount - 1)]
+    loads += [(slab(p, g_ref, b), gz[b]) for b in range(p.zcount)]
     copies = [pltpu.make_async_copy(src, dst, sems.at[i]) for i, (src, dst) in enumerate(loads)]
     for copy in copies:
         copy.start()
@@ -181,8 +190,8 @@
     lse01[...] = pick(p, lse_all, lane_class(p))
 
 
-def own_delta_kernel(p, vp, weight, *refs):
-    gz, (gp, g1, dprob, d0, d01, natural) = refs[: p.zcount], refs[p.zcount :]
+def gather_kernel(p, *refs):
+    gz, (gp, g1, natural) = refs[: p.zcount], refs[p.zcount :]
     z = lax.axis_index("head")
     share = p.tokens // p.zcount
     for b in range(p.zcount):
@@ -191,6 +200,9 @@
     g = nn(phase_order(p), natural[...])
     gp[...] = g.astype(BF16)
     g1[...] = pick(p, g, column_class(p)).astype(BF16)
+
+
+def own_delta_kernel(p, vp, weight, gp, dprob, d0, d01):
     lane = iota((1, LANES), 1)
     d_all = jnp.zeros((p.tokens, LANES), F32)
     for h in range(p.heads):
@@ -205,46 +217,30 @@
     d01[...] = pick(p, d_all, lane_class(p))
 
 
-def merge_kernel(p, *refs):
-    out = refs[-1]
-    at = 0
-    for ref in refs[:-1]:
-        out[at : at + ref.shape[0], :] = ref[...]
-        at += ref.shape[0]
-
-
 def columns(p, stat):
     return jnp.concatenate([stat[:, h : h + 1] for h in range(p.heads)], axis=0)
 
 
 def to_lanes(p, column):
     lane = iota((1, LANES), 1)
-    out = jnp.zeros((p.n1, LANES), F32)
+    count = 2 * p.n1
+    out = jnp.zeros((count, LANES), F32)
     for h in range(p.heads):
-        out = jnp.where(lane == h, column[h * p.n1 : (h + 1) * p.n1], out)
+        out = jnp.where(lane == h, column[h * count : (h + 1) * count], out)
     return out
 
 
 def wide_rows(p, column):
-    return jnp.concatenate([column[h * p.n1 : h * p.n1 + p.n2] for h in range(p.heads)], axis=0)
+    starts = range(0, 2 * p.heads * p.n1, p.n1)
+    return jnp.concatenate([column[s : s + p.n2] for s in starts], axis=0)
 
 
 def widen(p, column, fill):
     rest = jnp.full((p.n1 - p.n2, column.shape[1]), fill, F32)
     parts = []
-    for h in range(p.heads):
-        parts += [column[h * p.n2 : (h + 1) * p.n2], rest]
+    for s in range(0, 2 * p.heads * p.n2, p.n2):
+        parts += [column[s : s + p.n2], rest]
     return jnp.concatenate(parts, axis=0)
-
-
-def by_head(p, rows):
-    if rows.shape[0] % 16:
-        rows = rows.astype(F32)
-    parts = []
-    for h in range(p.heads):
-        mask = jnp.where(head_mask(p, h), 1.0, 0.0).astype(rows.dtype)
-        parts.append(rows * mask)
-    return jnp.concatenate(parts, axis=0).astype(BF16)
 
 
 def cut(p, block, start, count):
@@ -253,115 +249,164 @@
     return block[start : start + count]
 
 
-def merge_heads(p, rows, count):
-    out = jnp.zeros((count, p.width), F32)
-    for h in range(p.heads):
-        out = jnp.where(head_mask(p, h), rows[h * count : (h + 1) * count], out)
-    return out
-
-
-def scores_kernel(p, q1, lse01, came, *refs):
-    even = refs[: p.g2 // 2]
-    k1, v1, k2, v2, p1, p2, total1, share1 = refs[p.g2 // 2 :]
+def both_cores(p, own, other, count):
+    return jnp.concatenate([cut(p, own, 0, count), cut(p, other, 0, count)], axis=0)
+
+
+def by_head(p, rows, group):
+    first, end, low, high = group
+    parts = []
+    for h in range(first, end):
+        mask = jnp.where(window_mask(h, low, high), 1.0, 0.0).astype(rows.dtype)
+        parts.append(rows[:, low:high] * mask)
+    return jnp.concatenate(parts, axis=0).astype(BF16)
+
+
+def against(p, rows, cols):
+    parts = []
+    for group in head_groups(p):
+        low, high = group[2:]
+        parts.append(nt(by_head(p, rows, group), cols[:, low:high]))
+    return jnp.concatenate(parts, axis=0)
+
+
+def collect(p, weights, rows, out):
+    count = rows.shape[0]
+    for group in head_groups(p):
+        first, end, low, high = group
+        part = tn(weights[first * count : end * count], by_head(p, rows, group))
+        out[:, low:high] += part
+
+
+def back(p, weights, cols, count, out):
+    for first, end, low, high in head_groups(p):
+        part = nn(weights[first * count : end * count], cols[:, low:high])
+        for h in range(first, end):
+            low_h, high_h = window(h)
+            at = (h - first) * count
+            piece = part[at : at + count, low_h - low : high_h - low]
+            hit = window_mask(h, low_h, high_h)
+            out[:count, low_h:high_h] = jnp.where(hit, piece, out[:count, low_h:high_h])
+
+
+def key_blocks(p, half, kv):
+    blocks = [ref[...] for ref in kv]
+    near = [cut(p, blocks[i], half * p.n1, p.n1) for i in range(p.g1 // 2)]
+    wide = [cut(p, blocks[i], half * p.rows[2 * i] // 2, p.n2) for i in range(p.g2 // 2)]
+    return jnp.concatenate(near, axis=0).astype(BF16), jnp.concatenate(wide, axis=0).astype(BF16)
+
+
+def soft(scores):
+    top = jnp.maximum(jnp.max(scores, axis=1, keepdims=True), LOWEST)
+    e = jnp.exp2(scores - top)
+    return top, e, jnp.sum(e, axis=1, keepdims=True)
+
+
+def scores_kernel(p, q_own, q_other, *refs):
+    kv, (p1, p2, lse) = refs[: p.g2 // 2], refs[p.g2 // 2 :]
     d = lax.axis_index("seq")
     n1, n2 = p.n1, p.n2
-    blocks, at = [], 0
-    for b in range(p.g2):
-        if b % 2 == 0:
-            blocks.append(even[b // 2][...])
+    k1, k2 = key_blocks(p, 0, kv)
+    q1 = both_cores(p, q_own[...], q_other[...], n1)
+    q2 = both_cores(p, q_own[...], q_other[...], n2)
+
+    row = iota((2 * p.heads * n1, 1), 0)
+    col = iota((1, p.g1 // 2 * n1), 1)
+    head = first_head(p) + row // (2 * n1)
+    own = row % n1
+    device = jnp.bitwise_xor(d, row // n1 % 2)
+    qpos = p.tokens * device + p.r2 * (own % n2) + (head + DIL1 * (own // n2)) % p.r2
+    other = col % n1
+    kbase = p.tokens * jnp.bitwise_xor(d, 2 * (col // n1)) + p.r2 * (other % n2)
+    kpos = kbase + jnp.bitwise_and(head + DIL1 * (other // n2), p.r2 - 1)
+    s1 = jnp.where(kpos <= qpos, against(p, q1, k1) * SCALE2, -jnp.inf)
+    top1, e1, sum1 = soft(s1)
+
+    row2 = iota((2 * p.heads * n2, 1), 0)
+    row2 = jnp.bitwise_xor(d, row2 // n2 % 2) * n2 + row2 % n2
+    col2 = iota((1, p.g2 // 2 * n2), 1)
+    col2 = jnp.bitwise_xor(d, 2 * (col2 // n2)) * n2 + col2 % n2
+    s2 = jnp.where(col2 <= row2, against(p, q2, k2) * SCALE2, -jnp.inf)
+    top2, e2, sum2 = soft(s2)
+
+    top2_all, sum2_all = widen(p, top2, LOWEST), widen(p, sum2, 0.0)
+    peak = jnp.maximum(top1, top2_all)
+    both = sum1 * jnp.exp2(top1 - peak) + sum2_all * jnp.exp2(top2_all - peak)
+    part = peak + jnp.log2(jnp.maximum(both, TINY))
+    p1[...] = e1 * jnp.exp2(top1 - part)
+    p2[...] = e2 * jnp.exp2(top2 - wide_rows(p, part))
+    lse[...] = to_lanes(p, part)
+
+
+def delta_kernel(p, g_own, g_other, p1, p2, lse, lse01, d01, *refs):
+    kv, (dp1, dp2, stats) = refs[: p.g2 // 2], refs[p.g2 // 2 :]
+    n1 = p.n1
+    v1, v2 = key_blocks(p, 1, kv)
+    dp = against(p, both_cores(p, g_own[...], g_other[...], n1), v1)
+    dp1[...] = dp
+    d = jnp.sum(p1[...] * dp, axis=1, keepdims=True)
+    dp = against(p, both_cores(p, g_own[...], g_other[...], p.n2), v2)
+    dp2[...] = dp
+    d += widen(p, jnp.sum(p2[...] * dp, axis=1, keepdims=True), 0.0)
+    d = to_lanes(p, d)
+    part = lse[:n1, :]
+    total, delta = join(lse01[...], d01[...], part, d[:n1])
+    stats[...] = jnp.concatenate([total, delta, lse[n1:, :], d[n1:]], axis=0)
+
+
+def join(lse_a, d_a, lse_b, d_b):
+    peak = jnp.maximum(lse_a, lse_b)
+    total = peak + jnp.log2(jnp.exp2(lse_a - peak) + jnp.exp2(lse_b - peak))
+    return total, jnp.exp2(lse_a - total) * d_a + jnp.exp2(lse_b - total) * d_b
+
+
+def levels_kernel(p, q_own, q_other, g_own, g_other, p1, p2, dp1, dp2, lse, mine, theirs, *refs):
+    kv, refs = refs[: p.g2 // 2], refs[p.g2 // 2 :]
+    dq_own, dq_other, total1, delta1, own_part = refs[:5]
+    outs, (dk1, dv1, dk2, dv2, dq1, dq2) = refs[5:-6], refs[-6:]
+    n1, n2 = p.n1, p.n2
+    quarter = lambda ref, i: ref[i * n1 : (i + 1) * n1, :]
+    first = join(quarter(mine, 0), quarter(mine, 1), quarter(theirs, 2), quarter(theirs, 3))
+    second = join(quarter(theirs, 0), quarter(theirs, 1), quarter(mine, 2), quarter(mine, 3))
+    total1[...], delta1[...] = first
+    total = jnp.concatenate([first[0], second[0]], axis=0)
+    share = columns(p, jnp.exp2(lse[...] - total))
+    delta = columns(p, jnp.concatenate([first[1], second[1]], axis=0))
+    k1, k2 = key_blocks(p, 0, kv)
+    for ref in (dk1, dv1, dk2, dv2):
+        ref[...] = jnp.zeros_like(ref)
+
+    prob = p1[...] * share
+    ds = (prob * (dp1[...] - delta) * SCALE).astype(BF16)
+    collect(p, prob.astype(BF16), both_cores(p, g_own[...], g_other[...], n1), dv1)
+    collect(p, ds, both_cores(p, q_own[...], q_other[...], n1), dk1)
+    prob2 = p2[...] * wide_rows(p, share)
+    ds2 = (prob2 * (dp2[...] - wide_rows(p, delta)) * SCALE).astype(BF16)
+    collect(p, prob2.astype(BF16), both_cores(p, g_own[...], g_other[...], n2), dv2)
+    collect(p, ds2, both_cores(p, q_own[...], q_other[...], n2), dk2)
+    for i in range(p.g2 // 2):
+        rows = slice(i * n2, (i + 1) * n2)
+        if 2 * i < p.g1:
+            head = slice(i * n1, i * n1 + n2)
+            rest = slice(i * n1 + n2, (i + 1) * n1)
+            part = []
+            for near, wide in ((dk1, dk2), (dv1, dv2)):
+                part += [near[head, :] + wide[rows, :], near[rest, :]]
         else:
-            blocks.append(came[at : at + p.rows[b], :])
-            at += p.rows[b]
-    for half, (out1, out2) in enumerate(((k1, k2), (v1, v2))):
-        parts = [cut(p, blocks[b], half * n1, n1) for b in range(p.g1)]
-        out1[...] = jnp.concatenate(parts, axis=0).astype(BF16)
-        parts = [cut(p, blocks[b], half * p.rows[b] // 2, n2) for b in range(p.g2)]
-        out2[...] = jnp.concatenate(parts, axis=0).astype(BF16)
-    q_rows = q1[...]
-    q1b, q2b = by_head(p, q_rows), by_head(p, cut(p, q_rows, 0, n2))
-
-    shape1 = (p.heads * n1, p.g1 * n1)
-    row = iota((shape1[0], 1), 0)
-    col = iota((1, shape1[1]), 1)
-    head = first_head(p) + row // n1
-    own = row % n1
-    qpos = p.tokens * d + p.r2 * (own % n2) + (head + DIL1 * (own // n2)) % p.r2
-    other = col % n1
-    kbase = p.tokens * jnp.bitwise_xor(d, col // n1) + p.r2 * (other % n2)
-    kpos = kbase + jnp.bitwise_and(head + DIL1 * (other // n2), p.r2 - 1)
-    s1 = jnp.where(kpos <= qpos, nt(q1b, k1[...]) * SCALE2, -jnp.inf)
-    top1 = jnp.max(s1, axis=1, keepdims=True)
-    e1 = jnp.exp2(s1 - top1)
-    lse1 = top1 + jnp.log2(jnp.sum(e1, axis=1, keepdims=True))
-
-    row2 = d * n2 + iota((p.heads * n2, 1), 0) % n2
-    col2 = iota((1, p.g2 * n2), 1)
-    col2 = jnp.bitwise_xor(d, col2 // n2) * n2 + col2 % n2
-    s2 = jnp.where(col2 <= row2, nt(q2b, k2[...]) * SCALE2, -jnp.inf)
-    top2 = jnp.max(s2, axis=1, keepdims=True)
-    e2 = jnp.exp2(s2 - top2)
-    lse2 = top2 + jnp.log2(jnp.sum(e2, axis=1, keepdims=True))
-
-    lse0 = columns(p, lse01[...])
-    lse2 = widen(p, lse2, -jnp.inf)
-    peak = jnp.maximum(jnp.maximum(lse0, lse1), lse2)
-    total = peak + jnp.log2(jnp.exp2(lse0 - peak) + jnp.exp2(lse1 - peak) + jnp.exp2(lse2 - peak))
-    p1[...] = e1 * jnp.exp2(top1 - total)
-    p2[...] = e2 * jnp.exp2(top2 - wide_rows(p, total))
-    total1[...] = to_lanes(p, total)
-    share1[...] = to_lanes(p, jnp.exp2(lse0 - total))
-
-
-def levels_kernel(p, q1, g1, k1, v1, k2, v2, p1, p2, share1, d01, dq1, delta1, keep, send):
-    n1, n2 = p.n1, p.n2
-    q_rows, g_rows = q1[...], g1[...]
-    q1b, g1b = by_head(p, q_rows), by_head(p, g_rows)
-    q2b, g2b = by_head(p, cut(p, q_rows, 0, n2)), by_head(p, cut(p, g_rows, 0, n2))
-    prob1, prob2 = p1[...], p2[...]
-    dp1 = nt(g1b, v1[...])
-    dp2 = nt(g2b, v2[...])
-    delta = columns(p, share1[...] * d01[...])
-    delta += jnp.sum(prob1 * dp1, axis=1, keepdims=True)
-    delta += widen(p, jnp.sum(prob2 * dp2, axis=1, keepdims=True), 0.0)
-    ds1 = (prob1 * (dp1 - delta) * SCALE).astype(BF16)
-    ds2 = (prob2 * (dp2 - wide_rows(p, delta)) * SCALE).astype(BF16)
-
-    dk1, dk2 = tn(ds1, q1b), tn(ds2, q2b)
-    dv1, dv2 = tn(prob1.astype(BF16), g1b), tn(prob2.astype(BF16), g2b)
-    at = [0, 0]
-    for b in range(p.g2):
-        rows = slice(b * n2, (b + 1) * n2)
-        if b < p.g1:
-            first = slice(b * n1, b * n1 + n2)
-            rest = slice(b * n1 + n2, (b + 1) * n1)
-            part = [dk1[first] + dk2[rows], dk1[rest], dv1[first] + dv2[rows], dv1[rest]]
-        else:
-            part = [dk2[rows], dv2[rows]]
+            part = [dk2[rows, :], dv2[rows, :]]
         part = jnp.concatenate(part, axis=0)
-        odd = b % 2
-        ref = send if odd else keep
-        ref[at[odd] : at[odd] + p.rows[b], :] = part.astype(ref.dtype)
-        at[odd] += p.rows[b]
-    dq = merge_heads(p, nn(ds1, k1[...]), n1)
-    wide = merge_heads(p, nn(ds2, k2[...]), n2)
-    dq1[...] = jnp.concatenate([dq[:n2] + wide, dq[n2:]], axis=0)
-    delta1[...] = to_lanes(p, delta)
-
-
-def chip_kernel(p, keep, came, own, *outs):
-    at = 0
-    for index, b in enumerate(range(0, p.g2, 2)):
-        rows = slice(at, at + p.rows[b])
-        block = keep[rows, :] + came[rows, :].astype(F32)
-        if b == 0:
-            own[...] = block
-        else:
-            outs[index - 1][...] = block.astype(BF16)
-        at += p.rows[b]
+        ref = outs[i - 1] if i else own_part
+        ref[...] = part.astype(ref.dtype)
+    back(p, ds, k1, 2 * n1, dq1)
+    back(p, ds2, k2, 2 * n2, dq2)
+    for core, ref in enumerate((dq_own, dq_other)):
+        near = dq1[core * n1 : (core + 1) * n1, :]
+        near = jnp.concatenate([near[:n2] + dq2[core * n2 : (core + 1) * n2, :], near[n2:]], axis=0)
+        ref[...] = near.astype(ref.dtype)
 
 
 def own_grad_kernel(
-    p, qp, kp, gp, weight, dprob, lse0, d0, total1, delta1, dq1, grad_q, dk0, dv0, dq
+    p, qp, kp, gp, weight, dprob, lse0, d0, total1, delta1, dq1, dq2, grad_q, dk0, dv0, dq
 ):
     label = lane_class(p)
     lse = lse0[...]
@@ -380,7 +425,8 @@
         dk0[:, low:high] += tn(ds, qp[:, low:high] * mask)
         dv0[:, low:high] += tn(prob.astype(BF16), gp[:, low:high] * mask)
     zero = jnp.zeros((p.tokens, p.width), F32)
-    all_q = dq[...] + spread(p, dq1[...], column_class(p), zero)
+    kept = dq1[...] + dq2[...].astype(F32)
+    all_q = dq[...] + spread(p, kept, column_class(p), zero)
     grad_q[...] = nn(phase_order(p, True), all_q.astype(BF16)).astype(BF16)
 
 
@@ -430,56 +476,54 @@
     half_rows = sum(p.rows[::2])
     hbm = pl.BlockSpec(memory_space=pltpu.HBM)
 
-    (far,) = call(run(far_kernel), [(share, BF16)], [pltpu.SemaphoreType.DMA], specs=[hbm])(grad_out)
     outs = call(
         run(pack_kernel),
         [(row, BF16)] * 3
         + [(kept, BF16), ((2 * n1, width), BF16), ((2 * n2, width), BF16)]
-        + [(share, BF16)] * (p.zcount - 1),
-        [(row, BF16)] * 3 + [pltpu.SemaphoreType.DMA((p.zcount + 2,))],
+        + [(share, BF16)] * p.zcount,
+        [(row, BF16)] * 3 + [pltpu.SemaphoreType.DMA((p.zcount + 3,))],
         specs=[hbm] * 4,
     )(queries, keys, values, grad_out)
     qp, kp, vp, q1, kv1, kv2 = outs[:6]
-    gz = [*outs[6:], far]
+    gz = outs[6:]
     gz = [gz[0]] + [swap(gz[b], "head", b) for b in range(1, p.zcount)]
 
     kv = [kv1] + [swap(kv1 if b < p.g1 else kv2, "seq", b) for b in even[1:]]
-    (sent,) = call(run(merge_kernel), [((half_rows, width), BF16)])(*kv)
-    came = swap(sent, "seq", 1)
 
     weight, lse0, lse01 = call(
         run(own_scores_kernel), [(flat(p.heads * tokens), F32), (stat, F32), (stat1, F32)]
     )(qp, kp)
-    k1, v1, k2, v2, p1, p2, total1, share1 = call(
-        run(scores_kernel),
-        [(row, BF16)] * 4
-        + [(flat(p.heads * n1), F32), (flat(p.heads * n2), F32), (stat1, F32), (stat1, F32)],
-    )(q1, lse01, came, *kv)
-    gp, g1, dprob, d0, d01 = call(
-        run(own_delta_kernel),
-        [(row, BF16), (kept, BF16), (flat(p.heads * tokens), F32), (stat, F32), (stat1, F32)],
-        [(row, BF16)],
-        flops=2 * 10**10,
-    )(vp, weight, *gz)
-    dq1, delta1, keep, send = call(
+    q_other = swap(q1, "seq", 1)
+    near = (2 * p.heads * n1, p.g1 // 2 * n1)
+    wide = (2 * p.heads * n2, p.g2 // 2 * n2)
+    p1, p2, lse = call(run(scores_kernel), [(near, F32), (wide, F32), ((2 * n1, LANES), F32)])(
+        q1, q_other, *kv
+    )
+    gp, g1 = call(run(gather_kernel), [(row, BF16), (kept, BF16)], [(row, BF16)])(*gz)
+    g_other = swap(g1, "seq", 1)
+    dprob, d0, d01 = call(
+        run(own_delta_kernel), [(flat(p.heads * tokens), F32), (stat, F32), (stat1, F32)]
+    )(vp, weight, gp)
+    dp1, dp2, mine = call(
+        run(delta_kernel), [(near, F32), (wide, F32), ((4 * n1, LANES), F32)]
+    )(g1, g_other, p1, p2, lse, lse01, d01, *kv)
+    theirs = swap(mine, "seq", 1)
+    part = lambda b, dtype: ((p.rows[b], width), dtype)
+    outs = call(
         run(levels_kernel),
-        [
-            (kept, F32),
-            (stat1, F32),
-            ((half_rows, width), F32),
-            ((half_rows, width), BF16),
-        ],
-    )(q1, g1, k1, v1, k2, v2, p1, p2, share1, d01)
-    returned = swap(send, "seq", 1)
+        [(kept, F32), (kept, BF16), (stat1, F32), (stat1, F32), part(0, F32)]
+        + [part(b, BF16) for b in even[1:]],
+        [((near[1], width), F32)] * 2
+        + [((wide[1], width), F32)] * 2
+        + [((2 * n1, width), F32), ((2 * n2, width), F32)],
+    )(q1, q_other, g1, g_other, p1, p2, dp1, dp2, lse, mine, theirs, *kv)
+    dq_own, dq_other, total1, delta1, own_part = outs[:5]
+    parts = [swap(s, "seq", b) for s, b in zip(outs[5:], even[1:])]
+    dq_came = swap(dq_other, "seq", 1)
     grad_q, dk0, dv0 = call(
         run(own_grad_kernel), [(row, BF16), (row, F32), (row, F32)], [(row, F32)]
-    )(qp, kp, gp, weight, dprob, lse0, d0, total1, delta1, dq1)
-    sums = call(
-        run(chip_kernel),
-        [((p.rows[0], width), F32)] + [((p.rows[b], width), BF16) for b in even[1:]],
-    )(keep, returned)
-    parts = [swap(s, "seq", b) for s, b in zip(sums[1:], even[1:])]
-    grad_k, grad_v = call(run(last_kernel), [(row, BF16)] * 2)(dk0, dv0, sums[0], *parts)
+    )(qp, kp, gp, weight, dprob, lse0, d0, total1, delta1, dq_own, dq_came)
+    grad_k, grad_v = call(run(last_kernel), [(row, BF16)] * 2)(dk0, dv0, own_part, *parts)
     return grad_q, grad_k, grad_v
 
 

time: 35.6 us -> 33.4 us (0.938)
  waiting for transfers between devices: 8.84 us -> 7.33 us
  starting transfers between devices: 13.9 us -> 13.4 us
    ppermute x11 -> x13, waiting for transfers between devices: 8.84 us -> 7.33 us  [swap(): return lax.ppermute(block, axis, [(i, i ^ bits) for i in range(count)])]
    ppermute x11 -> x13, starting transfers between devices: 13.9 us -> 13.4 us  [swap(): return lax.ppermute(block, axis, [(i, i ^ bits) for i in range(count)])]
    pallas_call x7 -> x6, Pallas kernels: 6.5 us -> 6.32 us  [the longest x1 1.67 us: body(): call(run(scores_kernel), [(near, F32), (wide, F32), ((2 * n1, LANES), F32)])]
  transfers between devices with their start and end apart: 11 -> 13, of which waited for: 4 -> 4; matrix products, arithmetic and copies ran while one was open for 0% -> 0% of each run, Pallas kernels for 15% -> 18%
where the time goes in v3:
time: 33.4 us; the launch traced here: 33.2 us
  starting transfers between devices  13.4 us (40%)
  Pallas kernels  11.8 us (35%)
  waiting for transfers between devices  7.33 us (22%)
  between operations  0.74 us (2%)
    ppermute x13, starting transfers between devices, swap(): return lax.ppermute(block, axis, [(i, i ^ bits) for i in range(count)])  13.4 us
    ppermute x13, waiting for transfers between devices, swap(): return lax.ppermute(block, axis, [(i, i ^ bits) for i in range(count)])  7.33 us
    pallas_call x1, Pallas kernels, body(): call(run(own_grad_kernel), [(row, BF16), (row, F32), (row, F32)], [(row,...  2.6 us
    pallas_call x1, Pallas kernels, body(): call(run(pack_kernel), [(row, BF16)] * 3 + [(kept, BF16), ((2 * n1, width...  1.92 us
    pallas_call x1, Pallas kernels, body(): call(run(scores_kernel), [(near, F32), (wide, F32), ((2 * n1, LANES), F32)])  1.67 us
    pallas_call x1, Pallas kernels, body(): call(run(levels_kernel), [(kept, F32), (kept, BF16), (stat1, F32), (stat1...  1.43 us
    pallas_call x1, Pallas kernels, body(): call(run(last_kernel), [(row, BF16)] * 2)(dk0, dv0, own_part, *parts)  1.27 us
    pallas_call x1, Pallas kernels, body(): call(run(delta_kernel), [(near, F32), (wide, F32), ((4 * n1, LANES), F32)])  1.12 us
  transfers between devices with their start and end apart: 13, of which 4 were waited for; matrix products, arithmetic and copies ran while one was open for 0% of the time, Pallas kernels for 18%

profile of v3, /device:TPU:0, one launch (start us, length us, event | category | flops | bytes accessed | tf_op | source)
XLA Modules:
  0.0 33.2 jit_solution(6435732875395852356)
XLA Ops:
  0.6 1.9 %shard_map.67 = (bf16[256,640]{1,0:T(8,128)(2,1)S(1)}, bf16[256,640]{1,0:T(8,128)(2,1)S(1)}, bf16[256,640]{1,0:T(8,128)(2,1)S(1)}, bf16[64,640]{1,0:T(8,128)(2,1...) custom-call(bf16[256,640]{1,0:T(8,128)(2,1)} %q_ref.1, ...), custom_call_target="tpu_custom_call" | custom-call | bytes 1048576 | tf_op jit(solution)/shard_map/pallas_call | solution.py:479
  2.6 3.1 %collective-permute-start = (bf16[64,640]{1,0:T(8,128)(2,1)S(1)}, bf16[64,640]{1,0:T(8,128)(2,1)S(1)}, u32[]{:S(2)}, u32[]{:S(2)}) collective-permute-start(bf16[64,640]{1,0:T(8,128)(2,1)S(1)} %get-tuple-element.43), channel_id=1, source_target_pairs={{0,1},{1,0},{2,3},{3,2},{4,5},{5,4},{6,7},{7,6},{8,9},{9,8},{10,11... | collective-permute-start | bytes 245768 | tf_op jit(solution)/shard_map/ppermute | solution.py:459
  5.6 2.6 %collective-permute-start.1 = (bf16[64,640]{1,0:T(8,128)(2,1)S(1)}, bf16[64,640]{1,0:T(8,128)(2,1)S(1)}, u32[]{:S(2)}, u32[]{:S(2)}) collective-permute-start(bf16[64,640]{1,0:T(8,128)(2,1)S(1)} %get-tuple-element.44), channel_id=1, source_target_pairs={{0,2},{1,3},{2,0},{3,1},{4,6},{5,7},{6,4},{7,5},{8,10},{9,11},{10,... | collective-permute-start | bytes 245768 | tf_op jit(solution)/shard_map/ppermute | solution.py:459
  8.2 0.0 collective-permute-start.2
  8.2 1.7 %collective-permute-start.5 = (bf16[128,640]{1,0:T(8,128)(2,1)S(1)}, bf16[128,640]{1,0:T(8,128)(2,1)S(1)}, u32[]{:S(2)}, u32[]{:S(2)}) collective-permute-start(bf16[128,640]{1,0:T(8,128)(2,1)S(1)} %get-tuple-element.54.refs_0_), channel_id=1, source_target_pairs={{0,8},{4,12},{8,0},{12,4},{16,24},{20,28},{24,16},{28,20},{1,9},{5... | collective-permute-start | bytes 491528 | tf_op jit(solution)/shard_map/ppermute | solution.py:459
  9.9 1.5 %collective-permute-start.7 = (bf16[64,640]{1,0:T(8,128)(2,1)S(1)}, bf16[64,640]{1,0:T(8,128)(2,1)S(1)}, u32[]{:S(2)}, u32[]{:S(2)}) collective-permute-start(bf16[64,640]{1,0:T(8,128)(2,1)S(1)} %get-tuple-element.55), channel_id=1, source_target_pairs={{0,24},{4,28},{8,16},{12,20},{16,8},{20,12},{24,0},{28,4},{1,25},{... | collective-permute-start | bytes 245768 | tf_op jit(solution)/shard_map/ppermute | solution.py:459
  11.4 0.0 collective-permute-done.refs_1_
  11.4 0.3 collective-permute-start.6
  11.7 3.1 %collective-permute-done.1.refs_2_ = bf16[64,640]{1,0:T(8,128)(2,1)S(1)} collective-permute-done((bf16[64,640]{1,0:T(8,128)(2,1)S(1)}, bf16[64,640]{1,0:T(8,128)(2,1)S(1)}, u32[]{:S(2)}, u32[]{:S(2)}) %collective-permute-start.1) | collective-permute-done | bytes 81952 | tf_op jit(solution)/shard_map/ppermute | solution.py:459
  14.8 0.0 collective-permute-start.3
  14.8 0.0 collective-permute-done.2.refs_3_
  14.8 0.3 shard_map.68
  15.2 0.6 %collective-permute-start.4 = (bf16[64,640]{1,0:T(8,128)(2,1)S(1)}, bf16[64,640]{1,0:T(8,128)(2,1)S(1)}, u32[]{:S(2)}, u32[]{:S(2)}) collective-permute-start(bf16[64,640]{1,0:T(8,128)(2,1)S(1)} %get-tuple-element.53.g_own), channel_id=1, source_target_pairs={{0,4},{4,0},{8,12},{12,8},{16,20},{20,16},{24,28},{28,24},{1,5},{5... | collective-permute-start | bytes 245768 | tf_op jit(solution)/shard_map/ppermute | solution.py:459
  15.7 0.9 %shard_map.69 = (f32[2048,256]{1,0:T(8,128)S(1)}, f32[256,128]{1,0:T(8,128)S(1)}, f32[64,128]{1,0:T(8,128)S(1)}) custom-call(bf16[256,640]{1,0:T(8,128)(2,1)S(1)} %get-tuple-element.40.qp, bf16[256,640]{1,0:T(8,128)(2,1)S(1)} %get-tuple-element.41.kp), custom_call_target="tpu_custom_call" | custom-call | bytes 1048576 | tf_op jit(solution)/shard_map/pallas_call | solution.py:493
  16.7 0.5 %shard_map.70 = (f32[2048,256]{1,0:T(8,128)S(1)}, f32[256,128]{1,0:T(8,128)S(1)}, f32[64,128]{1,0:T(8,128)S(1)}) custom-call(bf16[256,640]{1,0:T(8,128)(2,1)S(1)} %get-tuple-element.48.vp, f32[2048,256]{1,0:T(8,128)S(1)} %get-tuple-element.47.weight, bf16[256,640]{1,0:T(8,128)(2,1)S(1)} %get-tuple-element.46.gp), custom_call_target="tpu_custom_call" | custom-call | bytes 1048576 | tf_op jit(solution)/shard_map/pallas_call | solution.py:504
  17.2 0.0 collective-permute-done.7.refs_3_
  17.2 0.0 collective-permute-done.6.refs_2_
  17.2 0.0 collective-permute-done.3.q_other
  17.3 1.7 %shard_map.71 = (f32[1024,128]{1,0:T(8,128)S(1)}, f32[512,128]{1,0:T(8,128)S(1)}, f32[128,128]{1,0:T(8,128)S(1)}) custom-call(bf16[64,640]{1,0:T(8,128)(2,1)S(1)} %get-tuple-element.52.q_own, bf16[64,640]{1,0:T(8,128)(2,1)S(1)} %collective-permute-done.3.q_other, bf16[128,640]{1,0:T(8,128)(2,1)S(1)} %get-tuple-element.54.refs_0_, ...), custom_call_target="tpu_custom_call" | custom-call | bytes 1048576 | tf_op jit(solution)/shard_map/pallas_call | solution.py:499
  18.9 0.0 collective-permute-done.4.g_other
  18.9 1.1 %shard_map.72 = (f32[1024,128]{1,0:T(8,128)S(1)}, f32[512,128]{1,0:T(8,128)S(1)}, f32[256,128]{1,0:T(8,128)S(1)}) custom-call(bf16[64,640]{1,0:T(8,128)(2,1)S(1)} %get-tuple-element.53.g_own, bf16[64,640]{1,0:T(8,128)(2,1)S(1)} %collective-permute-done.4.g_other, f32[1024,128]{1,0:T(8,128)S(1)} %get-tuple-element.56.p1, ...), custom_call_target="tpu_custom_call" | custom-call | bytes 1048576 | tf_op jit(solution)/shard_map/pallas_call | solution.py:507
  20.1 0.1 collective-permute-start.8
  20.1 1.3 %collective-permute-done.8.theirs = f32[256,128]{1,0:T(8,128)S(1)} collective-permute-done((f32[256,128]{1,0:T(8,128)S(1)}, f32[256,128]{1,0:T(8,128)S(1)}, u32[]{:S(2)}, u32[]{:S(2)}) %collective-permute-start.8) | collective-permute-done | bytes 131104 | tf_op jit(solution)/shard_map/ppermute | solution.py:459
  21.5 1.4 %shard_map.73 = (f32[64,640]{1,0:T(8,128)S(1)}, bf16[64,640]{1,0:T(8,128)(2,1)S(1)}, f32[64,128]{1,0:T(8,128)S(1)}, f32[64,128]{1,0:T(8,128)S(1)}, f32[128,640]{...) custom-call(bf16[64,640]{1,0:T(8,128)(2,1)S(1)} %get-tuple-element.52.q_own, ...), custom_call_target="tpu_custom_call" | custom-call | bytes 1048576 | tf_op jit(solution)/shard_map/pallas_call | solution.py:512
  22.9 1.5 %collective-permute-start.10 = (bf16[128,640]{1,0:T(8,128)(2,1)S(1)}, bf16[128,640]{1,0:T(8,128)(2,1)S(1)}, u32[]{:S(2)}, u32[]{:S(2)}) collective-permute-start(bf16[128,640]{1,0:T(8,128)(2,1)S(1)} %get-tuple-element.72), channel_id=1, source_target_pairs={{0,8},{4,12},{8,0},{12,4},{16,24},{20,28},{24,16},{28,20},{1,9},{5... | collective-permute-start | bytes 491528 | tf_op jit(solution)/shard_map/ppermute | solution.py:459
  24.5 1.5 %collective-permute-start.11 = (bf16[64,640]{1,0:T(8,128)(2,1)S(1)}, bf16[64,640]{1,0:T(8,128)(2,1)S(1)}, u32[]{:S(2)}, u32[]{:S(2)}) collective-permute-start(bf16[64,640]{1,0:T(8,128)(2,1)S(1)} %get-tuple-element.73), channel_id=1, source_target_pairs={{0,16},{4,20},{8,24},{12,28},{16,0},{20,4},{24,8},{28,12},{1,17},{... | collective-permute-start | bytes 245768 | tf_op jit(solution)/shard_map/ppermute | solution.py:459
  26.0 0.5 %collective-permute-start.12 = (bf16[64,640]{1,0:T(8,128)(2,1)S(1)}, bf16[64,640]{1,0:T(8,128)(2,1)S(1)}, u32[]{:S(2)}, u32[]{:S(2)}) collective-permute-start(bf16[64,640]{1,0:T(8,128)(2,1)S(1)} %get-tuple-element.74), channel_id=1, source_target_pairs={{0,24},{4,28},{8,16},{12,20},{16,8},{20,12},{24,0},{28,4},{1,25},{... | collective-permute-start | bytes 245768 | tf_op jit(solution)/shard_map/ppermute | solution.py:459
  26.5 2.6 %shard_map.74 = (bf16[256,640]{1,0:T(8,128)(2,1)}, f32[256,640]{1,0:T(8,128)S(1)}, f32[256,640]{1,0:T(8,128)S(1)}) custom-call(bf16[256,640]{1,0:T(8,128)(2,1)S(1)} %get-tuple-element.40.qp, bf16[256,640]{1,0:T(8,128)(2,1)S(1)} %get-tuple-element.41.kp, bf16[256,640]{1,0:T(8,128)(2,1)S(1)} %get-tuple-element.46.gp, ...), custom_call_target="tpu_custom_call" | custom-call | bytes 1048576 | tf_op jit(solution)/shard_map/pallas_call | solution.py:523
  29.1 0.2 collective-permute-done.11.refs_1_
  29.3 2.6 %collective-permute-done.12.refs_2_ = bf16[64,640]{1,0:T(8,128)(2,1)S(1)} collective-permute-done((bf16[64,640]{1,0:T(8,128)(2,1)S(1)}, bf16[64,640]{1,0:T(8,128)(2,1)S(1)}, u32[]{:S(2)}, u32[]{:S(2)}) %collective-permute-start.12) | collective-permute-done | bytes 81952 | tf_op jit(solution)/shard_map/ppermute | solution.py:459
  31.9 0.0 collective-permute-done.10.refs_0_
  31.9 1.3 %shard_map.75 = (bf16[256,640]{1,0:T(8,128)(2,1)}, bf16[256,640]{1,0:T(8,128)(2,1)}) custom-call(f32[256,640]{1,0:T(8,128)S(1)} %get-tuple-element.69.dk0, f32[256,640]{1,0:T(8,128)S(1)} %get-tuple-element.70.dv0, f32[128,640]{1,0:T(8,128)S(1)} %get-tuple-element.71.own, bf16[128,640]{1,0:T(8,128)(2,1)S(1)} %collective-permute-done.10.refs_0_, ...), custom_call_target="tpu_custom_call" | custom-call | bytes 1048576 | tf_op jit(solution)/shard_map/pallas_call | solution.py:526
  (3 shorter events, 0.0 us)
Async XLA Ops:
  2.6 8.9 %collective-permute-start = (bf16[64,640]{1,0:T(8,128)(2,1)S(1)}, bf16[64,640]{1,0:T(8,128)(2,1)S(1)}, u32[]{:S(2)}, u32[]{:S(2)}) collective-permute-start(bf16[64,640]{1,0:T(8,128)(2,1)S(1)} %get-tuple-element.43), channel_id=1, source_target_pairs={{0,1},{1,0},{2,3},{3,2},{4,5},{5,4},{6,7},{7,6},{8,9},{9,8},{10,11... | collective-permute-start | bytes 245768 | tf_op jit(solution)/shard_map/ppermute | solution.py:459
  5.6 9.2 %collective-permute-start.1 = (bf16[64,640]{1,0:T(8,128)(2,1)S(1)}, bf16[64,640]{1,0:T(8,128)(2,1)S(1)}, u32[]{:S(2)}, u32[]{:S(2)}) collective-permute-start(bf16[64,640]{1,0:T(8,128)(2,1)S(1)} %get-tuple-element.44), channel_id=1, source_target_pairs={{0,2},{1,3},{2,0},{3,1},{4,6},{5,7},{6,4},{7,5},{8,10},{9,11},{10,... | collective-permute-start | bytes 245768 | tf_op jit(solution)/shard_map/ppermute | solution.py:459
  8.2 6.6 %collective-permute-start.2 = (bf16[64,640]{1,0:T(8,128)(2,1)S(1)}, bf16[64,640]{1,0:T(8,128)(2,1)S(1)}, u32[]{:S(2)}, u32[]{:S(2)}) collective-permute-start(bf16[64,640]{1,0:T(8,128)(2,1)S(1)} %get-tuple-element.45), channel_id=1, source_target_pairs={{0,3},{1,2},{2,1},{3,0},{4,7},{5,6},{6,5},{7,4},{8,11},{9,10},{10,... | collective-permute-start | bytes 245768 | tf_op jit(solution)/shard_map/ppermute | solution.py:459
  8.2 9.0 %collective-permute-start.5 = (bf16[128,640]{1,0:T(8,128)(2,1)S(1)}, bf16[128,640]{1,0:T(8,128)(2,1)S(1)}, u32[]{:S(2)}, u32[]{:S(2)}) collective-permute-start(bf16[128,640]{1,0:T(8,128)(2,1)S(1)} %get-tuple-element.54.refs_0_), channel_id=1, source_target_pairs={{0,8},{4,12},{8,0},{12,4},{16,24},{20,28},{24,16},{28,20},{1,9},{5... | collective-permute-start | bytes 491528 | tf_op jit(solution)/shard_map/ppermute | solution.py:459
  9.9 7.3 %collective-permute-start.7 = (bf16[64,640]{1,0:T(8,128)(2,1)S(1)}, bf16[64,640]{1,0:T(8,128)(2,1)S(1)}, u32[]{:S(2)}, u32[]{:S(2)}) collective-permute-start(bf16[64,640]{1,0:T(8,128)(2,1)S(1)} %get-tuple-element.55), channel_id=1, source_target_pairs={{0,24},{4,28},{8,16},{12,20},{16,8},{20,12},{24,0},{28,4},{1,25},{... | collective-permute-start | bytes 245768 | tf_op jit(solution)/shard_map/ppermute | solution.py:459
  11.4 5.8 %collective-permute-start.6 = (bf16[64,640]{1,0:T(8,128)(2,1)S(1)}, bf16[64,640]{1,0:T(8,128)(2,1)S(1)}, u32[]{:S(2)}, u32[]{:S(2)}) collective-permute-start(bf16[64,640]{1,0:T(8,128)(2,1)S(1)} %get-tuple-element.55), channel_id=1, source_target_pairs={{0,16},{4,20},{8,24},{12,28},{16,0},{20,4},{24,8},{28,12},{1,17},{... | collective-permute-start | bytes 245768 | tf_op jit(solution)/shard_map/ppermute | solution.py:459
  14.8 2.4 %collective-permute-start.3 = (bf16[64,640]{1,0:T(8,128)(2,1)S(1)}, bf16[64,640]{1,0:T(8,128)(2,1)S(1)}, u32[]{:S(2)}, u32[]{:S(2)}) collective-permute-start(bf16[64,640]{1,0:T(8,128)(2,1)S(1)} %get-tuple-element.52.q_own), channel_id=1, source_target_pairs={{0,4},{4,0},{8,12},{12,8},{16,20},{20,16},{24,28},{28,24},{1,5},{5... | collective-permute-start | bytes 245768 | tf_op jit(solution)/shard_map/ppermute | solution.py:459
  15.2 3.8 %collective-permute-start.4 = (bf16[64,640]{1,0:T(8,128)(2,1)S(1)}, bf16[64,640]{1,0:T(8,128)(2,1)S(1)}, u32[]{:S(2)}, u32[]{:S(2)}) collective-permute-start(bf16[64,640]{1,0:T(8,128)(2,1)S(1)} %get-tuple-element.53.g_own), channel_id=1, source_target_pairs={{0,4},{4,0},{8,12},{12,8},{16,20},{20,16},{24,28},{28,24},{1,5},{5... | collective-permute-start | bytes 245768 | tf_op jit(solution)/shard_map/ppermute | solution.py:459
  20.1 1.4 %collective-permute-start.8 = (f32[256,128]{1,0:T(8,128)S(1)}, f32[256,128]{1,0:T(8,128)S(1)}, u32[]{:S(2)}, u32[]{:S(2)}) collective-permute-start(f32[256,128]{1,0:T(8,128)S(1)} %get-tuple-element.63.mine), channel_id=1, source_target_pairs={{0,4},{4,0},{8,12},{12,8},{16,20},{20,16},{24,28},{28,24},{1,5},{5... | collective-permute-start | bytes 393224 | tf_op jit(solution)/shard_map/ppermute | solution.py:459
  22.9 9.0 %collective-permute-start.10 = (bf16[128,640]{1,0:T(8,128)(2,1)S(1)}, bf16[128,640]{1,0:T(8,128)(2,1)S(1)}, u32[]{:S(2)}, u32[]{:S(2)}) collective-permute-start(bf16[128,640]{1,0:T(8,128)(2,1)S(1)} %get-tuple-element.72), channel_id=1, source_target_pairs={{0,8},{4,12},{8,0},{12,4},{16,24},{20,28},{24,16},{28,20},{1,9},{5... | collective-permute-start | bytes 491528 | tf_op jit(solution)/shard_map/ppermute | solution.py:459
  24.5 2.0 %collective-permute-start.9 = (bf16[64,640]{1,0:T(8,128)(2,1)S(1)}, bf16[64,640]{1,0:T(8,128)(2,1)S(1)}, u32[]{:S(2)}, u32[]{:S(2)}) collective-permute-start(bf16[64,640]{1,0:T(8,128)(2,1)S(1)} %get-tuple-element.67), channel_id=1, source_target_pairs={{0,4},{4,0},{8,12},{12,8},{16,20},{20,16},{24,28},{28,24},{1,5},{5... | collective-permute-start | bytes 245768 | tf_op jit(solution)/shard_map/ppermute | solution.py:459
  24.5 4.9 %collective-permute-start.11 = (bf16[64,640]{1,0:T(8,128)(2,1)S(1)}, bf16[64,640]{1,0:T(8,128)(2,1)S(1)}, u32[]{:S(2)}, u32[]{:S(2)}) collective-permute-start(bf16[64,640]{1,0:T(8,128)(2,1)S(1)} %get-tuple-element.73), channel_id=1, source_target_pairs={{0,16},{4,20},{8,24},{12,28},{16,0},{20,4},{24,8},{28,12},{1,17},{... | collective-permute-start | bytes 245768 | tf_op jit(solution)/shard_map/ppermute | solution.py:459
  26.0 6.0 %collective-permute-start.12 = (bf16[64,640]{1,0:T(8,128)(2,1)S(1)}, bf16[64,640]{1,0:T(8,128)(2,1)S(1)}, u32[]{:S(2)}, u32[]{:S(2)}) collective-permute-start(bf16[64,640]{1,0:T(8,128)(2,1)S(1)} %get-tuple-element.74), channel_id=1, source_target_pairs={{0,24},{4,28},{8,16},{12,20},{16,8},{20,12},{24,0},{28,4},{1,25},{... | collective-permute-start | bytes 245768 | tf_op jit(solution)/shard_map/ppermute | solution.py:459

commit v4 on v3

--- a/solution.py
+++ b/solution.py
@@ -130,14 +130,14 @@
     return jnp.where(qpos >= kpos, 0.0, -jnp.inf)
 
 
-def call(kernel, outs, scratch=(), flops=0, specs=None):
+def call(kernel, outs, scratch=(), flops=0, **specs):
     return pl.pallas_call(
         kernel,
         out_shape=[jax.ShapeDtypeStruct(s, d) for s, d in outs],
-        **({} if specs is None else {"in_specs": specs}),
         scratch_shapes=[pltpu.VMEM(*s) if isinstance(s, tuple) else s for s in scratch],
         compiler_params=pltpu.CompilerParams(vmem_limit_bytes=VMEM_BYTES),
         cost_estimate=pl.CostEstimate(flops=flops, bytes_accessed=2**20, transcendentals=0),
+        **specs,
     )
 
 
@@ -173,7 +173,7 @@
         copy.wait()
 
 
-def own_scores_kernel(p, qp, kp, weight, lse0, lse01):
+def own_scores_kernel(p, qp, kp, after, weight, lse0, lse01):
     bias = own_bias(p)
     lane = iota((1, LANES), 1)
     lse_all = jnp.zeros((p.tokens, LANES), F32)
@@ -190,13 +190,13 @@
     lse01[...] = pick(p, lse_all, lane_class(p))
 
 
-def gather_kernel(p, *refs):
+def gather_kernel(p, after, *refs):
     gz, (gp, g1, natural) = refs[: p.zcount], refs[p.zcount :]
     z = lax.axis_index("head")
     share = p.tokens // p.zcount
     for b in range(p.zcount):
         start = pl.multiple_of(jnp.bitwise_xor(z, b) * share, share)
-        natural[pl.ds(start, share), :] = gz[b][...]
+        natural[pl.ds(start, share), :] = gz[p.zcount - 1 - b][...]
     g = nn(phase_order(p), natural[...])
     gp[...] = g.astype(BF16)
     g1[...] = pick(p, g, column_class(p)).astype(BF16)
@@ -221,26 +221,21 @@
     return jnp.concatenate([stat[:, h : h + 1] for h in range(p.heads)], axis=0)
 
 
-def to_lanes(p, column):
+def to_lanes(p, column, count):
     lane = iota((1, LANES), 1)
-    count = 2 * p.n1
-    out = jnp.zeros((count, LANES), F32)
+    out = jnp.zeros((2 * count, LANES), F32)
     for h in range(p.heads):
-        out = jnp.where(lane == h, column[h * count : (h + 1) * count], out)
+        out = jnp.where(lane == h, column[2 * h * count : 2 * (h + 1) * count], out)
     return out
 
 
-def wide_rows(p, column):
-    starts = range(0, 2 * p.heads * p.n1, p.n1)
-    return jnp.concatenate([column[s : s + p.n2] for s in starts], axis=0)
-
-
-def widen(p, column, fill):
-    rest = jnp.full((p.n1 - p.n2, column.shape[1]), fill, F32)
-    parts = []
-    for s in range(0, 2 * p.heads * p.n2, p.n2):
-        parts += [column[s : s + p.n2], rest]
-    return jnp.concatenate(parts, axis=0)
+def wide_rows(p, stat):
+    return jnp.concatenate([stat[: p.n2], stat[p.n1 : p.n1 + p.n2]], axis=0)
+
+
+def widen(p, stat, fill):
+    rest = jnp.full((p.n1 - p.n2, LANES), fill, F32)
+    return jnp.concatenate([stat[: p.n2], rest, stat[p.n2 :], rest], axis=0)
 
 
 def cut(p, block, start, count):
@@ -289,27 +284,29 @@
             out[:count, low_h:high_h] = jnp.where(hit, piece, out[:count, low_h:high_h])
 
 
-def key_blocks(p, half, kv):
-    blocks = [ref[...] for ref in kv]
-    near = [cut(p, blocks[i], half * p.n1, p.n1) for i in range(p.g1 // 2)]
-    wide = [cut(p, blocks[i], half * p.rows[2 * i] // 2, p.n2) for i in range(p.g2 // 2)]
-    return jnp.concatenate(near, axis=0).astype(BF16), jnp.concatenate(wide, axis=0).astype(BF16)
-
-
-def soft(scores):
+def near_blocks(p, half, kv):
+    blocks = [cut(p, ref[...], half * p.n1, p.n1) for ref in kv[: p.g1 // 2]]
+    return jnp.concatenate(blocks, axis=0).astype(BF16)
+
+
+def wide_blocks(p, half, kv):
+    blocks = [cut(p, ref[...], half * ref.shape[0] // 2, p.n2) for ref in kv]
+    return jnp.concatenate(blocks, axis=0).astype(BF16)
+
+
+def soft(p, scores, count, e, tops, sums):
     top = jnp.maximum(jnp.max(scores, axis=1, keepdims=True), LOWEST)
-    e = jnp.exp2(scores - top)
-    return top, e, jnp.sum(e, axis=1, keepdims=True)
-
-
-def scores_kernel(p, q_own, q_other, *refs):
-    kv, (p1, p2, lse) = refs[: p.g2 // 2], refs[p.g2 // 2 :]
+    weight = jnp.exp2(scores - top)
+    e[...] = weight
+    tops[...] = to_lanes(p, top, count)
+    sums[...] = to_lanes(p, jnp.sum(weight, axis=1, keepdims=True), count)
+
+
+def near_kernel(p, q_own, q_other, *refs):
+    kv, outs = refs[: p.g1 // 2], refs[p.g1 // 2 :]
     d = lax.axis_index("seq")
     n1, n2 = p.n1, p.n2
-    k1, k2 = key_blocks(p, 0, kv)
-    q1 = both_cores(p, q_own[...], q_other[...], n1)
-    q2 = both_cores(p, q_own[...], q_other[...], n2)
-
+    q = both_cores(p, q_own[...], q_other[...], n1)
     row = iota((2 * p.heads * n1, 1), 0)
     col = iota((1, p.g1 // 2 * n1), 1)
     head = first_head(p) + row // (2 * n1)
@@ -319,39 +316,41 @@
     other = col % n1
     kbase = p.tokens * jnp.bitwise_xor(d, 2 * (col // n1)) + p.r2 * (other % n2)
     kpos = kbase + jnp.bitwise_and(head + DIL1 * (other // n2), p.r2 - 1)
-    s1 = jnp.where(kpos <= qpos, against(p, q1, k1) * SCALE2, -jnp.inf)
-    top1, e1, sum1 = soft(s1)
-
-    row2 = iota((2 * p.heads * n2, 1), 0)
-    row2 = jnp.bitwise_xor(d, row2 // n2 % 2) * n2 + row2 % n2
-    col2 = iota((1, p.g2 // 2 * n2), 1)
-    col2 = jnp.bitwise_xor(d, 2 * (col2 // n2)) * n2 + col2 % n2
-    s2 = jnp.where(col2 <= row2, against(p, q2, k2) * SCALE2, -jnp.inf)
-    top2, e2, sum2 = soft(s2)
-
-    top2_all, sum2_all = widen(p, top2, LOWEST), widen(p, sum2, 0.0)
-    peak = jnp.maximum(top1, top2_all)
-    both = sum1 * jnp.exp2(top1 - peak) + sum2_all * jnp.exp2(top2_all - peak)
-    part = peak + jnp.log2(jnp.maximum(both, TINY))
-    p1[...] = e1 * jnp.exp2(top1 - part)
-    p2[...] = e2 * jnp.exp2(top2 - wide_rows(p, part))
-    lse[...] = to_lanes(p, part)
-
-
-def delta_kernel(p, g_own, g_other, p1, p2, lse, lse01, d01, *refs):
+    s = jnp.where(kpos <= qpos, against(p, q, near_blocks(p, 0, kv)) * SCALE2, -jnp.inf)
+    soft(p, s, n1, *outs)
+
+
+def wide_kernel(p, q_own, q_other, *refs):
+    kv, outs = refs[: p.g2 // 2], refs[p.g2 // 2 :]
+    d = lax.axis_index("seq")
+    n2 = p.n2
+    q = both_cores(p, q_own[...], q_other[...], n2)
+    row = iota((2 * p.heads * n2, 1), 0)
+    row = jnp.bitwise_xor(d, row // n2 % 2) * n2 + row % n2
+    col = iota((1, p.g2 // 2 * n2), 1)
+    col = jnp.bitwise_xor(d, 2 * (col // n2)) * n2 + col % n2
+    s = jnp.where(col <= row, against(p, q, wide_blocks(p, 0, kv)) * SCALE2, -jnp.inf)
+    soft(p, s, n2, *outs)
+
+
+def delta_kernel(p, g_own, g_other, e1, e2, top1, sum1, top2, sum2, lse01, d01, *refs):
     kv, (dp1, dp2, stats) = refs[: p.g2 // 2], refs[p.g2 // 2 :]
-    n1 = p.n1
-    v1, v2 = key_blocks(p, 1, kv)
-    dp = against(p, both_cores(p, g_own[...], g_other[...], n1), v1)
+    n1, n2 = p.n1, p.n2
+    dp = against(p, both_cores(p, g_own[...], g_other[...], n1), near_blocks(p, 1, kv))
     dp1[...] = dp
-    d = jnp.sum(p1[...] * dp, axis=1, keepdims=True)
-    dp = against(p, both_cores(p, g_own[...], g_other[...], p.n2), v2)
+    near = to_lanes(p, jnp.sum(e1[...] * dp, axis=1, keepdims=True), n1)
+    dp = against(p, both_cores(p, g_own[...], g_other[...], n2), wide_blocks(p, 1, kv))
     dp2[...] = dp
-    d += widen(p, jnp.sum(p2[...] * dp, axis=1, keepdims=True), 0.0)
-    d = to_lanes(p, d)
-    part = lse[:n1, :]
-    total, delta = join(lse01[...], d01[...], part, d[:n1])
-    stats[...] = jnp.concatenate([total, delta, lse[n1:, :], d[n1:]], axis=0)
+    wide = to_lanes(p, jnp.sum(e2[...] * dp, axis=1, keepdims=True), n2)
+
+    top1, top2 = top1[...], widen(p, top2[...], LOWEST)
+    peak = jnp.maximum(top1, top2)
+    up1, up2 = jnp.exp2(top1 - peak), jnp.exp2(top2 - peak)
+    both = jnp.maximum(sum1[...] * up1 + widen(p, sum2[...], 0.0) * up2, TINY)
+    lse = peak + jnp.log2(both)
+    d = (near * up1 + widen(p, wide, 0.0) * up2) / both
+    total, delta = join(lse01[...], d01[...], lse[:n1], d[:n1])
+    stats[...] = jnp.concatenate([total, delta, lse[n1:], d[n1:]], axis=0)
 
 
 def join(lse_a, d_a, lse_b, d_b):
@@ -360,7 +359,9 @@
     return total, jnp.exp2(lse_a - total) * d_a + jnp.exp2(lse_b - total) * d_b
 
 
-def levels_kernel(p, q_own, q_other, g_own, g_other, p1, p2, dp1, dp2, lse, mine, theirs, *refs):
+def levels_kernel(
+    p, q_own, q_other, g_own, g_other, e1, e2, top1, top2, dp1, dp2, mine, theirs, *refs
+):
     kv, refs = refs[: p.g2 // 2], refs[p.g2 // 2 :]
     dq_own, dq_other, total1, delta1, own_part = refs[:5]
     outs, (dk1, dv1, dk2, dv2, dq1, dq2) = refs[5:-6], refs[-6:]
@@ -370,18 +371,17 @@
     second = join(quarter(theirs, 0), quarter(theirs, 1), quarter(mine, 2), quarter(mine, 3))
     total1[...], delta1[...] = first
     total = jnp.concatenate([first[0], second[0]], axis=0)
-    share = columns(p, jnp.exp2(lse[...] - total))
-    delta = columns(p, jnp.concatenate([first[1], second[1]], axis=0))
-    k1, k2 = key_blocks(p, 0, kv)
+    delta = jnp.concatenate([first[1], second[1]], axis=0)
+    k1, k2 = near_blocks(p, 0, kv), wide_blocks(p, 0, kv)
     for ref in (dk1, dv1, dk2, dv2):
         ref[...] = jnp.zeros_like(ref)
 
-    prob = p1[...] * share
-    ds = (prob * (dp1[...] - delta) * SCALE).astype(BF16)
+    prob = e1[...] * columns(p, jnp.exp2(top1[...] - total))
+    ds = (prob * (dp1[...] - columns(p, delta)) * SCALE).astype(BF16)
     collect(p, prob.astype(BF16), both_cores(p, g_own[...], g_other[...], n1), dv1)
     collect(p, ds, both_cores(p, q_own[...], q_other[...], n1), dk1)
-    prob2 = p2[...] * wide_rows(p, share)
-    ds2 = (prob2 * (dp2[...] - wide_rows(p, delta)) * SCALE).astype(BF16)
+    prob2 = e2[...] * columns(p, jnp.exp2(top2[...] - wide_rows(p, total)))
+    ds2 = (prob2 * (dp2[...] - columns(p, wide_rows(p, delta))) * SCALE).astype(BF16)
     collect(p, prob2.astype(BF16), both_cores(p, g_own[...], g_other[...], n2), dv2)
     collect(p, ds2, both_cores(p, q_own[...], q_other[...], n2), dk2)
     for i in range(p.g2 // 2):
@@ -431,27 +431,27 @@
 
 
 def last_kernel(p, dk0, dv0, own, *refs):
-    came, (grad_k, grad_v) = refs[:-2], refs[-2:]
+    came, (grad_k, grad_v, out_k, out_v, sems) = refs[:-5], refs[-5:]
     order = phase_order(p, True)
     label = column_class(p)
     zero = jnp.zeros((p.tokens, p.width), F32)
-    sums = own[...]
-    wide = []
-    for ref, b in zip(came, range(2, p.g2, 2)):
-        block = ref[...].astype(F32)
-        if b < p.g1:
-            sums = sums + block
-        else:
-            wide.append(block)
-    for index, (base, grad) in enumerate(((dk0, grad_k), (dv0, grad_v))):
-        kept = sums[index * p.n1 : (index + 1) * p.n1]
-        if wide:
-            first = kept[: p.n2]
-            for block in wide:
-                first = first + block[index * p.n2 : (index + 1) * p.n2]
-            kept = jnp.concatenate([first, kept[p.n2 :]], axis=0)
+    copies = []
+    for index, (base, out, grad) in enumerate(((dk0, out_k, grad_k), (dv0, out_v, grad_v))):
+        first = own[index * p.n1 : index * p.n1 + p.n2, :]
+        rest = own[index * p.n1 + p.n2 : (index + 1) * p.n1, :]
+        for ref in came:
+            half = ref.shape[0] // 2
+            block = ref[...].astype(F32)
+            first = first + block[index * half : index * half + p.n2]
+            if half == p.n1:
+                rest = rest + block[index * half + p.n2 : (index + 1) * half]
+        kept = jnp.concatenate([first, rest], axis=0)
         whole = base[...] + spread(p, kept, label, zero)
-        grad[...] = nn(order, whole.astype(BF16)).astype(BF16)
+        out[...] = nn(order, whole.astype(BF16)).astype(BF16)
+        copies.append(pltpu.make_async_copy(out, grad, sems.at[index]))
+        copies[-1].start()
+    for copy in copies:
+        copy.wait()
 
 
 def swap(block, axis, bits):
@@ -482,7 +482,7 @@
         + [(kept, BF16), ((2 * n1, width), BF16), ((2 * n2, width), BF16)]
         + [(share, BF16)] * p.zcount,
         [(row, BF16)] * 3 + [pltpu.SemaphoreType.DMA((p.zcount + 3,))],
-        specs=[hbm] * 4,
+        in_specs=[hbm] * 4,
     )(queries, keys, values, grad_out)
     qp, kp, vp, q1, kv1, kv2 = outs[:6]
     gz = outs[6:]
@@ -490,23 +490,28 @@
 
     kv = [kv1] + [swap(kv1 if b < p.g1 else kv2, "seq", b) for b in even[1:]]
 
+    q_other = swap(q1, "seq", 1)
     weight, lse0, lse01 = call(
         run(own_scores_kernel), [(flat(p.heads * tokens), F32), (stat, F32), (stat1, F32)]
-    )(qp, kp)
-    q_other = swap(q1, "seq", 1)
+    )(qp, kp, q_other)
     near = (2 * p.heads * n1, p.g1 // 2 * n1)
     wide = (2 * p.heads * n2, p.g2 // 2 * n2)
-    p1, p2, lse = call(run(scores_kernel), [(near, F32), (wide, F32), ((2 * n1, LANES), F32)])(
+    e1, top1, sum1 = call(run(near_kernel), [(near, F32)] + [((2 * n1, LANES), F32)] * 2)(
+        q1, q_other, *kv[: p.g1 // 2]
+    )
+    e2, top2, sum2 = call(run(wide_kernel), [(wide, F32)] + [((2 * n2, LANES), F32)] * 2)(
         q1, q_other, *kv
     )
-    gp, g1 = call(run(gather_kernel), [(row, BF16), (kept, BF16)], [(row, BF16)])(*gz)
+    gp, g1 = call(run(gather_kernel), [(row, BF16), (kept, BF16)], [(row, BF16)])(
+        lse01, *gz[::-1]
+    )
     g_other = swap(g1, "seq", 1)
     dprob, d0, d01 = call(
         run(own_delta_kernel), [(flat(p.heads * tokens), F32), (stat, F32), (stat1, F32)]
     )(vp, weight, gp)
     dp1, dp2, mine = call(
         run(delta_kernel), [(near, F32), (wide, F32), ((4 * n1, LANES), F32)]
-    )(g1, g_other, p1, p2, lse, lse01, d01, *kv)
+    )(g1, g_other, e1, e2, top1, sum1, top2, sum2, lse01, d01, *kv)
     theirs = swap(mine, "seq", 1)
     part = lambda b, dtype: ((p.rows[b], width), dtype)
     outs = call(
@@ -516,14 +521,19 @@
         [((near[1], width), F32)] * 2
         + [((wide[1], width), F32)] * 2
         + [((2 * n1, width), F32), ((2 * n2, width), F32)],
-    )(q1, q_other, g1, g_other, p1, p2, dp1, dp2, lse, mine, theirs, *kv)
+    )(q1, q_other, g1, g_other, e1, e2, top1, top2, dp1, dp2, mine, theirs, *kv)
     dq_own, dq_other, total1, delta1, own_part = outs[:5]
     parts = [swap(s, "seq", b) for s, b in zip(outs[5:], even[1:])]
     dq_came = swap(dq_other, "seq", 1)
     grad_q, dk0, dv0 = call(
         run(own_grad_kernel), [(row, BF16), (row, F32), (row, F32)], [(row, F32)]
     )(qp, kp, gp, weight, dprob, lse0, d0, total1, delta1, dq_own, dq_came)
-    grad_k, grad_v = call(run(last_kernel), [(row, BF16)] * 2)(dk0, dv0, own_part, *parts)
+    grad_k, grad_v = call(
+        run(last_kernel),
+        [(row, BF16)] * 2,
+        [(row, BF16)] * 2 + [pltpu.SemaphoreType.DMA((2,))],
+        out_specs=[hbm] * 2,
+    )(dk0, dv0, own_part, *parts)
     return grad_q, grad_k, grad_v
 
 

time: 33.4 us -> 32 us (0.958)
  Pallas kernels: 11.8 us -> 10.9 us
    pallas_call x1, Pallas kernels: 1.12 us -> 0.47 us  [body(): call(run(delta_kernel), [(near, F32), (wide, F32), ((4 * n1, LANES), F32)])]
    pallas_call x3 -> x4, Pallas kernels: 3.25 us -> 2.9 us  [the longest x1 1.27 us: body(): call(run(last_kernel), [(row, BF16)] * 2, [(row, BF16)] * 2 + [pltpu.Sema...]
  transfers between devices with their start and end apart: 13 -> 13, of which waited for: 4 -> 6; matrix products, arithmetic and copies ran while one was open for 0% -> 0% of each run, Pallas kernels for 18% -> 18%
where the time goes in v4:
time: 32 us; the launch traced here: 31.8 us
  starting transfers between devices  13.2 us (41%)
  Pallas kernels  10.9 us (34%)
  waiting for transfers between devices  7.03 us (22%)
  between operations  0.74 us (2%)
    ppermute x13, starting transfers between devices, swap(): return lax.ppermute(block, axis, [(i, i ^ bits) for i in range(count)])  13.2 us
    ppermute x13, waiting for transfers between devices, swap(): return lax.ppermute(block, axis, [(i, i ^ bits) for i in range(count)])  7.03 us
    pallas_call x1, Pallas kernels, body(): call(run(own_grad_kernel), [(row, BF16), (row, F32), (row, F32)], [(row,...  2.6 us
    pallas_call x1, Pallas kernels, body(): call(run(pack_kernel), [(row, BF16)] * 3 + [(kept, BF16), ((2 * n1, width...  1.92 us
    pallas_call x1, Pallas kernels, body(): call(run(levels_kernel), [(kept, F32), (kept, BF16), (stat1, F32), (stat1...  1.56 us
    pallas_call x1, Pallas kernels, body(): call(run(last_kernel), [(row, BF16)] * 2, [(row, BF16)] * 2 + [pltpu.Sema...  1.27 us
    pallas_call x1, Pallas kernels, body(): call(run(own_scores_kernel), [(flat(p.heads * tokens), F32), (stat, F32),...  0.93 us
    pallas_call x1, Pallas kernels, body(): call(run(near_kernel), [(near, F32)] + [((2 * n1, LANES), F32)] * 2)  0.91 us
  transfers between devices with their start and end apart: 13, of which 6 were waited for; matrix products, arithmetic and copies ran while one was open for 0% of the time, Pallas kernels for 18%

profile of v4, /device:TPU:0, one launch (start us, length us, event | category | flops | bytes accessed | tf_op | source)
XLA Modules:
  0.0 31.8 jit_solution(11016411069783116356)
XLA Ops:
  0.6 1.9 %shard_map.67 = (bf16[256,640]{1,0:T(8,128)(2,1)S(1)}, bf16[256,640]{1,0:T(8,128)(2,1)S(1)}, bf16[256,640]{1,0:T(8,128)(2,1)S(1)}, bf16[64,640]{1,0:T(8,128)(2,1...) custom-call(bf16[256,640]{1,0:T(8,128)(2,1)} %q_ref.1, ...), custom_call_target="tpu_custom_call" | custom-call | bytes 1048576 | tf_op jit(solution)/shard_map/pallas_call | solution.py:479
  2.6 0.5 %collective-permute-start = (bf16[64,640]{1,0:T(8,128)(2,1)S(1)}, bf16[64,640]{1,0:T(8,128)(2,1)S(1)}, u32[]{:S(2)}, u32[]{:S(2)}) collective-permute-start(bf16[64,640]{1,0:T(8,128)(2,1)S(1)} %get-tuple-element.45.q_own), channel_id=1, source_target_pairs={{0,4},{4,0},{8,12},{12,8},{16,20},{20,16},{24,28},{28,24},{1,5},{5... | collective-permute-start | bytes 245768 | tf_op jit(solution)/shard_map/ppermute | solution.py:459
  3.1 4.7 %collective-permute-start.1 = (bf16[64,640]{1,0:T(8,128)(2,1)S(1)}, bf16[64,640]{1,0:T(8,128)(2,1)S(1)}, u32[]{:S(2)}, u32[]{:S(2)}) collective-permute-start(bf16[64,640]{1,0:T(8,128)(2,1)S(1)} %get-tuple-element.47), channel_id=1, source_target_pairs={{0,3},{1,2},{2,1},{3,0},{4,7},{5,6},{6,5},{7,4},{8,11},{9,10},{10,... | collective-permute-start | bytes 245768 | tf_op jit(solution)/shard_map/ppermute | solution.py:459
  7.8 1.5 %collective-permute-start.5 = (bf16[128,640]{1,0:T(8,128)(2,1)S(1)}, bf16[128,640]{1,0:T(8,128)(2,1)S(1)}, u32[]{:S(2)}, u32[]{:S(2)}) collective-permute-start(bf16[128,640]{1,0:T(8,128)(2,1)S(1)} %get-tuple-element.58.refs_0_), channel_id=1, source_target_pairs={{0,8},{4,12},{8,0},{12,4},{16,24},{20,28},{24,16},{28,20},{1,9},{5... | collective-permute-start | bytes 491528 | tf_op jit(solution)/shard_map/ppermute | solution.py:459
  9.2 0.8 %collective-permute-start.3 = (bf16[64,640]{1,0:T(8,128)(2,1)S(1)}, bf16[64,640]{1,0:T(8,128)(2,1)S(1)}, u32[]{:S(2)}, u32[]{:S(2)}) collective-permute-start(bf16[64,640]{1,0:T(8,128)(2,1)S(1)} %get-tuple-element.49), channel_id=1, source_target_pairs={{0,1},{1,0},{2,3},{3,2},{4,5},{5,4},{6,7},{7,6},{8,9},{9,8},{10,11... | collective-permute-start | bytes 245768 | tf_op jit(solution)/shard_map/ppermute | solution.py:459
  10.0 0.0 collective-permute-done.after.q_other
  10.0 1.5 %collective-permute-start.7 = (bf16[64,640]{1,0:T(8,128)(2,1)S(1)}, bf16[64,640]{1,0:T(8,128)(2,1)S(1)}, u32[]{:S(2)}, u32[]{:S(2)}) collective-permute-start(bf16[64,640]{1,0:T(8,128)(2,1)S(1)} %get-tuple-element.60), channel_id=1, source_target_pairs={{0,24},{4,28},{8,16},{12,20},{16,8},{20,12},{24,0},{28,4},{1,25},{... | collective-permute-start | bytes 245768 | tf_op jit(solution)/shard_map/ppermute | solution.py:459
  11.5 0.9 %shard_map.68 = (f32[2048,256]{1,0:T(8,128)S(1)}, f32[256,128]{1,0:T(8,128)S(1)}, f32[64,128]{1,0:T(8,128)S(1)}) custom-call(bf16[256,640]{1,0:T(8,128)(2,1)S(1)} %get-tuple-element.43.qp, bf16[256,640]{1,0:T(8,128)(2,1)S(1)} %get-tuple-element.44.kp, bf16[64,640]{1,0:T(8,128)(2,1)S(1)} %collective-permute-done.after.q_other), custom_call_target="tpu_custom_call" | custom-call | bytes 1048576 | tf_op jit(solution)/shard_map/pallas_call | solution.py:494
  12.5 0.4 %collective-permute-start.6 = (bf16[64,640]{1,0:T(8,128)(2,1)S(1)}, bf16[64,640]{1,0:T(8,128)(2,1)S(1)}, u32[]{:S(2)}, u32[]{:S(2)}) collective-permute-start(bf16[64,640]{1,0:T(8,128)(2,1)S(1)} %get-tuple-element.60), channel_id=1, source_target_pairs={{0,16},{4,20},{8,24},{12,28},{16,0},{20,4},{24,8},{28,12},{1,17},{... | collective-permute-start | bytes 245768 | tf_op jit(solution)/shard_map/ppermute | solution.py:459
  12.9 2.4 %collective-permute-done.2.refs_1_ = bf16[64,640]{1,0:T(8,128)(2,1)S(1)} collective-permute-done((bf16[64,640]{1,0:T(8,128)(2,1)S(1)}, bf16[64,640]{1,0:T(8,128)(2,1)S(1)}, u32[]{:S(2)}, u32[]{:S(2)}) %collective-permute-start.2) | collective-permute-done | bytes 81952 | tf_op jit(solution)/shard_map/ppermute | solution.py:459
  15.3 0.1 collective-permute-done.3.refs_2_
  15.4 0.3 shard_map.69
  15.8 0.1 collective-permute-start.4
  15.8 0.5 %shard_map.70 = (f32[2048,256]{1,0:T(8,128)S(1)}, f32[256,128]{1,0:T(8,128)S(1)}, f32[64,128]{1,0:T(8,128)S(1)}) custom-call(bf16[256,640]{1,0:T(8,128)(2,1)S(1)} %get-tuple-element.53.vp, f32[2048,256]{1,0:T(8,128)S(1)} %get-tuple-element.52.weight, bf16[256,640]{1,0:T(8,128)(2,1)S(1)} %get-tuple-element.51.gp), custom_call_target="tpu_custom_call" | custom-call | bytes 1048576 | tf_op jit(solution)/shard_map/pallas_call | solution.py:509
  16.4 0.0 collective-permute-done.5.refs_1_
  16.4 0.9 %shard_map.71 = (f32[1024,128]{1,0:T(8,128)S(1)}, f32[128,128]{1,0:T(8,128)S(1)}, f32[128,128]{1,0:T(8,128)S(1)}) custom-call(bf16[64,640]{1,0:T(8,128)(2,1)S(1)} %get-tuple-element.45.q_own, bf16[64,640]{1,0:T(8,128)(2,1)S(1)} %collective-permute-done.after.q_other, bf16[128,640]{1,0:T(8,128)(2,1)S(1)} %get-tuple-element.58.refs_0_, ...), custom_call_target="tpu_custom_call" | custom-call | bytes 1048576 | tf_op jit(solution)/shard_map/pallas_call | solution.py:499
  17.3 0.0 collective-permute-done.7.refs_3_
  17.3 0.4 %collective-permute-done.6.refs_2_ = bf16[64,640]{1,0:T(8,128)(2,1)S(1)} collective-permute-done((bf16[64,640]{1,0:T(8,128)(2,1)S(1)}, bf16[64,640]{1,0:T(8,128)(2,1)S(1)}, u32[]{:S(2)}, u32[]{:S(2)}) %collective-permute-start.6) | collective-permute-done | bytes 81952 | tf_op jit(solution)/shard_map/ppermute | solution.py:459
  17.7 0.4 %shard_map.72 = (f32[512,128]{1,0:T(8,128)S(1)}, f32[64,128]{1,0:T(8,128)S(1)}, f32[64,128]{1,0:T(8,128)S(1)}) custom-call(bf16[64,640]{1,0:T(8,128)(2,1)S(1)} %get-tuple-element.45.q_own, bf16[64,640]{1,0:T(8,128)(2,1)S(1)} %collective-permute-done.after.q_other, bf16[128,640]{1,0:T(8,128)(2,1)S(1)} %get-tuple-element.58.refs_0_, ...), custom_call_target="tpu_custom_call" | custom-call | bytes 1048576 | tf_op jit(solution)/shard_map/pallas_call | solution.py:502
  18.2 0.5 %shard_map.73 = (f32[1024,128]{1,0:T(8,128)S(1)}, f32[512,128]{1,0:T(8,128)S(1)}, f32[256,128]{1,0:T(8,128)S(1)}) custom-call(bf16[64,640]{1,0:T(8,128)(2,1)S(1)} %get-tuple-element.57.g_own, bf16[64,640]{1,0:T(8,128)(2,1)S(1)} %collective-permute-done.4.g_other, f32[1024,128]{1,0:T(8,128)S(1)} %get-tuple-element.59.e1, ...), custom_call_target="tpu_custom_call" | custom-call | bytes 1048576 | tf_op jit(solution)/shard_map/pallas_call | solution.py:512
  18.6 0.2 collective-permute-start.8
  18.8 1.3 %collective-permute-done.8.theirs = f32[256,128]{1,0:T(8,128)S(1)} collective-permute-done((f32[256,128]{1,0:T(8,128)S(1)}, f32[256,128]{1,0:T(8,128)S(1)}, u32[]{:S(2)}, u32[]{:S(2)}) %collective-permute-start.8) | collective-permute-done | bytes 131104 | tf_op jit(solution)/shard_map/ppermute | solution.py:459
  20.0 1.6 %shard_map.74 = (f32[64,640]{1,0:T(8,128)S(1)}, bf16[64,640]{1,0:T(8,128)(2,1)S(1)}, f32[64,128]{1,0:T(8,128)S(1)}, f32[64,128]{1,0:T(8,128)S(1)}, f32[128,640]{...) custom-call(bf16[64,640]{1,0:T(8,128)(2,1)S(1)} %get-tuple-element.45.q_own, ...), custom_call_target="tpu_custom_call" | custom-call | bytes 1048576 | tf_op jit(solution)/shard_map/pallas_call | solution.py:517
  21.6 1.6 %collective-permute-start.10 = (bf16[128,640]{1,0:T(8,128)(2,1)S(1)}, bf16[128,640]{1,0:T(8,128)(2,1)S(1)}, u32[]{:S(2)}, u32[]{:S(2)}) collective-permute-start(bf16[128,640]{1,0:T(8,128)(2,1)S(1)} %get-tuple-element.78), channel_id=1, source_target_pairs={{0,8},{4,12},{8,0},{12,4},{16,24},{20,28},{24,16},{28,20},{1,9},{5... | collective-permute-start | bytes 491528 | tf_op jit(solution)/shard_map/ppermute | solution.py:459
  23.2 0.0 collective-permute-start.9
  23.2 1.1 %collective-permute-start.11 = (bf16[64,640]{1,0:T(8,128)(2,1)S(1)}, bf16[64,640]{1,0:T(8,128)(2,1)S(1)}, u32[]{:S(2)}, u32[]{:S(2)}) collective-permute-start(bf16[64,640]{1,0:T(8,128)(2,1)S(1)} %get-tuple-element.79), channel_id=1, source_target_pairs={{0,16},{4,20},{8,24},{12,28},{16,0},{20,4},{24,8},{28,12},{1,17},{... | collective-permute-start | bytes 245768 | tf_op jit(solution)/shard_map/ppermute | solution.py:459
  24.3 0.9 %collective-permute-start.12 = (bf16[64,640]{1,0:T(8,128)(2,1)S(1)}, bf16[64,640]{1,0:T(8,128)(2,1)S(1)}, u32[]{:S(2)}, u32[]{:S(2)}) collective-permute-start(bf16[64,640]{1,0:T(8,128)(2,1)S(1)} %get-tuple-element.80), channel_id=1, source_target_pairs={{0,24},{4,28},{8,16},{12,20},{16,8},{20,12},{24,0},{28,4},{1,25},{... | collective-permute-start | bytes 245768 | tf_op jit(solution)/shard_map/ppermute | solution.py:459
  25.2 0.0 collective-permute-done.9.dq2
  25.2 2.6 %shard_map.75 = (bf16[256,640]{1,0:T(8,128)(2,1)}, f32[256,640]{1,0:T(8,128)S(1)}, f32[256,640]{1,0:T(8,128)S(1)}) custom-call(bf16[256,640]{1,0:T(8,128)(2,1)S(1)} %get-tuple-element.43.qp, bf16[256,640]{1,0:T(8,128)(2,1)S(1)} %get-tuple-element.44.kp, bf16[256,640]{1,0:T(8,128)(2,1)S(1)} %get-tuple-element.51.gp, ...), custom_call_target="tpu_custom_call" | custom-call | bytes 1048576 | tf_op jit(solution)/shard_map/pallas_call | solution.py:528
  27.8 0.3 collective-permute-done.11.refs_1_
  28.0 2.5 %collective-permute-done.12.refs_2_ = bf16[64,640]{1,0:T(8,128)(2,1)S(1)} collective-permute-done((bf16[64,640]{1,0:T(8,128)(2,1)S(1)}, bf16[64,640]{1,0:T(8,128)(2,1)S(1)}, u32[]{:S(2)}, u32[]{:S(2)}) %collective-permute-start.12) | collective-permute-done | bytes 81952 | tf_op jit(solution)/shard_map/ppermute | solution.py:459
  30.6 1.3 %shard_map.76 = (bf16[256,640]{1,0:T(8,128)(2,1)}, bf16[256,640]{1,0:T(8,128)(2,1)}) custom-call(f32[256,640]{1,0:T(8,128)S(1)} %get-tuple-element.75.dk0, f32[256,640]{1,0:T(8,128)S(1)} %get-tuple-element.76.dv0, f32[128,640]{1,0:T(8,128)S(1)} %get-tuple-element.77.own, bf16[128,640]{1,0:T(8,128)(2,1)S(1)} %collective-permute-done.10.refs_0_, ...), custom_call_target="tpu_custom_call" | custom-call | bytes 1048576 | tf_op jit(solution)/shard_map/pallas_call | solution.py:531
  (4 shorter events, 0.0 us)
Async XLA Ops:
  2.6 7.5 %collective-permute-start = (bf16[64,640]{1,0:T(8,128)(2,1)S(1)}, bf16[64,640]{1,0:T(8,128)(2,1)S(1)}, u32[]{:S(2)}, u32[]{:S(2)}) collective-permute-start(bf16[64,640]{1,0:T(8,128)(2,1)S(1)} %get-tuple-element.45.q_own), channel_id=1, source_target_pairs={{0,4},{4,0},{8,12},{12,8},{16,20},{20,16},{24,28},{28,24},{1,5},{5... | collective-permute-start | bytes 245768 | tf_op jit(solution)/shard_map/ppermute | solution.py:459
  3.1 9.4 %collective-permute-start.1 = (bf16[64,640]{1,0:T(8,128)(2,1)S(1)}, bf16[64,640]{1,0:T(8,128)(2,1)S(1)}, u32[]{:S(2)}, u32[]{:S(2)}) collective-permute-start(bf16[64,640]{1,0:T(8,128)(2,1)S(1)} %get-tuple-element.47), channel_id=1, source_target_pairs={{0,3},{1,2},{2,1},{3,0},{4,7},{5,6},{6,5},{7,4},{8,11},{9,10},{10,... | collective-permute-start | bytes 245768 | tf_op jit(solution)/shard_map/ppermute | solution.py:459
  7.8 7.6 %collective-permute-start.2 = (bf16[64,640]{1,0:T(8,128)(2,1)S(1)}, bf16[64,640]{1,0:T(8,128)(2,1)S(1)}, u32[]{:S(2)}, u32[]{:S(2)}) collective-permute-start(bf16[64,640]{1,0:T(8,128)(2,1)S(1)} %get-tuple-element.48), channel_id=1, source_target_pairs={{0,2},{1,3},{2,0},{3,1},{4,6},{5,7},{6,4},{7,5},{8,10},{9,11},{10,... | collective-permute-start | bytes 245768 | tf_op jit(solution)/shard_map/ppermute | solution.py:459
  7.8 8.6 %collective-permute-start.5 = (bf16[128,640]{1,0:T(8,128)(2,1)S(1)}, bf16[128,640]{1,0:T(8,128)(2,1)S(1)}, u32[]{:S(2)}, u32[]{:S(2)}) collective-permute-start(bf16[128,640]{1,0:T(8,128)(2,1)S(1)} %get-tuple-element.58.refs_0_), channel_id=1, source_target_pairs={{0,8},{4,12},{8,0},{12,4},{16,24},{20,28},{24,16},{28,20},{1,9},{5... | collective-permute-start | bytes 491528 | tf_op jit(solution)/shard_map/ppermute | solution.py:459
  9.2 6.2 %collective-permute-start.3 = (bf16[64,640]{1,0:T(8,128)(2,1)S(1)}, bf16[64,640]{1,0:T(8,128)(2,1)S(1)}, u32[]{:S(2)}, u32[]{:S(2)}) collective-permute-start(bf16[64,640]{1,0:T(8,128)(2,1)S(1)} %get-tuple-element.49), channel_id=1, source_target_pairs={{0,1},{1,0},{2,3},{3,2},{4,5},{5,4},{6,7},{7,6},{8,9},{9,8},{10,11... | collective-permute-start | bytes 245768 | tf_op jit(solution)/shard_map/ppermute | solution.py:459
  10.0 7.3 %collective-permute-start.7 = (bf16[64,640]{1,0:T(8,128)(2,1)S(1)}, bf16[64,640]{1,0:T(8,128)(2,1)S(1)}, u32[]{:S(2)}, u32[]{:S(2)}) collective-permute-start(bf16[64,640]{1,0:T(8,128)(2,1)S(1)} %get-tuple-element.60), channel_id=1, source_target_pairs={{0,24},{4,28},{8,16},{12,20},{16,8},{20,12},{24,0},{28,4},{1,25},{... | collective-permute-start | bytes 245768 | tf_op jit(solution)/shard_map/ppermute | solution.py:459
  12.5 5.3 %collective-permute-start.6 = (bf16[64,640]{1,0:T(8,128)(2,1)S(1)}, bf16[64,640]{1,0:T(8,128)(2,1)S(1)}, u32[]{:S(2)}, u32[]{:S(2)}) collective-permute-start(bf16[64,640]{1,0:T(8,128)(2,1)S(1)} %get-tuple-element.60), channel_id=1, source_target_pairs={{0,16},{4,20},{8,24},{12,28},{16,0},{20,4},{24,8},{28,12},{1,17},{... | collective-permute-start | bytes 245768 | tf_op jit(solution)/shard_map/ppermute | solution.py:459
  15.8 2.4 %collective-permute-start.4 = (bf16[64,640]{1,0:T(8,128)(2,1)S(1)}, bf16[64,640]{1,0:T(8,128)(2,1)S(1)}, u32[]{:S(2)}, u32[]{:S(2)}) collective-permute-start(bf16[64,640]{1,0:T(8,128)(2,1)S(1)} %get-tuple-element.57.g_own), channel_id=1, source_target_pairs={{0,4},{4,0},{8,12},{12,8},{16,20},{20,16},{24,28},{28,24},{1,5},{5... | collective-permute-start | bytes 245768 | tf_op jit(solution)/shard_map/ppermute | solution.py:459
  18.6 1.4 %collective-permute-start.8 = (f32[256,128]{1,0:T(8,128)S(1)}, f32[256,128]{1,0:T(8,128)S(1)}, u32[]{:S(2)}, u32[]{:S(2)}) collective-permute-start(f32[256,128]{1,0:T(8,128)S(1)} %get-tuple-element.69.mine), channel_id=1, source_target_pairs={{0,4},{4,0},{8,12},{12,8},{16,20},{20,16},{24,28},{28,24},{1,5},{5... | collective-permute-start | bytes 393224 | tf_op jit(solution)/shard_map/ppermute | solution.py:459
  21.6 9.0 %collective-permute-start.10 = (bf16[128,640]{1,0:T(8,128)(2,1)S(1)}, bf16[128,640]{1,0:T(8,128)(2,1)S(1)}, u32[]{:S(2)}, u32[]{:S(2)}) collective-permute-start(bf16[128,640]{1,0:T(8,128)(2,1)S(1)} %get-tuple-element.78), channel_id=1, source_target_pairs={{0,8},{4,12},{8,0},{12,4},{16,24},{20,28},{24,16},{28,20},{1,9},{5... | collective-permute-start | bytes 491528 | tf_op jit(solution)/shard_map/ppermute | solution.py:459
  23.2 2.0 %collective-permute-start.9 = (bf16[64,640]{1,0:T(8,128)(2,1)S(1)}, bf16[64,640]{1,0:T(8,128)(2,1)S(1)}, u32[]{:S(2)}, u32[]{:S(2)}) collective-permute-start(bf16[64,640]{1,0:T(8,128)(2,1)S(1)} %get-tuple-element.73), channel_id=1, source_target_pairs={{0,4},{4,0},{8,12},{12,8},{16,20},{20,16},{24,28},{28,24},{1,5},{5... | collective-permute-start | bytes 245768 | tf_op jit(solution)/shard_map/ppermute | solution.py:459
  23.2 4.9 %collective-permute-start.11 = (bf16[64,640]{1,0:T(8,128)(2,1)S(1)}, bf16[64,640]{1,0:T(8,128)(2,1)S(1)}, u32[]{:S(2)}, u32[]{:S(2)}) collective-permute-start(bf16[64,640]{1,0:T(8,128)(2,1)S(1)} %get-tuple-element.79), channel_id=1, source_target_pairs={{0,16},{4,20},{8,24},{12,28},{16,0},{20,4},{24,8},{28,12},{1,17},{... | collective-permute-start | bytes 245768 | tf_op jit(solution)/shard_map/ppermute | solution.py:459
  24.3 6.3 %collective-permute-start.12 = (bf16[64,640]{1,0:T(8,128)(2,1)S(1)}, bf16[64,640]{1,0:T(8,128)(2,1)S(1)}, u32[]{:S(2)}, u32[]{:S(2)}) collective-permute-start(bf16[64,640]{1,0:T(8,128)(2,1)S(1)} %get-tuple-element.80), channel_id=1, source_target_pairs={{0,24},{4,28},{8,16},{12,20},{16,8},{20,12},{24,0},{28,4},{1,25},{... | collective-permute-start | bytes 245768 | tf_op jit(solution)/shard_map/ppermute | solution.py:459

commit v5 on v4

v5 whole, which is shorter than its diff:
```python
import functools
import math

import jax
import jax.numpy as jnp
from jax import lax
from jax.experimental import pallas as pl
from jax.experimental.pallas import tpu as pltpu
from jax.sharding import PartitionSpec as P

HD = 80
SPAN1 = 4
DIL1 = 4
WIDEST = 32
LANES = 128
BF16 = jnp.bfloat16
F32 = jnp.float32
SCALE = HD**-0.5
SCALE2 = SCALE * math.log2(math.e)
VMEM_BYTES = 28 * 2**20
LOWEST = -1e30
TINY = 1e-30


class Plan:
    def __init__(self, tokens, width, seq_count, head_count):
        self.tokens = tokens
        self.width = width
        self.heads = width // HD
        self.g1 = SPAN1
        self.g2 = min(WIDEST, seq_count)
        self.r2 = self.g2
        self.n1 = tokens // DIL1
        self.n2 = tokens // self.r2
        self.turns = self.r2 // DIL1
        self.zcount = head_count
        self.rows = [2 * (self.n1 if b < self.g1 else self.n2) for b in range(self.g2)]


def nt(a, b):
    return lax.dot_general(a, b, (((1,), (1,)), ((), ())), preferred_element_type=F32)


def nn(a, b):
    return lax.dot_general(a, b, (((1,), (0,)), ((), ())), preferred_element_type=F32)


def tn(a, b):
    return lax.dot_general(a, b, (((0,), (0,)), ((), ())), preferred_element_type=F32)


def iota(shape, dim):
    return lax.broadcasted_iota(jnp.int32, shape, dim)


def phase_order(p, inverse=False):
    shape = (p.tokens, p.tokens)
    row, col = (iota(shape, 1), iota(shape, 0)) if inverse else (iota(shape, 0), iota(shape, 1))
    return jnp.where(col == p.r2 * (row % p.n2) + row // p.n2, 1.0, 0.0).astype(BF16)


def first_head(p):
    return lax.axis_index("head") * p.heads


def column_class(p):
    return (first_head(p) + iota((1, p.width), 1) // HD) % p.r2


def row_class(p):
    return (first_head(p) + iota((p.heads, 1), 0)) % p.r2


def pick(p, whole, label):
    parts = []
    for t in range(p.turns):
        want = (label + DIL1 * t) % p.r2
        part = jnp.zeros((p.n2, whole.shape[1]), F32)
        for c in range(p.r2):
            part = jnp.where(want == c, whole[c * p.n2 : (c + 1) * p.n2], part)
        parts.append(part)
    return jnp.concatenate(parts, axis=0)


def spread(p, kept, label, base):
    parts = []
    for c in range(p.r2):
        part = base[c * p.n2 : (c + 1) * p.n2]
        for t in range(p.turns):
            hit = (label + DIL1 * t) % p.r2 == c
            part = jnp.where(hit, kept[t * p.n2 : (t + 1) * p.n2], part)
        parts.append(part)
    return jnp.concatenate(parts, axis=0)


def window(h):
    low = h * HD // LANES * LANES
    high = -(-(h + 1) * HD // LANES) * LANES
    return low, high


def window_mask(h, low, high):
    lane = low + iota((1, high - low), 1)
    return (lane >= h * HD) & (lane < (h + 1) * HD)


def head_groups(p):
    groups, h = [], 0
    while h < p.heads:
        low, high = window(h)
        end = h + 1
        while end < p.heads and window(end)[1] - low <= 2 * LANES:
            high = window(end)[1]
            end += 1
        groups.append((h, end, low, high))
        h = end
    return groups


def head_mask(p, h):
    lane = iota((1, p.width), 1)
    return (lane >= h * HD) & (lane < (h + 1) * HD)


def own_bias(p):
    shape = (p.tokens, p.tokens)
    key, query = iota(shape, 0), iota(shape, 1)
    qpos = p.r2 * (query % p.n2) + query // p.n2
    kpos = p.r2 * (key % p.n2) + key // p.n2
    return jnp.where(qpos >= kpos, 0.0, -jnp.inf)


def pick_stat(p, stat, fill):
    lane = iota((1, 2 * p.n1), 1)
    label = row_class(p)
    out = jnp.full((p.heads, 2 * p.n1), fill, F32)
    for t in range(p.turns):
        here = (lane >= t * p.n2) & (lane < (t + 1) * p.n2)
        for c in range(p.r2):
            moved = pltpu.roll(stat, (t - c) * p.n2 % p.tokens, 1)[:, : 2 * p.n1]
            out = jnp.where(here & ((label + DIL1 * t) % p.r2 == c), moved, out)
    return out


def spread_stat(p, kept, base):
    lane = iota((1, p.tokens), 1)
    label = row_class(p)
    padded = jnp.concatenate([kept] * (p.tokens // kept.shape[1]), axis=1)
    out = base
    for t in range(p.turns):
        for c in range(p.r2):
            moved = pltpu.roll(padded, (c - t) * p.n2 % p.tokens, 1)
            here = (lane >= c * p.n2) & (lane < (c + 1) * p.n2)
            out = jnp.where(here & ((label + DIL1 * t) % p.r2 == c), moved, out)
    return out


def by_rows(p, flat):
    count = flat.shape[1] // p.heads
    return jnp.concatenate([flat[:, h * count : (h + 1) * count] for h in range(p.heads)], axis=0)


def along(p, stat):
    return jnp.concatenate([stat[h : h + 1, :] for h in range(p.heads)], axis=1)


def call(kernel, outs, scratch=(), flops=0, **specs):
    return pl.pallas_call(
        kernel,
        out_shape=[jax.ShapeDtypeStruct(s, d) for s, d in outs],
        scratch_shapes=[pltpu.VMEM(*s) if isinstance(s, tuple) else s for s in scratch],
        compiler_params=pltpu.CompilerParams(vmem_limit_bytes=VMEM_BYTES),
        cost_estimate=pl.CostEstimate(flops=flops, bytes_accessed=2**20, transcendentals=0),
        **specs,
    )


def slab(p, g_ref, b):
    start = pl.multiple_of(jnp.bitwise_xor(lax.axis_index("head"), b) * p.width, LANES)
    return g_ref.at[:, pl.ds(start, p.width)]


def pack_kernel(p, q_ref, k_ref, v_ref, g_ref, qp, kp, vp, q1, kv1, kv2, *refs):
    gz, (q_in, k_in, v_in, sems) = refs[: p.zcount], refs[p.zcount :]
    loads = [(k_ref, k_in), (v_ref, v_in), (q_ref, q_in)]
    loads += [(slab(p, g_ref, b), gz[b]) for b in range(p.zcount)]
    copies = [pltpu.make_async_copy(src, dst, sems.at[i]) for i, (src, dst) in enumerate(loads)]
    for copy in copies:
        copy.start()
    order = phase_order(p)
    label = column_class(p)
    copies[0].wait()
    k = nn(order, k_in[...])
    kp[...] = k.astype(BF16)
    k_kept = pick(p, k, label)
    copies[1].wait()
    v = nn(order, v_in[...])
    vp[...] = v.astype(BF16)
    v_kept = pick(p, v, label)
    kv1[...] = jnp.concatenate([k_kept, v_kept], axis=0).astype(BF16)
    kv2[...] = jnp.concatenate([k_kept[: p.n2], v_kept[: p.n2]], axis=0).astype(BF16)
    copies[2].wait()
    q = nn(order, q_in[...])
    qp[...] = q.astype(BF16)
    q1[...] = pick(p, q, label).astype(BF16)
    for copy in copies[3:]:
        copy.wait()


def own_scores_kernel(p, qp, kp, after, weight, lse0, lse01):
    bias = own_bias(p)
    rows = []
    for h in range(p.heads):
        low, high = window(h)
        mask = jnp.where(window_mask(h, low, high), 1.0, 0.0).astype(BF16)
        s = nt(kp[:, low:high], qp[:, low:high] * mask) * SCALE2 + bias
        top = jnp.max(s, axis=0, keepdims=True)
        e = jnp.exp2(s - top)
        denom = jnp.sum(e, axis=0, keepdims=True)
        weight[h * p.tokens : (h + 1) * p.tokens, :] = e * (1.0 / denom)
        rows.append(top + jnp.log2(denom))
    lse = jnp.concatenate(rows, axis=0)
    lse0[...] = lse
    lse01[...] = pick_stat(p, lse, LOWEST)


def gather_kernel(p, after, *refs):
    gz, (gp, g1, natural) = refs[: p.zcount], refs[p.zcount :]
    z = lax.axis_index("head")
    share = p.tokens // p.zcount
    for b in range(p.zcount):
        start = pl.multiple_of(jnp.bitwise_xor(z, b) * share, share)
        natural[pl.ds(start, share), :] = gz[p.zcount - 1 - b][...]
    g = nn(phase_order(p), natural[...])
    gp[...] = g.astype(BF16)
    g1[...] = pick(p, g, column_class(p)).astype(BF16)


def own_delta_kernel(p, vp, weight, gp, dprob, d0, d01):
    sums = []
    for h in range(p.heads):
        low, high = window(h)
        rows = slice(h * p.tokens, (h + 1) * p.tokens)
        mask = jnp.where(window_mask(h, low, high), 1.0, 0.0).astype(BF16)
        dp = nt(vp[:, low:high], gp[:, low:high] * mask)
        dprob[rows, :] = dp
        sums.append(jnp.sum(weight[rows, :] * dp, axis=0, keepdims=True))
    d = jnp.concatenate(sums, axis=0)
    d0[...] = d
    d01[...] = pick_stat(p, d, 0.0)


def cut(p, block, start, count):
    if start % 16 or count % 16:
        block = block.astype(F32)
    return block[start : start + count]


def both_cores(own, other):
    return jnp.concatenate([own[...], other[...]], axis=0)


def by_head(rows, group):
    first, end, low, high = group
    parts = []
    for h in range(first, end):
        mask = jnp.where(window_mask(h, low, high), 1.0, 0.0).astype(BF16)
        parts.append(rows[:, low:high] * mask)
    return jnp.concatenate(parts, axis=0)


def against(p, cols, rows):
    parts = []
    for group in head_groups(p):
        low, high = group[2:]
        parts.append(nt(cols[:, low:high], by_head(rows, group)))
    return jnp.concatenate(parts, axis=1)


def collect(p, weights, rows, out):
    count = rows.shape[0]
    for group in head_groups(p):
        first, end, low, high = group
        part = nn(weights[:, first * count : end * count], by_head(rows, group))
        out[:, low:high] += part


def near_blocks(p, half, kv):
    blocks = [cut(p, ref[...], half * p.n1, p.n1) for ref in kv[: p.g1 // 2]]
    return jnp.concatenate(blocks, axis=0).astype(BF16)


def wide_blocks(p, half, kv):
    blocks = [cut(p, ref[...], half * ref.shape[0] // 2, p.n2) for ref in kv]
    return jnp.concatenate(blocks, axis=0).astype(BF16)


def soft(p, scores, e, tops, sums):
    top = jnp.maximum(jnp.max(scores, axis=0, keepdims=True), LOWEST)
    weight = jnp.exp2(scores - top)
    e[...] = weight
    tops[...] = by_rows(p, top)
    sums[...] = by_rows(p, jnp.sum(weight, axis=0, keepdims=True))


def near_kernel(p, q_own, q_other, *refs):
    kv, outs = refs[: p.g1 // 2], refs[p.g1 // 2 :]
    d = lax.axis_index("seq")
    n1, n2 = p.n1, p.n2
    row = iota((p.g1 // 2 * n1, 1), 0)
    col = iota((1, 2 * p.heads * n1), 1)
    head = first_head(p) + col // (2 * n1)
    own = col % n1
    device = jnp.bitwise_xor(d, col // n1 % 2)
    qpos = p.tokens * device + p.r2 * (own % n2) + (head + DIL1 * (own // n2)) % p.r2
    other = row % n1
    kbase = p.tokens * jnp.bitwise_xor(d, 2 * (row // n1)) + p.r2 * (other % n2)
    kpos = kbase + jnp.bitwise_and(head + DIL1 * (other // n2), p.r2 - 1)
    s = against(p, near_blocks(p, 0, kv), both_cores(q_own, q_other)) * SCALE2
    soft(p, jnp.where(kpos <= qpos, s, -jnp.inf), *outs)


def wide_kernel(p, q_own, q_other, *refs):
    kv, outs = refs[: p.g2 // 2], refs[p.g2 // 2 :]
    d = lax.axis_index("seq")
    n1, n2 = p.n1, p.n2
    row = iota((p.g2 // 2 * n2, 1), 0)
    row = jnp.bitwise_xor(d, 2 * (row // n2)) * n2 + row % n2
    col = iota((1, 2 * p.heads * n1), 1)
    last = jnp.bitwise_xor(d, col // n1 % 2) * n2 + col % n1
    last = jnp.where(col % n1 < n2, last, -1)
    s = against(p, wide_blocks(p, 0, kv), both_cores(q_own, q_other)) * SCALE2
    soft(p, jnp.where(row <= last, s, -jnp.inf), *outs)


def delta_kernel(p, g_own, g_other, e1, e2, top1, sum1, top2, sum2, lse01, d01, *refs):
    kv, (dp1, dp2, stats) = refs[: p.g2 // 2], refs[p.g2 // 2 :]
    g = both_cores(g_own, g_other)
    dp = against(p, near_blocks(p, 1, kv), g)
    dp1[...] = dp
    near = by_rows(p, jnp.sum(e1[...] * dp, axis=0, keepdims=True))
    dp = against(p, wide_blocks(p, 1, kv), g)
    dp2[...] = dp
    wide = by_rows(p, jnp.sum(e2[...] * dp, axis=0, keepdims=True))

    peak = jnp.maximum(top1[...], top2[...])
    up1, up2 = jnp.exp2(top1[...] - peak), jnp.exp2(top2[...] - peak)
    both = jnp.maximum(sum1[...] * up1 + sum2[...] * up2, TINY)
    d = (near * up1 + wide * up2) / both
    total, delta = join(lse01[...], d01[...], peak + jnp.log2(both), d)
    stats[...] = jnp.concatenate([total, delta], axis=0)


def join(lse_a, d_a, lse_b, d_b):
    peak = jnp.maximum(lse_a, lse_b)
    total = peak + jnp.log2(jnp.exp2(lse_a - peak) + jnp.exp2(lse_b - peak))
    return total, jnp.exp2(lse_a - total) * d_a + jnp.exp2(lse_b - total) * d_b


def levels_kernel(
    p, q_own, q_other, g_own, g_other, e1, e2, top1, top2, dp1, dp2, mine, theirs, *refs
):
    ds1, ds2, total1, delta1, own_part = refs[:5]
    outs, (dk1, dv1, dk2, dv2) = refs[5:-4], refs[-4:]
    n1, n2 = p.n1, p.n2
    came = pltpu.roll(theirs[...], n1, 1)
    total, delta = join(mine[: p.heads, :], mine[p.heads :, :], came[: p.heads], came[p.heads :])
    total1[...] = total
    delta1[...] = delta
    delta = along(p, delta)
    q, g = both_cores(q_own, q_other), both_cores(g_own, g_other)
    for ref in (dk1, dv1, dk2, dv2):
        ref[...] = jnp.zeros_like(ref)
    for e, top, dp, kept, dk, dv in ((e1, top1, dp1, ds1, dk1, dv1), (e2, top2, dp2, ds2, dk2, dv2)):
        prob = e[...] * along(p, jnp.exp2(top[...] - total))
        ds = (prob * (dp[...] - delta) * SCALE).astype(BF16)
        kept[...] = ds
        collect(p, prob.astype(BF16), g, dv)
        collect(p, ds, q, dk)
    for i in range(p.g2 // 2):
        rows = slice(i * n2, (i + 1) * n2)
        if 2 * i < p.g1:
            head = slice(i * n1, i * n1 + n2)
            rest = slice(i * n1 + n2, (i + 1) * n1)
            part = []
            for near, wide in ((dk1, dk2), (dv1, dv2)):
                part += [near[head, :] + wide[rows, :], near[rest, :]]
        else:
            part = [dk2[rows, :], dv2[rows, :]]
        part = jnp.concatenate(part, axis=0)
        ref = outs[i - 1] if i else own_part
        ref[...] = part.astype(ref.dtype)


def queries_kernel(p, ds1, ds2, *refs):
    kv, (dq_own, dq_other, dq) = refs[: p.g2 // 2], refs[p.g2 // 2 :]
    k1, k2 = near_blocks(p, 0, kv), wide_blocks(p, 0, kv)
    count = 2 * p.n1
    for first, end, low, high in head_groups(p):
        columns = slice(first * count, end * count)
        part = tn(ds1[:, columns], k1[:, low:high]) + tn(ds2[:, columns], k2[:, low:high])
        for h in range(first, end):
            low_h, high_h = window(h)
            at = (h - first) * count
            piece = part[at : at + count, low_h - low : high_h - low]
            hit = window_mask(h, low_h, high_h)
            dq[:, low_h:high_h] = jnp.where(hit, piece, dq[:, low_h:high_h])
    dq_own[...] = dq[: p.n1, :]
    dq_other[...] = dq[p.n1 :, :].astype(BF16)


def own_grad_kernel(
    p, qp, kp, gp, weight, dprob, lse0, d0, total1, delta1, own_part, dq, dk0, dv0
):
    lse = lse0[...]
    share = jnp.exp2(lse - spread_stat(p, total1[...], lse))
    delta = spread_stat(p, delta1[...], d0[...])
    zero = jnp.zeros((p.tokens, p.width), F32)
    dk0[...] = spread(p, own_part[: p.n1, :], column_class(p), zero)
    dv0[...] = spread(p, own_part[p.n1 :, :], column_class(p), zero)
    for h in range(p.heads):
        low, high = window(h)
        rows = slice(h * p.tokens, (h + 1) * p.tokens)
        hit = window_mask(h, low, high)
        mask = jnp.where(hit, 1.0, 0.0).astype(BF16)
        prob = weight[rows, :] * share[h : h + 1, :]
        ds = (prob * (dprob[rows, :] - delta[h : h + 1, :]) * SCALE).astype(BF16)
        dq[:, low:high] = jnp.where(hit, tn(ds, kp[:, low:high]), dq[:, low:high])
        dk0[:, low:high] += nn(ds, qp[:, low:high] * mask)
        dv0[:, low:high] += nn(prob.astype(BF16), gp[:, low:high] * mask)


def finish_kernel(p, dq, dq_own, dq_came, grad_q):
    kept = dq_own[...] + dq_came[...].astype(F32)
    zero = jnp.zeros((p.tokens, p.width), F32)
    whole = dq[...] + spread(p, kept, column_class(p), zero)
    grad_q[...] = nn(phase_order(p, True), whole.astype(BF16)).astype(BF16)


def last_kernel(p, dk0, dv0, *refs):
    came, (grad_k, grad_v, out_k, out_v, sems) = refs[:-5], refs[-5:]
    order = phase_order(p, True)
    label = column_class(p)
    zero = jnp.zeros((p.tokens, p.width), F32)
    copies = []
    for index, (base, out, grad) in enumerate(((dk0, out_k, grad_k), (dv0, out_v, grad_v))):
        first = jnp.zeros((p.n2, p.width), F32)
        rest = jnp.zeros((p.n1 - p.n2, p.width), F32)
        for ref in came:
            half = ref.shape[0] // 2
            block = ref[...].astype(F32)
            first = first + block[index * half : index * half + p.n2]
            if half == p.n1:
                rest = rest + block[index * half + p.n2 : (index + 1) * half]
        kept = jnp.concatenate([first, rest], axis=0)
        whole = base[...] + spread(p, kept, label, zero)
        out[...] = nn(order, whole.astype(BF16)).astype(BF16)
        copies.append(pltpu.make_async_copy(out, grad, sems.at[index]))
        copies[-1].start()
    for copy in copies:
        copy.wait()


def swap(block, axis, bits):
    count = lax.axis_size(axis)
    return lax.ppermute(block, axis, [(i, i ^ bits) for i in range(count)])


def body(queries, keys, values, grad_out):
    tokens, width = queries.shape
    queries, keys, values, grad_out = (
        pltpu.with_memory_space_constraint(field, pltpu.HBM)
        for field in (queries, keys, values, grad_out)
    )
    p = Plan(tokens, width, lax.axis_size("seq"), lax.axis_size("head"))
    n1, n2 = p.n1, p.n2
    run = lambda kernel: functools.partial(kernel, p)
    row, kept = (tokens, width), (n1, width)
    share = (tokens // p.zcount, width)
    stat, stat1 = (p.heads, tokens), (p.heads, 2 * n1)
    flat = lambda count: (count, tokens)
    even = range(0, p.g2, 2)
    half_rows = sum(p.rows[::2])
    hbm = pl.BlockSpec(memory_space=pltpu.HBM)

    outs = call(
        run(pack_kernel),
        [(row, BF16)] * 3
        + [(kept, BF16), ((2 * n1, width), BF16), ((2 * n2, width), BF16)]
        + [(share, BF16)] * p.zcount,
        [(row, BF16)] * 3 + [pltpu.SemaphoreType.DMA((p.zcount + 3,))],
        in_specs=[hbm] * 4,
    )(queries, keys, values, grad_out)
    qp, kp, vp, q1, kv1, kv2 = outs[:6]
    gz = outs[6:]
    gz = [gz[0]] + [swap(gz[b], "head", b) for b in range(1, p.zcount)]

    kv = [kv1] + [swap(kv1 if b < p.g1 else kv2, "seq", b) for b in even[1:]]

    q_other = swap(q1, "seq", 1)
    weight, lse0, lse01 = call(
        run(own_scores_kernel), [(flat(p.heads * tokens), F32), (stat, F32), (stat1, F32)]
    )(qp, kp, q_other)
    near = (p.g1 // 2 * n1, 2 * p.heads * n1)
    wide = (p.g2 // 2 * n2, 2 * p.heads * n1)
    e1, top1, sum1 = call(run(near_kernel), [(near, F32)] + [(stat1, F32)] * 2)(
        q1, q_other, *kv[: p.g1 // 2]
    )
    e2, top2, sum2 = call(run(wide_kernel), [(wide, F32)] + [(stat1, F32)] * 2)(
        q1, q_other, *kv
    )
    gp, g1 = call(run(gather_kernel), [(row, BF16), (kept, BF16)], [(row, BF16)])(
        lse01, *gz[::-1]
    )
    g_other = swap(g1, "seq", 1)
    dprob, d0, d01 = call(
        run(own_delta_kernel), [(flat(p.heads * tokens), F32), (stat, F32), (stat1, F32)]
    )(vp, weight, gp)
    dp1, dp2, mine = call(
        run(delta_kernel), [(near, F32), (wide, F32), ((2 * p.heads, 2 * n1), F32)]
    )(g1, g_other, e1, e2, top1, sum1, top2, sum2, lse01, d01, *kv)
    theirs = swap(mine, "seq", 1)
    part = lambda b, dtype: ((p.rows[b], width), dtype)
    outs = call(
        run(levels_kernel),
        [(near, BF16), (wide, BF16), (stat1, F32), (stat1, F32), part(0, F32)]
        + [part(b, BF16) for b in even[1:]],
        [((near[0], width), F32)] * 2 + [((wide[0], width), F32)] * 2,
    )(q1, q_other, g1, g_other, e1, e2, top1, top2, dp1, dp2, mine, theirs)
    ds1, ds2, total1, delta1, own_part = outs[:5]
    parts = [swap(s, "seq", b) for s, b in zip(outs[5:], even[1:])]
    dq_own, dq_other = call(
        run(queries_kernel),
        [(kept, F32), (kept, BF16)],
        [((2 * n1, width), F32)],
    )(ds1, ds2, *kv)
    dq_came = swap(dq_other, "seq", 1)
    dq, dk0, dv0 = call(run(own_grad_kernel), [(row, F32)] * 3)(
        qp, kp, gp, weight, dprob, lse0, d0, total1, delta1, own_part
    )
    (grad_q,) = call(run(finish_kernel), [(row, BF16)])(dq, dq_own, dq_came)
    grad_k, grad_v = call(
        run(last_kernel),
        [(row, BF16)] * 2,
        [(row, BF16)] * 2 + [pltpu.SemaphoreType.DMA((2,))],
        out_specs=[hbm] * 2,
    )(dk0, dv0, *parts)
    return grad_q, grad_k, grad_v


def solution(mesh):
    return jax.shard_map(
        body,
        mesh=mesh,
        in_specs=(P("seq", "head"), P("seq", "head"), P("seq", "head"), P(("seq", "head"), None)),
        out_specs=(P("seq", "head"), P("seq", "head"), P("seq", "head")),
        check_vma=False,
    )
```

time: 32 us -> 30.9 us (0.966)
  Pallas kernels: 10.9 us -> 9.98 us
    pallas_call x5 -> x7, Pallas kernels: 5.94 us -> 4.94 us  [the longest x1 1.4 us: body(): call(run(own_grad_kernel), [(row, F32)] * 3)]
  transfers between devices with their start and end apart: 13 -> 13, of which waited for: 6 -> 5; matrix products, arithmetic and copies ran while one was open for 0% -> 0% of each run, Pallas kernels for 18% -> 18%
where the time goes in v5:
time: 30.9 us; the launch traced here: 30.7 us
  starting transfers between devices  13.2 us (43%)
  Pallas kernels  9.98 us (32%)
  waiting for transfers between devices  6.78 us (22%)
  between operations  0.75 us (2%)
    ppermute x13, starting transfers between devices, swap(): return lax.ppermute(block, axis, [(i, i ^ bits) for i in range(count)])  13.2 us
    ppermute x13, waiting for transfers between devices, swap(): return lax.ppermute(block, axis, [(i, i ^ bits) for i in range(count)])  6.78 us
    pallas_call x1, Pallas kernels, body(): call(run(pack_kernel), [(row, BF16)] * 3 + [(kept, BF16), ((2 * n1, width...  1.92 us
    pallas_call x1, Pallas kernels, body(): call(run(own_grad_kernel), [(row, F32)] * 3)  1.4 us
    pallas_call x1, Pallas kernels, body(): call(run(last_kernel), [(row, BF16)] * 2, [(row, BF16)] * 2 + [pltpu.Sema...  1.27 us
    pallas_call x1, Pallas kernels, body(): grad_q, = call(run(finish_kernel), [(row, BF16)])(dq, dq_own, dq_came)  1.06 us
    pallas_call x1, Pallas kernels, body(): call(run(own_scores_kernel), [(flat(p.heads * tokens), F32), (stat, F32),...  0.95 us
    pallas_call x1, Pallas kernels, body(): call(run(levels_kernel), [(near, BF16), (wide, BF16), (stat1, F32), (stat...  0.71 us
  transfers between devices with their start and end apart: 13, of which 5 were waited for; matrix products, arithmetic and copies ran while one was open for 0% of the time, Pallas kernels for 18%

profile of v5, /device:TPU:0, one launch (start us, length us, event | category | flops | bytes accessed | tf_op | source)
XLA Modules:
  0.0 30.7 jit_solution(7231193047797057195)
XLA Ops:
  0.6 1.9 %shard_map.67 = (bf16[256,640]{1,0:T(8,128)(2,1)S(1)}, bf16[256,640]{1,0:T(8,128)(2,1)S(1)}, bf16[256,640]{1,0:T(8,128)(2,1)S(1)}, bf16[64,640]{1,0:T(8,128)(2,1...) custom-call(bf16[256,640]{1,0:T(8,128)(2,1)} %q_ref.1, ...), custom_call_target="tpu_custom_call" | custom-call | bytes 1048576 | tf_op jit(solution)/shard_map/pallas_call | solution.py:486
  2.6 0.5 %collective-permute-start = (bf16[64,640]{1,0:T(8,128)(2,1)S(1)}, bf16[64,640]{1,0:T(8,128)(2,1)S(1)}, u32[]{:S(2)}, u32[]{:S(2)}) collective-permute-start(bf16[64,640]{1,0:T(8,128)(2,1)S(1)} %get-tuple-element.47.q_own), channel_id=1, source_target_pairs={{0,4},{4,0},{8,12},{12,8},{16,20},{20,16},{24,28},{28,24},{1,5},{5... | collective-permute-start | bytes 245768 | tf_op jit(solution)/shard_map/ppermute | solution.py:466
  3.1 4.7 %collective-permute-start.1 = (bf16[64,640]{1,0:T(8,128)(2,1)S(1)}, bf16[64,640]{1,0:T(8,128)(2,1)S(1)}, u32[]{:S(2)}, u32[]{:S(2)}) collective-permute-start(bf16[64,640]{1,0:T(8,128)(2,1)S(1)} %get-tuple-element.49), channel_id=1, source_target_pairs={{0,3},{1,2},{2,1},{3,0},{4,7},{5,6},{6,5},{7,4},{8,11},{9,10},{10,... | collective-permute-start | bytes 245768 | tf_op jit(solution)/shard_map/ppermute | solution.py:466
  7.8 0.0 collective-permute-start.2
  7.8 0.6 %collective-permute-start.3 = (bf16[64,640]{1,0:T(8,128)(2,1)S(1)}, bf16[64,640]{1,0:T(8,128)(2,1)S(1)}, u32[]{:S(2)}, u32[]{:S(2)}) collective-permute-start(bf16[64,640]{1,0:T(8,128)(2,1)S(1)} %get-tuple-element.51), channel_id=1, source_target_pairs={{0,1},{1,0},{2,3},{3,2},{4,5},{5,4},{6,7},{7,6},{8,9},{9,8},{10,11... | collective-permute-start | bytes 245768 | tf_op jit(solution)/shard_map/ppermute | solution.py:466
  8.4 1.6 %collective-permute-start.5 = (bf16[128,640]{1,0:T(8,128)(2,1)S(1)}, bf16[128,640]{1,0:T(8,128)(2,1)S(1)}, u32[]{:S(2)}, u32[]{:S(2)}) collective-permute-start(bf16[128,640]{1,0:T(8,128)(2,1)S(1)} %get-tuple-element.60.refs_0_), channel_id=1, source_target_pairs={{0,8},{4,12},{8,0},{12,4},{16,24},{20,28},{24,16},{28,20},{1,9},{5... | collective-permute-start | bytes 491528 | tf_op jit(solution)/shard_map/ppermute | solution.py:466
  10.0 1.5 %collective-permute-start.7 = (bf16[64,640]{1,0:T(8,128)(2,1)S(1)}, bf16[64,640]{1,0:T(8,128)(2,1)S(1)}, u32[]{:S(2)}, u32[]{:S(2)}) collective-permute-start(bf16[64,640]{1,0:T(8,128)(2,1)S(1)} %get-tuple-element.62), channel_id=1, source_target_pairs={{0,24},{4,28},{8,16},{12,20},{16,8},{20,12},{24,0},{28,4},{1,25},{... | collective-permute-start | bytes 245768 | tf_op jit(solution)/shard_map/ppermute | solution.py:466
  11.5 0.9 %shard_map.68 = (f32[2048,256]{1,0:T(8,128)S(1)}, f32[8,256]{1,0:T(8,128)S(1)}, f32[8,128]{1,0:T(8,128)S(1)}) custom-call(bf16[256,640]{1,0:T(8,128)(2,1)S(1)} %get-tuple-element.45.qp, bf16[256,640]{1,0:T(8,128)(2,1)S(1)} %get-tuple-element.46.kp, bf16[64,640]{1,0:T(8,128)(2,1)S(1)} %collective-permute-done.after.q_other), custom_call_target="tpu_custom_call" | custom-call | bytes 1048576 | tf_op jit(solution)/shard_map/pallas_call | solution.py:501
  12.5 0.0 collective-permute-done.1.refs_0_
  12.5 0.4 %collective-permute-start.6 = (bf16[64,640]{1,0:T(8,128)(2,1)S(1)}, bf16[64,640]{1,0:T(8,128)(2,1)S(1)}, u32[]{:S(2)}, u32[]{:S(2)}) collective-permute-start(bf16[64,640]{1,0:T(8,128)(2,1)S(1)} %get-tuple-element.62), channel_id=1, source_target_pairs={{0,16},{4,20},{8,24},{12,28},{16,0},{20,4},{24,8},{28,12},{1,17},{... | collective-permute-start | bytes 245768 | tf_op jit(solution)/shard_map/ppermute | solution.py:466
  12.9 2.3 %collective-permute-done.2.refs_1_ = bf16[64,640]{1,0:T(8,128)(2,1)S(1)} collective-permute-done((bf16[64,640]{1,0:T(8,128)(2,1)S(1)}, bf16[64,640]{1,0:T(8,128)(2,1)S(1)}, u32[]{:S(2)}, u32[]{:S(2)}) %collective-permute-start.2) | collective-permute-done | bytes 81952 | tf_op jit(solution)/shard_map/ppermute | solution.py:466
  15.2 0.0 collective-permute-done.3.refs_2_
  15.2 0.3 %shard_map.69 = (bf16[256,640]{1,0:T(8,128)(2,1)S(1)}, bf16[64,640]{1,0:T(8,128)(2,1)S(1)}) custom-call(f32[8,128]{1,0:T(8,128)S(1)} %get-tuple-element.48.after.lse01, bf16[64,640]{1,0:T(8,128)(2,1)S(1)} %collective-permute-done.1.refs_0_, bf16[64,640]{1,0:T(8,128)(2,1)S(1)} %collective-permute-done.2.refs_1_, ...), custom_call_target="tpu_custom_call" | custom-call | bytes 1048576 | tf_op jit(solution)/shard_map/pallas_call | solution.py:512
  15.5 0.1 collective-permute-start.4
  15.6 0.6 %shard_map.70 = (f32[2048,256]{1,0:T(8,128)S(1)}, f32[8,256]{1,0:T(8,128)S(1)}, f32[8,128]{1,0:T(8,128)S(1)}) custom-call(bf16[256,640]{1,0:T(8,128)(2,1)S(1)} %get-tuple-element.55.vp, f32[2048,256]{1,0:T(8,128)S(1)} %get-tuple-element.54.weight, bf16[256,640]{1,0:T(8,128)(2,1)S(1)} %get-tuple-element.53.gp), custom_call_target="tpu_custom_call" | custom-call | bytes 1048576 | tf_op jit(solution)/shard_map/pallas_call | solution.py:516
  16.2 0.4 %shard_map.71 = (f32[128,1024]{1,0:T(8,128)S(1)}, f32[8,128]{1,0:T(8,128)S(1)}, f32[8,128]{1,0:T(8,128)S(1)}) custom-call(bf16[64,640]{1,0:T(8,128)(2,1)S(1)} %get-tuple-element.47.q_own, bf16[64,640]{1,0:T(8,128)(2,1)S(1)} %collective-permute-done.after.q_other, bf16[128,640]{1,0:T(8,128)(2,1)S(1)} %get-tuple-element.60.refs_0_, ...), custom_call_target="tpu_custom_call" | custom-call | bytes 1048576 | tf_op jit(solution)/shard_map/pallas_call | solution.py:506
  16.7 0.5 %collective-permute-done.7.refs_3_ = bf16[64,640]{1,0:T(8,128)(2,1)S(1)} collective-permute-done((bf16[64,640]{1,0:T(8,128)(2,1)S(1)}, bf16[64,640]{1,0:T(8,128)(2,1)S(1)}, u32[]{:S(2)}, u32[]{:S(2)}) %collective-permute-start.7) | collective-permute-done | bytes 81952 | tf_op jit(solution)/shard_map/ppermute | solution.py:466
  17.1 0.8 %collective-permute-done.6.refs_2_ = bf16[64,640]{1,0:T(8,128)(2,1)S(1)} collective-permute-done((bf16[64,640]{1,0:T(8,128)(2,1)S(1)}, bf16[64,640]{1,0:T(8,128)(2,1)S(1)}, u32[]{:S(2)}, u32[]{:S(2)}) %collective-permute-start.6) | collective-permute-done | bytes 81952 | tf_op jit(solution)/shard_map/ppermute | solution.py:466
  17.9 0.4 %shard_map.72 = (f32[128,1024]{1,0:T(8,128)S(1)}, f32[8,128]{1,0:T(8,128)S(1)}, f32[8,128]{1,0:T(8,128)S(1)}) custom-call(bf16[64,640]{1,0:T(8,128)(2,1)S(1)} %get-tuple-element.47.q_own, bf16[64,640]{1,0:T(8,128)(2,1)S(1)} %collective-permute-done.after.q_other, bf16[128,640]{1,0:T(8,128)(2,1)S(1)} %get-tuple-element.60.refs_0_, ...), custom_call_target="tpu_custom_call" | custom-call | bytes 1048576 | tf_op jit(solution)/shard_map/pallas_call | solution.py:509
  18.3 0.5 %shard_map.73 = (f32[128,1024]{1,0:T(8,128)S(1)}, f32[128,1024]{1,0:T(8,128)S(1)}, f32[16,128]{1,0:T(8,128)S(1)}) custom-call(bf16[64,640]{1,0:T(8,128)(2,1)S(1)} %get-tuple-element.59.g_own, bf16[64,640]{1,0:T(8,128)(2,1)S(1)} %collective-permute-done.4.g_other, f32[128,1024]{1,0:T(8,128)S(1)} %get-tuple-element.61.e1, ...), custom_call_target="tpu_custom_call" | custom-call | bytes 1048576 | tf_op jit(solution)/shard_map/pallas_call | solution.py:519
  18.8 0.1 collective-permute-start.8
  18.8 1.2 %collective-permute-done.8.theirs = f32[16,128]{1,0:T(8,128)S(1)} collective-permute-done((f32[16,128]{1,0:T(8,128)S(1)}, f32[16,128]{1,0:T(8,128)S(1)}, u32[]{:S(2)}, u32[]{:S(2)}) %collective-permute-start.8) | collective-permute-done | bytes 8224 | tf_op jit(solution)/shard_map/ppermute | solution.py:466
  20.0 0.7 %shard_map.74 = (bf16[128,1024]{1,0:T(8,128)(2,1)S(1)}, bf16[128,1024]{1,0:T(8,128)(2,1)S(1)}, f32[8,128]{1,0:T(8,128)S(1)}, f32[8,128]{1,0:T(8,128)S(1)}, f32[1...) custom-call(bf16[64,640]{1,0:T(8,128)(2,1)S(1)} %get-tuple-element.4, ...), custom_call_target="tpu_custom_call" | custom-call | bytes 1048576 | tf_op jit(solution)/shard_map/pallas_call | solution.py:524
  20.7 1.6 %collective-permute-start.10 = (bf16[128,640]{1,0:T(8,128)(2,1)S(1)}, bf16[128,640]{1,0:T(8,128)(2,1)S(1)}, u32[]{:S(2)}, u32[]{:S(2)}) collective-permute-start(bf16[128,640]{1,0:T(8,128)(2,1)S(1)} %get-tuple-element.82), channel_id=1, source_target_pairs={{0,8},{4,12},{8,0},{12,4},{16,24},{20,28},{24,16},{28,20},{1,9},{5... | collective-permute-start | bytes 491528 | tf_op jit(solution)/shard_map/ppermute | solution.py:466
  22.3 0.5 %shard_map.76 = (f32[64,640]{1,0:T(8,128)S(1)}, bf16[64,640]{1,0:T(8,128)(2,1)S(1)}) custom-call(bf16[128,1024]{1,0:T(8,128)(2,1)S(1)} %get-tuple-element.76.ds1, bf16[128,1024]{1,0:T(8,128)(2,1)S(1)} %get-tuple-element.77.ds2, bf16[128,640]{1,0:T(8,128)(2,1)S(1)} %get-tuple-element.60.refs_0_, bf16[128,640]{1,0:T(8,128)(2,1)S(1)} %collective-permute-done.5.refs_1_, ...), custom_call_target="tpu_custom_call" | custom-call | bytes 1048576 | tf_op jit(solution)/shard_map/pallas_call | solution.py:532
  22.8 0.1 collective-permute-start.9
  22.8 0.6 %collective-permute-start.11 = (bf16[64,640]{1,0:T(8,128)(2,1)S(1)}, bf16[64,640]{1,0:T(8,128)(2,1)S(1)}, u32[]{:S(2)}, u32[]{:S(2)}) collective-permute-start(bf16[64,640]{1,0:T(8,128)(2,1)S(1)} %get-tuple-element.83), channel_id=1, source_target_pairs={{0,16},{4,20},{8,24},{12,28},{16,0},{20,4},{24,8},{28,12},{1,17},{... | collective-permute-start | bytes 245768 | tf_op jit(solution)/shard_map/ppermute | solution.py:466
  23.4 1.5 %collective-permute-start.12 = (bf16[64,640]{1,0:T(8,128)(2,1)S(1)}, bf16[64,640]{1,0:T(8,128)(2,1)S(1)}, u32[]{:S(2)}, u32[]{:S(2)}) collective-permute-start(bf16[64,640]{1,0:T(8,128)(2,1)S(1)} %get-tuple-element.84), channel_id=1, source_target_pairs={{0,24},{4,28},{8,16},{12,20},{16,8},{20,12},{24,0},{28,4},{1,25},{... | collective-permute-start | bytes 245768 | tf_op jit(solution)/shard_map/ppermute | solution.py:466
  24.9 1.4 %shard_map.75 = (f32[256,640]{1,0:T(8,128)S(1)}, f32[256,640]{1,0:T(8,128)S(1)}, f32[256,640]{1,0:T(8,128)S(1)}) custom-call(bf16[256,640]{1,0:T(8,128)(2,1)S(1)} %get-tuple-element.45.qp, bf16[256,640]{1,0:T(8,128)(2,1)S(1)} %get-tuple-element.46.kp, bf16[256,640]{1,0:T(8,128)(2,1)S(1)} %get-tuple-element.53.gp, f32[2048,256]{1,0:T(8,128)S(1)} %get-tuple-element.54.weight, ...), custom_call_target="tpu_custom_call" | custom-call | bytes 1048576 | tf_op jit(solution)/shard_map/pallas_call | solution.py:538
  26.3 1.1 %shard_map.77 = bf16[256,640]{1,0:T(8,128)(2,1)} custom-call(f32[256,640]{1,0:T(8,128)S(1)} %get-tuple-element.75.dq, f32[64,640]{1,0:T(8,128)S(1)} %get-tuple-element.78.dq_own, bf16[64,640]{1,0:T(8,128)(2,1)S(1)} %collective-permute-done.9.dq_came), custom_call_target="tpu_custom_call" | custom-call | bytes 1048576 | tf_op jit(solution)/shard_map/pallas_call | solution.py:541
  27.4 2.1 %collective-permute-done.11.refs_1_ = bf16[64,640]{1,0:T(8,128)(2,1)S(1)} collective-permute-done((bf16[64,640]{1,0:T(8,128)(2,1)S(1)}, bf16[64,640]{1,0:T(8,128)(2,1)S(1)}, u32[]{:S(2)}, u32[]{:S(2)}) %collective-permute-start.11) | collective-permute-done | bytes 81952 | tf_op jit(solution)/shard_map/ppermute | solution.py:466
  29.5 1.3 %shard_map.78 = (bf16[256,640]{1,0:T(8,128)(2,1)}, bf16[256,640]{1,0:T(8,128)(2,1)}) custom-call(f32[256,640]{1,0:T(8,128)S(1)} %get-tuple-element.80.dk0, f32[256,640]{1,0:T(8,128)S(1)} %get-tuple-element.81.dv0, bf16[128,640]{1,0:T(8,128)(2,1)S(1)} %collective-permute-done.10.refs_0_, bf16[64,640]{1,0:T(8,128)(2,1)S(1)} %collective-permute-done.11.refs_1_, ...), custom_call_target="tpu_custom_call" | custom-call | bytes 1048576 | tf_op jit(solution)/shard_map/pallas_call | solution.py:542
  (6 shorter events, 0.0 us)
Async XLA Ops:
  2.6 7.5 %collective-permute-start = (bf16[64,640]{1,0:T(8,128)(2,1)S(1)}, bf16[64,640]{1,0:T(8,128)(2,1)S(1)}, u32[]{:S(2)}, u32[]{:S(2)}) collective-permute-start(bf16[64,640]{1,0:T(8,128)(2,1)S(1)} %get-tuple-element.47.q_own), channel_id=1, source_target_pairs={{0,4},{4,0},{8,12},{12,8},{16,20},{20,16},{24,28},{28,24},{1,5},{5... | collective-permute-start | bytes 245768 | tf_op jit(solution)/shard_map/ppermute | solution.py:466
  3.1 9.4 %collective-permute-start.1 = (bf16[64,640]{1,0:T(8,128)(2,1)S(1)}, bf16[64,640]{1,0:T(8,128)(2,1)S(1)}, u32[]{:S(2)}, u32[]{:S(2)}) collective-permute-start(bf16[64,640]{1,0:T(8,128)(2,1)S(1)} %get-tuple-element.49), channel_id=1, source_target_pairs={{0,3},{1,2},{2,1},{3,0},{4,7},{5,6},{6,5},{7,4},{8,11},{9,10},{10,... | collective-permute-start | bytes 245768 | tf_op jit(solution)/shard_map/ppermute | solution.py:466
  7.8 7.5 %collective-permute-start.2 = (bf16[64,640]{1,0:T(8,128)(2,1)S(1)}, bf16[64,640]{1,0:T(8,128)(2,1)S(1)}, u32[]{:S(2)}, u32[]{:S(2)}) collective-permute-start(bf16[64,640]{1,0:T(8,128)(2,1)S(1)} %get-tuple-element.50), channel_id=1, source_target_pairs={{0,2},{1,3},{2,0},{3,1},{4,6},{5,7},{6,4},{7,5},{8,10},{9,11},{10,... | collective-permute-start | bytes 245768 | tf_op jit(solution)/shard_map/ppermute | solution.py:466
  7.8 7.5 %collective-permute-start.3 = (bf16[64,640]{1,0:T(8,128)(2,1)S(1)}, bf16[64,640]{1,0:T(8,128)(2,1)S(1)}, u32[]{:S(2)}, u32[]{:S(2)}) collective-permute-start(bf16[64,640]{1,0:T(8,128)(2,1)S(1)} %get-tuple-element.51), channel_id=1, source_target_pairs={{0,1},{1,0},{2,3},{3,2},{4,5},{5,4},{6,7},{7,6},{8,9},{9,8},{10,11... | collective-permute-start | bytes 245768 | tf_op jit(solution)/shard_map/ppermute | solution.py:466
  8.4 7.8 %collective-permute-start.5 = (bf16[128,640]{1,0:T(8,128)(2,1)S(1)}, bf16[128,640]{1,0:T(8,128)(2,1)S(1)}, u32[]{:S(2)}, u32[]{:S(2)}) collective-permute-start(bf16[128,640]{1,0:T(8,128)(2,1)S(1)} %get-tuple-element.60.refs_0_), channel_id=1, source_target_pairs={{0,8},{4,12},{8,0},{12,4},{16,24},{20,28},{24,16},{28,20},{1,9},{5... | collective-permute-start | bytes 491528 | tf_op jit(solution)/shard_map/ppermute | solution.py:466
  10.0 7.1 %collective-permute-start.7 = (bf16[64,640]{1,0:T(8,128)(2,1)S(1)}, bf16[64,640]{1,0:T(8,128)(2,1)S(1)}, u32[]{:S(2)}, u32[]{:S(2)}) collective-permute-start(bf16[64,640]{1,0:T(8,128)(2,1)S(1)} %get-tuple-element.62), channel_id=1, source_target_pairs={{0,24},{4,28},{8,16},{12,20},{16,8},{20,12},{24,0},{28,4},{1,25},{... | collective-permute-start | bytes 245768 | tf_op jit(solution)/shard_map/ppermute | solution.py:466
  12.5 5.4 %collective-permute-start.6 = (bf16[64,640]{1,0:T(8,128)(2,1)S(1)}, bf16[64,640]{1,0:T(8,128)(2,1)S(1)}, u32[]{:S(2)}, u32[]{:S(2)}) collective-permute-start(bf16[64,640]{1,0:T(8,128)(2,1)S(1)} %get-tuple-element.62), channel_id=1, source_target_pairs={{0,16},{4,20},{8,24},{12,28},{16,0},{20,4},{24,8},{28,12},{1,17},{... | collective-permute-start | bytes 245768 | tf_op jit(solution)/shard_map/ppermute | solution.py:466
  15.5 2.7 %collective-permute-start.4 = (bf16[64,640]{1,0:T(8,128)(2,1)S(1)}, bf16[64,640]{1,0:T(8,128)(2,1)S(1)}, u32[]{:S(2)}, u32[]{:S(2)}) collective-permute-start(bf16[64,640]{1,0:T(8,128)(2,1)S(1)} %get-tuple-element.59.g_own), channel_id=1, source_target_pairs={{0,4},{4,0},{8,12},{12,8},{16,20},{20,16},{24,28},{28,24},{1,5},{5... | collective-permute-start | bytes 245768 | tf_op jit(solution)/shard_map/ppermute | solution.py:466
  18.8 1.2 %collective-permute-start.8 = (f32[16,128]{1,0:T(8,128)S(1)}, f32[16,128]{1,0:T(8,128)S(1)}, u32[]{:S(2)}, u32[]{:S(2)}) collective-permute-start(f32[16,128]{1,0:T(8,128)S(1)} %get-tuple-element.71.mine), channel_id=1, source_target_pairs={{0,4},{4,0},{8,12},{12,8},{16,20},{20,16},{24,28},{28,24},{1,5},{5... | collective-permute-start | bytes 24584 | tf_op jit(solution)/shard_map/ppermute | solution.py:466
  20.7 8.7 %collective-permute-start.10 = (bf16[128,640]{1,0:T(8,128)(2,1)S(1)}, bf16[128,640]{1,0:T(8,128)(2,1)S(1)}, u32[]{:S(2)}, u32[]{:S(2)}) collective-permute-start(bf16[128,640]{1,0:T(8,128)(2,1)S(1)} %get-tuple-element.82), channel_id=1, source_target_pairs={{0,8},{4,12},{8,0},{12,4},{16,24},{20,28},{24,16},{28,20},{1,9},{5... | collective-permute-start | bytes 491528 | tf_op jit(solution)/shard_map/ppermute | solution.py:466
  22.8 3.5 %collective-permute-start.9 = (bf16[64,640]{1,0:T(8,128)(2,1)S(1)}, bf16[64,640]{1,0:T(8,128)(2,1)S(1)}, u32[]{:S(2)}, u32[]{:S(2)}) collective-permute-start(bf16[64,640]{1,0:T(8,128)(2,1)S(1)} %get-tuple-element.79), channel_id=1, source_target_pairs={{0,4},{4,0},{8,12},{12,8},{16,20},{20,16},{24,28},{28,24},{1,5},{5... | collective-permute-start | bytes 245768 | tf_op jit(solution)/shard_map/ppermute | solution.py:466
  22.8 6.6 %collective-permute-start.11 = (bf16[64,640]{1,0:T(8,128)(2,1)S(1)}, bf16[64,640]{1,0:T(8,128)(2,1)S(1)}, u32[]{:S(2)}, u32[]{:S(2)}) collective-permute-start(bf16[64,640]{1,0:T(8,128)(2,1)S(1)} %get-tuple-element.83), channel_id=1, source_target_pairs={{0,16},{4,20},{8,24},{12,28},{16,0},{20,4},{24,8},{28,12},{1,17},{... | collective-permute-start | bytes 245768 | tf_op jit(solution)/shard_map/ppermute | solution.py:466
  23.4 6.1 %collective-permute-start.12 = (bf16[64,640]{1,0:T(8,128)(2,1)S(1)}, bf16[64,640]{1,0:T(8,128)(2,1)S(1)}, u32[]{:S(2)}, u32[]{:S(2)}) collective-permute-start(bf16[64,640]{1,0:T(8,128)(2,1)S(1)} %get-tuple-element.84), channel_id=1, source_target_pairs={{0,24},{4,28},{8,16},{12,20},{16,8},{20,12},{24,0},{28,4},{1,25},{... | collective-permute-start | bytes 245768 | tf_op jit(solution)/shard_map/ppermute | solution.py:466

commit v6 on v5

--- a/solution.py
+++ b/solution.py
@@ -393,7 +393,7 @@
 
 
 def queries_kernel(p, ds1, ds2, *refs):
-    kv, (dq_own, dq_other, dq) = refs[: p.g2 // 2], refs[p.g2 // 2 :]
+    kv, (dq_own, dq_low, dq_high, dq) = refs[: p.g2 // 2], refs[p.g2 // 2 :]
     k1, k2 = near_blocks(p, 0, kv), wide_blocks(p, 0, kv)
     count = 2 * p.n1
     for first, end, low, high in head_groups(p):
@@ -406,7 +406,9 @@
             hit = window_mask(h, low_h, high_h)
             dq[:, low_h:high_h] = jnp.where(hit, piece, dq[:, low_h:high_h])
     dq_own[...] = dq[: p.n1, :]
-    dq_other[...] = dq[p.n1 :, :].astype(BF16)
+    half = p.n1 // 2
+    dq_low[...] = dq[p.n1 : p.n1 + half, :].astype(BF16)
+    dq_high[...] = dq[p.n1 + half :, :].astype(BF16)
 
 
 def own_grad_kernel(
@@ -430,8 +432,8 @@
         dv0[:, low:high] += nn(prob.astype(BF16), gp[:, low:high] * mask)
 
 
-def finish_kernel(p, dq, dq_own, dq_came, grad_q):
-    kept = dq_own[...] + dq_came[...].astype(F32)
+def finish_kernel(p, dq, dq_own, dq_low, dq_high, grad_q):
+    kept = dq_own[...] + both_cores(dq_low, dq_high).astype(F32)
     zero = jnp.zeros((p.tokens, p.width), F32)
     whole = dq[...] + spread(p, kept, column_class(p), zero)
     grad_q[...] = nn(phase_order(p, True), whole.astype(BF16)).astype(BF16)
@@ -529,16 +531,16 @@
     )(q1, q_other, g1, g_other, e1, e2, top1, top2, dp1, dp2, mine, theirs)
     ds1, ds2, total1, delta1, own_part = outs[:5]
     parts = [swap(s, "seq", b) for s, b in zip(outs[5:], even[1:])]
-    dq_own, dq_other = call(
+    dq_own, *dq_other = call(
         run(queries_kernel),
-        [(kept, F32), (kept, BF16)],
+        [(kept, F32)] + [((n1 // 2, width), BF16)] * 2,
         [((2 * n1, width), F32)],
     )(ds1, ds2, *kv)
-    dq_came = swap(dq_other, "seq", 1)
+    dq_came = [swap(half, "seq", 1) for half in dq_other]
     dq, dk0, dv0 = call(run(own_grad_kernel), [(row, F32)] * 3)(
         qp, kp, gp, weight, dprob, lse0, d0, total1, delta1, own_part
     )
-    (grad_q,) = call(run(finish_kernel), [(row, BF16)])(dq, dq_own, dq_came)
+    (grad_q,) = call(run(finish_kernel), [(row, BF16)])(dq, dq_own, *dq_came)
     grad_k, grad_v = call(
         run(last_kernel),
         [(row, BF16)] * 2,

time: 30.9 us -> 30.3 us (0.981)
  waiting for transfers between devices: 6.78 us -> 5.79 us
  starting transfers between devices: 13.2 us -> 13.7 us
    ppermute x13 -> x14, waiting for transfers between devices: 6.78 us -> 5.79 us  [swap(): return lax.ppermute(block, axis, [(i, i ^ bits) for i in range(count)])]
    ppermute x13 -> x14, starting transfers between devices: 13.2 us -> 13.7 us  [swap(): return lax.ppermute(block, axis, [(i, i ^ bits) for i in range(count)])]
  transfers between devices with their start and end apart: 13 -> 14, of which waited for: 5 -> 5; matrix products, arithmetic and copies ran while one was open for 0% -> 0% of each run, Pallas kernels for 18% -> 19%
where the time goes in v6:
time: 30.3 us; the launch traced here: 30.2 us
  starting transfers between devices  13.7 us (45%)
  Pallas kernels  9.97 us (33%)
  waiting for transfers between devices  5.79 us (19%)
  between operations  0.76 us (3%)
    ppermute x14, starting transfers between devices, swap(): return lax.ppermute(block, axis, [(i, i ^ bits) for i in range(count)])  13.7 us
    ppermute x14, waiting for transfers between devices, swap(): return lax.ppermute(block, axis, [(i, i ^ bits) for i in range(count)])  5.79 us
    pallas_call x1, Pallas kernels, body(): call(run(pack_kernel), [(row, BF16)] * 3 + [(kept, BF16), ((2 * n1, width...  1.92 us
    pallas_call x1, Pallas kernels, body(): call(run(own_grad_kernel), [(row, F32)] * 3)  1.4 us
    pallas_call x1, Pallas kernels, body(): call(run(last_kernel), [(row, BF16)] * 2, [(row, BF16)] * 2 + [pltpu.Sema...  1.27 us
    pallas_call x1, Pallas kernels, body(): grad_q, = call(run(finish_kernel), [(row, BF16)])(dq, dq_own, *dq_came)  1.06 us
    pallas_call x1, Pallas kernels, body(): call(run(own_scores_kernel), [(flat(p.heads * tokens), F32), (stat, F32),...  0.95 us
    pallas_call x1, Pallas kernels, body(): call(run(levels_kernel), [(near, BF16), (wide, BF16), (stat1, F32), (stat...  0.71 us
  transfers between devices with their start and end apart: 14, of which 5 were waited for; matrix products, arithmetic and copies ran while one was open for 0% of the time, Pallas kernels for 19%

profile of v6, /device:TPU:0, one launch (start us, length us, event | category | flops | bytes accessed | tf_op | source)
XLA Modules:
  0.0 30.2 jit_solution(4179244078775893642)
XLA Ops:
  0.6 1.9 %shard_map.67 = (bf16[256,640]{1,0:T(8,128)(2,1)S(1)}, bf16[256,640]{1,0:T(8,128)(2,1)S(1)}, bf16[256,640]{1,0:T(8,128)(2,1)S(1)}, bf16[64,640]{1,0:T(8,128)(2,1...) custom-call(bf16[256,640]{1,0:T(8,128)(2,1)} %q_ref.1, ...), custom_call_target="tpu_custom_call" | custom-call | bytes 1048576 | tf_op jit(solution)/shard_map/pallas_call | solution.py:488
  2.6 0.5 %collective-permute-start = (bf16[64,640]{1,0:T(8,128)(2,1)S(1)}, bf16[64,640]{1,0:T(8,128)(2,1)S(1)}, u32[]{:S(2)}, u32[]{:S(2)}) collective-permute-start(bf16[64,640]{1,0:T(8,128)(2,1)S(1)} %get-tuple-element.48.q_own), channel_id=1, source_target_pairs={{0,4},{4,0},{8,12},{12,8},{16,20},{20,16},{24,28},{28,24},{1,5},{5... | collective-permute-start | bytes 245768 | tf_op jit(solution)/shard_map/ppermute | solution.py:468
  3.1 4.7 %collective-permute-start.1 = (bf16[64,640]{1,0:T(8,128)(2,1)S(1)}, bf16[64,640]{1,0:T(8,128)(2,1)S(1)}, u32[]{:S(2)}, u32[]{:S(2)}) collective-permute-start(bf16[64,640]{1,0:T(8,128)(2,1)S(1)} %get-tuple-element.50), channel_id=1, source_target_pairs={{0,3},{1,2},{2,1},{3,0},{4,7},{5,6},{6,5},{7,4},{8,11},{9,10},{10,... | collective-permute-start | bytes 245768 | tf_op jit(solution)/shard_map/ppermute | solution.py:468
  7.8 0.6 %collective-permute-start.3 = (bf16[64,640]{1,0:T(8,128)(2,1)S(1)}, bf16[64,640]{1,0:T(8,128)(2,1)S(1)}, u32[]{:S(2)}, u32[]{:S(2)}) collective-permute-start(bf16[64,640]{1,0:T(8,128)(2,1)S(1)} %get-tuple-element.52), channel_id=1, source_target_pairs={{0,1},{1,0},{2,3},{3,2},{4,5},{5,4},{6,7},{7,6},{8,9},{9,8},{10,11... | collective-permute-start | bytes 245768 | tf_op jit(solution)/shard_map/ppermute | solution.py:468
  8.4 1.6 %collective-permute-start.5 = (bf16[128,640]{1,0:T(8,128)(2,1)S(1)}, bf16[128,640]{1,0:T(8,128)(2,1)S(1)}, u32[]{:S(2)}, u32[]{:S(2)}) collective-permute-start(bf16[128,640]{1,0:T(8,128)(2,1)S(1)} %get-tuple-element.61.refs_0_), channel_id=1, source_target_pairs={{0,8},{4,12},{8,0},{12,4},{16,24},{20,28},{24,16},{28,20},{1,9},{5... | collective-permute-start | bytes 491528 | tf_op jit(solution)/shard_map/ppermute | solution.py:468
  10.0 0.0 collective-permute-done.after.q_other
  10.0 1.5 %collective-permute-start.7 = (bf16[64,640]{1,0:T(8,128)(2,1)S(1)}, bf16[64,640]{1,0:T(8,128)(2,1)S(1)}, u32[]{:S(2)}, u32[]{:S(2)}) collective-permute-start(bf16[64,640]{1,0:T(8,128)(2,1)S(1)} %get-tuple-element.63), channel_id=1, source_target_pairs={{0,24},{4,28},{8,16},{12,20},{16,8},{20,12},{24,0},{28,4},{1,25},{... | collective-permute-start | bytes 245768 | tf_op jit(solution)/shard_map/ppermute | solution.py:468
  11.5 0.9 %shard_map.68 = (f32[2048,256]{1,0:T(8,128)S(1)}, f32[8,256]{1,0:T(8,128)S(1)}, f32[8,128]{1,0:T(8,128)S(1)}) custom-call(bf16[256,640]{1,0:T(8,128)(2,1)S(1)} %get-tuple-element.46.qp, bf16[256,640]{1,0:T(8,128)(2,1)S(1)} %get-tuple-element.47.kp, bf16[64,640]{1,0:T(8,128)(2,1)S(1)} %collective-permute-done.after.q_other), custom_call_target="tpu_custom_call" | custom-call | bytes 1048576 | tf_op jit(solution)/shard_map/pallas_call | solution.py:503
  12.5 0.4 %collective-permute-start.6 = (bf16[64,640]{1,0:T(8,128)(2,1)S(1)}, bf16[64,640]{1,0:T(8,128)(2,1)S(1)}, u32[]{:S(2)}, u32[]{:S(2)}) collective-permute-start(bf16[64,640]{1,0:T(8,128)(2,1)S(1)} %get-tuple-element.63), channel_id=1, source_target_pairs={{0,16},{4,20},{8,24},{12,28},{16,0},{20,4},{24,8},{28,12},{1,17},{... | collective-permute-start | bytes 245768 | tf_op jit(solution)/shard_map/ppermute | solution.py:468
  12.9 2.3 %collective-permute-done.2.refs_1_ = bf16[64,640]{1,0:T(8,128)(2,1)S(1)} collective-permute-done((bf16[64,640]{1,0:T(8,128)(2,1)S(1)}, bf16[64,640]{1,0:T(8,128)(2,1)S(1)}, u32[]{:S(2)}, u32[]{:S(2)}) %collective-permute-start.2) | collective-permute-done | bytes 81952 | tf_op jit(solution)/shard_map/ppermute | solution.py:468
  15.2 0.3 %shard_map.69 = (bf16[256,640]{1,0:T(8,128)(2,1)S(1)}, bf16[64,640]{1,0:T(8,128)(2,1)S(1)}) custom-call(f32[8,128]{1,0:T(8,128)S(1)} %get-tuple-element.49.after.lse01, bf16[64,640]{1,0:T(8,128)(2,1)S(1)} %collective-permute-done.1.refs_0_, bf16[64,640]{1,0:T(8,128)(2,1)S(1)} %collective-permute-done.2.refs_1_, ...), custom_call_target="tpu_custom_call" | custom-call | bytes 1048576 | tf_op jit(solution)/shard_map/pallas_call | solution.py:514
  15.5 0.1 collective-permute-start.4
  15.6 0.6 %shard_map.70 = (f32[2048,256]{1,0:T(8,128)S(1)}, f32[8,256]{1,0:T(8,128)S(1)}, f32[8,128]{1,0:T(8,128)S(1)}) custom-call(bf16[256,640]{1,0:T(8,128)(2,1)S(1)} %get-tuple-element.56.vp, f32[2048,256]{1,0:T(8,128)S(1)} %get-tuple-element.55.weight, bf16[256,640]{1,0:T(8,128)(2,1)S(1)} %get-tuple-element.54.gp), custom_call_target="tpu_custom_call" | custom-call | bytes 1048576 | tf_op jit(solution)/shard_map/pallas_call | solution.py:518
  16.2 0.0 collective-permute-done.5.refs_1_
  16.2 0.4 %shard_map.71 = (f32[128,1024]{1,0:T(8,128)S(1)}, f32[8,128]{1,0:T(8,128)S(1)}, f32[8,128]{1,0:T(8,128)S(1)}) custom-call(bf16[64,640]{1,0:T(8,128)(2,1)S(1)} %get-tuple-element.48.q_own, bf16[64,640]{1,0:T(8,128)(2,1)S(1)} %collective-permute-done.after.q_other, bf16[128,640]{1,0:T(8,128)(2,1)S(1)} %get-tuple-element.61.refs_0_, ...), custom_call_target="tpu_custom_call" | custom-call | bytes 1048576 | tf_op jit(solution)/shard_map/pallas_call | solution.py:508
  16.7 0.5 %collective-permute-done.7.refs_3_ = bf16[64,640]{1,0:T(8,128)(2,1)S(1)} collective-permute-done((bf16[64,640]{1,0:T(8,128)(2,1)S(1)}, bf16[64,640]{1,0:T(8,128)(2,1)S(1)}, u32[]{:S(2)}, u32[]{:S(2)}) %collective-permute-start.7) | collective-permute-done | bytes 81952 | tf_op jit(solution)/shard_map/ppermute | solution.py:468
  17.1 0.8 %collective-permute-done.6.refs_2_ = bf16[64,640]{1,0:T(8,128)(2,1)S(1)} collective-permute-done((bf16[64,640]{1,0:T(8,128)(2,1)S(1)}, bf16[64,640]{1,0:T(8,128)(2,1)S(1)}, u32[]{:S(2)}, u32[]{:S(2)}) %collective-permute-start.6) | collective-permute-done | bytes 81952 | tf_op jit(solution)/shard_map/ppermute | solution.py:468
  17.9 0.4 %shard_map.72 = (f32[128,1024]{1,0:T(8,128)S(1)}, f32[8,128]{1,0:T(8,128)S(1)}, f32[8,128]{1,0:T(8,128)S(1)}) custom-call(bf16[64,640]{1,0:T(8,128)(2,1)S(1)} %get-tuple-element.48.q_own, bf16[64,640]{1,0:T(8,128)(2,1)S(1)} %collective-permute-done.after.q_other, bf16[128,640]{1,0:T(8,128)(2,1)S(1)} %get-tuple-element.61.refs_0_, ...), custom_call_target="tpu_custom_call" | custom-call | bytes 1048576 | tf_op jit(solution)/shard_map/pallas_call | solution.py:511
  18.3 0.5 %shard_map.73 = (f32[128,1024]{1,0:T(8,128)S(1)}, f32[128,1024]{1,0:T(8,128)S(1)}, f32[16,128]{1,0:T(8,128)S(1)}) custom-call(bf16[64,640]{1,0:T(8,128)(2,1)S(1)} %get-tuple-element.60.g_own, bf16[64,640]{1,0:T(8,128)(2,1)S(1)} %collective-permute-done.4.g_other, f32[128,1024]{1,0:T(8,128)S(1)} %get-tuple-element.62.e1, ...), custom_call_target="tpu_custom_call" | custom-call | bytes 1048576 | tf_op jit(solution)/shard_map/pallas_call | solution.py:521
  18.8 0.1 collective-permute-start.8
  18.8 1.2 %collective-permute-done.8.theirs = f32[16,128]{1,0:T(8,128)S(1)} collective-permute-done((f32[16,128]{1,0:T(8,128)S(1)}, f32[16,128]{1,0:T(8,128)S(1)}, u32[]{:S(2)}, u32[]{:S(2)}) %collective-permute-start.8) | collective-permute-done | bytes 8224 | tf_op jit(solution)/shard_map/ppermute | solution.py:468
  20.0 0.7 %shard_map.74 = (bf16[128,1024]{1,0:T(8,128)(2,1)S(1)}, bf16[128,1024]{1,0:T(8,128)(2,1)S(1)}, f32[8,128]{1,0:T(8,128)S(1)}, f32[8,128]{1,0:T(8,128)S(1)}, f32[1...) custom-call(bf16[64,640]{1,0:T(8,128)(2,1)S(1)} %get-tuple-element.4, ...), custom_call_target="tpu_custom_call" | custom-call | bytes 1048576 | tf_op jit(solution)/shard_map/pallas_call | solution.py:526
  20.7 1.6 %collective-permute-start.11 = (bf16[128,640]{1,0:T(8,128)(2,1)S(1)}, bf16[128,640]{1,0:T(8,128)(2,1)S(1)}, u32[]{:S(2)}, u32[]{:S(2)}) collective-permute-start(bf16[128,640]{1,0:T(8,128)(2,1)S(1)} %get-tuple-element.84), channel_id=1, source_target_pairs={{0,8},{4,12},{8,0},{12,4},{16,24},{20,28},{24,16},{28,20},{1,9},{5... | collective-permute-start | bytes 491528 | tf_op jit(solution)/shard_map/ppermute | solution.py:468
  22.3 0.5 %collective-permute-start.12 = (bf16[64,640]{1,0:T(8,128)(2,1)S(1)}, bf16[64,640]{1,0:T(8,128)(2,1)S(1)}, u32[]{:S(2)}, u32[]{:S(2)}) collective-permute-start(bf16[64,640]{1,0:T(8,128)(2,1)S(1)} %get-tuple-element.85), channel_id=1, source_target_pairs={{0,16},{4,20},{8,24},{12,28},{16,0},{20,4},{24,8},{28,12},{1,17},{... | collective-permute-start | bytes 245768 | tf_op jit(solution)/shard_map/ppermute | solution.py:468
  22.8 1.5 %collective-permute-start.13 = (bf16[64,640]{1,0:T(8,128)(2,1)S(1)}, bf16[64,640]{1,0:T(8,128)(2,1)S(1)}, u32[]{:S(2)}, u32[]{:S(2)}) collective-permute-start(bf16[64,640]{1,0:T(8,128)(2,1)S(1)} %get-tuple-element.86), channel_id=1, source_target_pairs={{0,24},{4,28},{8,16},{12,20},{16,8},{20,12},{24,0},{28,4},{1,25},{... | collective-permute-start | bytes 245768 | tf_op jit(solution)/shard_map/ppermute | solution.py:468
  24.3 0.5 %shard_map.76 = (f32[64,640]{1,0:T(8,128)S(1)}, bf16[32,640]{1,0:T(8,128)(2,1)S(1)}, bf16[32,640]{1,0:T(8,128)(2,1)S(1)}) custom-call(bf16[128,1024]{1,0:T(8,128)(2,1)S(1)} %get-tuple-element.77.ds1, bf16[128,1024]{1,0:T(8,128)(2,1)S(1)} %get-tuple-element.78.ds2, bf16[128,640]{1,0:T(8,128)(2,1)S(1)} %get-tuple-element.61.refs_0_, ...), custom_call_target="tpu_custom_call" | custom-call | bytes 1048576 | tf_op jit(solution)/shard_map/pallas_call | solution.py:534
  24.8 0.1 collective-permute-start.9
  24.8 0.5 %collective-permute-start.10 = (bf16[32,640]{1,0:T(8,128)(2,1)S(1)}, bf16[32,640]{1,0:T(8,128)(2,1)S(1)}, u32[]{:S(2)}, u32[]{:S(2)}) collective-permute-start(bf16[32,640]{1,0:T(8,128)(2,1)S(1)} %get-tuple-element.81), channel_id=1, source_target_pairs={{0,4},{4,0},{8,12},{12,8},{16,20},{20,16},{24,28},{28,24},{1,5},{5... | collective-permute-start | bytes 122888 | tf_op jit(solution)/shard_map/ppermute | solution.py:468
  25.3 1.4 %shard_map.75 = (f32[256,640]{1,0:T(8,128)S(1)}, f32[256,640]{1,0:T(8,128)S(1)}, f32[256,640]{1,0:T(8,128)S(1)}) custom-call(bf16[256,640]{1,0:T(8,128)(2,1)S(1)} %get-tuple-element.46.qp, bf16[256,640]{1,0:T(8,128)(2,1)S(1)} %get-tuple-element.47.kp, bf16[256,640]{1,0:T(8,128)(2,1)S(1)} %get-tuple-element.54.gp, f32[2048,256]{1,0:T(8,128)S(1)} %get-tuple-element.55.weight, ...), custom_call_target="tpu_custom_call" | custom-call | bytes 1048576 | tf_op jit(solution)/shard_map/pallas_call | solution.py:540
  26.7 1.1 %shard_map.77 = bf16[256,640]{1,0:T(8,128)(2,1)} custom-call(f32[256,640]{1,0:T(8,128)S(1)} %get-tuple-element.76.dq, f32[64,640]{1,0:T(8,128)S(1)} %get-tuple-element.79.dq_own, bf16[32,640]{1,0:T(8,128)(2,1)S(1)} %collective-permute-done.9.dq_low, bf16[32,640]{1,0:T(8,128)(2,1)S(1)} %collective-permute-done.10.dq_high), custom_call_target="tpu_custom_call" | custom-call | bytes 1048576 | tf_op jit(solution)/shard_map/pallas_call | solution.py:543
  27.8 1.1 %collective-permute-done.13.refs_2_ = bf16[64,640]{1,0:T(8,128)(2,1)S(1)} collective-permute-done((bf16[64,640]{1,0:T(8,128)(2,1)S(1)}, bf16[64,640]{1,0:T(8,128)(2,1)S(1)}, u32[]{:S(2)}, u32[]{:S(2)}) %collective-permute-start.13) | collective-permute-done | bytes 81952 | tf_op jit(solution)/shard_map/ppermute | solution.py:468
  28.9 1.3 %shard_map.78 = (bf16[256,640]{1,0:T(8,128)(2,1)}, bf16[256,640]{1,0:T(8,128)(2,1)}) custom-call(f32[256,640]{1,0:T(8,128)S(1)} %get-tuple-element.82.dk0, f32[256,640]{1,0:T(8,128)S(1)} %get-tuple-element.83.dv0, bf16[128,640]{1,0:T(8,128)(2,1)S(1)} %collective-permute-done.11.refs_0_, bf16[64,640]{1,0:T(8,128)(2,1)S(1)} %collective-permute-done.12.refs_1_, ...), custom_call_target="tpu_custom_call" | custom-call | bytes 1048576 | tf_op jit(solution)/shard_map/pallas_call | solution.py:544
  (8 shorter events, 0.0 us)
Async XLA Ops:
  2.6 7.5 %collective-permute-start = (bf16[64,640]{1,0:T(8,128)(2,1)S(1)}, bf16[64,640]{1,0:T(8,128)(2,1)S(1)}, u32[]{:S(2)}, u32[]{:S(2)}) collective-permute-start(bf16[64,640]{1,0:T(8,128)(2,1)S(1)} %get-tuple-element.48.q_own), channel_id=1, source_target_pairs={{0,4},{4,0},{8,12},{12,8},{16,20},{20,16},{24,28},{28,24},{1,5},{5... | collective-permute-start | bytes 245768 | tf_op jit(solution)/shard_map/ppermute | solution.py:468
  3.1 9.4 %collective-permute-start.1 = (bf16[64,640]{1,0:T(8,128)(2,1)S(1)}, bf16[64,640]{1,0:T(8,128)(2,1)S(1)}, u32[]{:S(2)}, u32[]{:S(2)}) collective-permute-start(bf16[64,640]{1,0:T(8,128)(2,1)S(1)} %get-tuple-element.50), channel_id=1, source_target_pairs={{0,3},{1,2},{2,1},{3,0},{4,7},{5,6},{6,5},{7,4},{8,11},{9,10},{10,... | collective-permute-start | bytes 245768 | tf_op jit(solution)/shard_map/ppermute | solution.py:468
  7.8 7.5 %collective-permute-start.2 = (bf16[64,640]{1,0:T(8,128)(2,1)S(1)}, bf16[64,640]{1,0:T(8,128)(2,1)S(1)}, u32[]{:S(2)}, u32[]{:S(2)}) collective-permute-start(bf16[64,640]{1,0:T(8,128)(2,1)S(1)} %get-tuple-element.51), channel_id=1, source_target_pairs={{0,2},{1,3},{2,0},{3,1},{4,6},{5,7},{6,4},{7,5},{8,10},{9,11},{10,... | collective-permute-start | bytes 245768 | tf_op jit(solution)/shard_map/ppermute | solution.py:468
  7.8 7.5 %collective-permute-start.3 = (bf16[64,640]{1,0:T(8,128)(2,1)S(1)}, bf16[64,640]{1,0:T(8,128)(2,1)S(1)}, u32[]{:S(2)}, u32[]{:S(2)}) collective-permute-start(bf16[64,640]{1,0:T(8,128)(2,1)S(1)} %get-tuple-element.52), channel_id=1, source_target_pairs={{0,1},{1,0},{2,3},{3,2},{4,5},{5,4},{6,7},{7,6},{8,9},{9,8},{10,11... | collective-permute-start | bytes 245768 | tf_op jit(solution)/shard_map/ppermute | solution.py:468
  8.4 7.8 %collective-permute-start.5 = (bf16[128,640]{1,0:T(8,128)(2,1)S(1)}, bf16[128,640]{1,0:T(8,128)(2,1)S(1)}, u32[]{:S(2)}, u32[]{:S(2)}) collective-permute-start(bf16[128,640]{1,0:T(8,128)(2,1)S(1)} %get-tuple-element.61.refs_0_), channel_id=1, source_target_pairs={{0,8},{4,12},{8,0},{12,4},{16,24},{20,28},{24,16},{28,20},{1,9},{5... | collective-permute-start | bytes 491528 | tf_op jit(solution)/shard_map/ppermute | solution.py:468
  10.0 7.1 %collective-permute-start.7 = (bf16[64,640]{1,0:T(8,128)(2,1)S(1)}, bf16[64,640]{1,0:T(8,128)(2,1)S(1)}, u32[]{:S(2)}, u32[]{:S(2)}) collective-permute-start(bf16[64,640]{1,0:T(8,128)(2,1)S(1)} %get-tuple-element.63), channel_id=1, source_target_pairs={{0,24},{4,28},{8,16},{12,20},{16,8},{20,12},{24,0},{28,4},{1,25},{... | collective-permute-start | bytes 245768 | tf_op jit(solution)/shard_map/ppermute | solution.py:468
  12.5 5.4 %collective-permute-start.6 = (bf16[64,640]{1,0:T(8,128)(2,1)S(1)}, bf16[64,640]{1,0:T(8,128)(2,1)S(1)}, u32[]{:S(2)}, u32[]{:S(2)}) collective-permute-start(bf16[64,640]{1,0:T(8,128)(2,1)S(1)} %get-tuple-element.63), channel_id=1, source_target_pairs={{0,16},{4,20},{8,24},{12,28},{16,0},{20,4},{24,8},{28,12},{1,17},{... | collective-permute-start | bytes 245768 | tf_op jit(solution)/shard_map/ppermute | solution.py:468
  15.5 2.7 %collective-permute-start.4 = (bf16[64,640]{1,0:T(8,128)(2,1)S(1)}, bf16[64,640]{1,0:T(8,128)(2,1)S(1)}, u32[]{:S(2)}, u32[]{:S(2)}) collective-permute-start(bf16[64,640]{1,0:T(8,128)(2,1)S(1)} %get-tuple-element.60.g_own), channel_id=1, source_target_pairs={{0,4},{4,0},{8,12},{12,8},{16,20},{20,16},{24,28},{28,24},{1,5},{5... | collective-permute-start | bytes 245768 | tf_op jit(solution)/shard_map/ppermute | solution.py:468
  18.8 1.2 %collective-permute-start.8 = (f32[16,128]{1,0:T(8,128)S(1)}, f32[16,128]{1,0:T(8,128)S(1)}, u32[]{:S(2)}, u32[]{:S(2)}) collective-permute-start(f32[16,128]{1,0:T(8,128)S(1)} %get-tuple-element.72.mine), channel_id=1, source_target_pairs={{0,4},{4,0},{8,12},{12,8},{16,20},{20,16},{24,28},{28,24},{1,5},{5... | collective-permute-start | bytes 24584 | tf_op jit(solution)/shard_map/ppermute | solution.py:468
  20.7 8.2 %collective-permute-start.11 = (bf16[128,640]{1,0:T(8,128)(2,1)S(1)}, bf16[128,640]{1,0:T(8,128)(2,1)S(1)}, u32[]{:S(2)}, u32[]{:S(2)}) collective-permute-start(bf16[128,640]{1,0:T(8,128)(2,1)S(1)} %get-tuple-element.84), channel_id=1, source_target_pairs={{0,8},{4,12},{8,0},{12,4},{16,24},{20,28},{24,16},{28,20},{1,9},{5... | collective-permute-start | bytes 491528 | tf_op jit(solution)/shard_map/ppermute | solution.py:468
  22.3 5.5 %collective-permute-start.12 = (bf16[64,640]{1,0:T(8,128)(2,1)S(1)}, bf16[64,640]{1,0:T(8,128)(2,1)S(1)}, u32[]{:S(2)}, u32[]{:S(2)}) collective-permute-start(bf16[64,640]{1,0:T(8,128)(2,1)S(1)} %get-tuple-element.85), channel_id=1, source_target_pairs={{0,16},{4,20},{8,24},{12,28},{16,0},{20,4},{24,8},{28,12},{1,17},{... | collective-permute-start | bytes 245768 | tf_op jit(solution)/shard_map/ppermute | solution.py:468
  22.8 6.1 %collective-permute-start.13 = (bf16[64,640]{1,0:T(8,128)(2,1)S(1)}, bf16[64,640]{1,0:T(8,128)(2,1)S(1)}, u32[]{:S(2)}, u32[]{:S(2)}) collective-permute-start(bf16[64,640]{1,0:T(8,128)(2,1)S(1)} %get-tuple-element.86), channel_id=1, source_target_pairs={{0,24},{4,28},{8,16},{12,20},{16,8},{20,12},{24,0},{28,4},{1,25},{... | collective-permute-start | bytes 245768 | tf_op jit(solution)/shard_map/ppermute | solution.py:468
  24.8 2.0 %collective-permute-start.9 = (bf16[32,640]{1,0:T(8,128)(2,1)S(1)}, bf16[32,640]{1,0:T(8,128)(2,1)S(1)}, u32[]{:S(2)}, u32[]{:S(2)}) collective-permute-start(bf16[32,640]{1,0:T(8,128)(2,1)S(1)} %get-tuple-element.80), channel_id=1, source_target_pairs={{0,4},{4,0},{8,12},{12,8},{16,20},{20,16},{24,28},{28,24},{1,5},{5... | collective-permute-start | bytes 122888 | tf_op jit(solution)/shard_map/ppermute | solution.py:468
  24.8 1.9 %collective-permute-start.10 = (bf16[32,640]{1,0:T(8,128)(2,1)S(1)}, bf16[32,640]{1,0:T(8,128)(2,1)S(1)}, u32[]{:S(2)}, u32[]{:S(2)}) collective-permute-start(bf16[32,640]{1,0:T(8,128)(2,1)S(1)} %get-tuple-element.81), channel_id=1, source_target_pairs={{0,4},{4,0},{8,12},{12,8},{16,20},{20,16},{24,28},{28,24},{1,5},{5... | collective-permute-start | bytes 122888 | tf_op jit(solution)/shard_map/ppermute | solution.py:468

commit v7 on v6

--- a/solution.py
+++ b/solution.py
@@ -71,9 +71,29 @@
     return (first_head(p) + iota((p.heads, 1), 0)) % p.r2
 
 
+def tiles(p):
+    out = []
+    for low in range(0, p.width, LANES):
+        high = min(low + LANES, p.width)
+        out.append((low, high, range(low // HD, -(-high // HD))))
+    return out
+
+
 def pick(p, whole, label):
     parts = []
     for t in range(p.turns):
+        if p.heads % p.r2 == 0:
+            lanes = []
+            for low, high, heads in tiles(p):
+                lane = low + iota((1, high - low), 1)
+                part = None
+                for h in heads:
+                    c = (h + DIL1 * t) % p.r2
+                    rows = whole[c * p.n2 : (c + 1) * p.n2, low:high]
+                    part = rows if part is None else jnp.where(lane >= h * HD, rows, part)
+                lanes.append(part)
+            parts.append(jnp.concatenate(lanes, axis=1))
+            continue
         want = (label + DIL1 * t) % p.r2
         part = jnp.zeros((p.n2, whole.shape[1]), F32)
         for c in range(p.r2):
@@ -85,7 +105,22 @@
 def spread(p, kept, label, base):
     parts = []
     for c in range(p.r2):
-        part = base[c * p.n2 : (c + 1) * p.n2]
+        rows = slice(c * p.n2, (c + 1) * p.n2)
+        if p.heads % p.r2 == 0:
+            lanes = []
+            for low, high, heads in tiles(p):
+                lane = low + iota((1, high - low), 1)
+                part = base[rows, low:high]
+                for t in range(p.turns):
+                    for h in heads:
+                        if (h + DIL1 * t) % p.r2 == c:
+                            hit = (lane >= h * HD) & (lane < (h + 1) * HD)
+                            moved = kept[t * p.n2 : (t + 1) * p.n2, low:high]
+                            part = jnp.where(hit, moved, part)
+                lanes.append(part)
+            parts.append(jnp.concatenate(lanes, axis=1))
+            continue
+        part = base[rows]
         for t in range(p.turns):
             hit = (label + DIL1 * t) % p.r2 == c
             part = jnp.where(hit, kept[t * p.n2 : (t + 1) * p.n2], part)

time: 30.3 us -> 30.2 us (level)
  transfers between devices with their start and end apart: 14 -> 14, of which waited for: 5 -> 5; matrix products, arithmetic and copies ran while one was open for 0% -> 0% of each run, Pallas kernels for 19% -> 18%
where the time goes in v7:
time: 30.2 us; the launch traced here: 30.1 us
  starting transfers between devices  13.7 us (45%)
  Pallas kernels  9.81 us (32%)
  waiting for transfers between devices  5.87 us (19%)
  between operations  0.76 us (3%)
    ppermute x14, starting transfers between devices, swap(): return lax.ppermute(block, axis, [(i, i ^ bits) for i in range(count)])  13.7 us
    ppermute x14, waiting for transfers between devices, swap(): return lax.ppermute(block, axis, [(i, i ^ bits) for i in range(count)])  5.87 us
    pallas_call x1, Pallas kernels, body(): call(run(pack_kernel), [(row, BF16)] * 3 + [(kept, BF16), ((2 * n1, width...  1.92 us
    pallas_call x1, Pallas kernels, body(): call(run(own_grad_kernel), [(row, F32)] * 3)  1.35 us
    pallas_call x1, Pallas kernels, body(): call(run(last_kernel), [(row, BF16)] * 2, [(row, BF16)] * 2 + [pltpu.Sema...  1.2 us
    pallas_call x1, Pallas kernels, body(): grad_q, = call(run(finish_kernel), [(row, BF16)])(dq, dq_own, *dq_came)  1.02 us
    pallas_call x1, Pallas kernels, body(): call(run(own_scores_kernel), [(flat(p.heads * tokens), F32), (stat, F32),...  0.95 us
    pallas_call x1, Pallas kernels, body(): call(run(levels_kernel), [(near, BF16), (wide, BF16), (stat1, F32), (stat...  0.71 us
  transfers between devices with their start and end apart: 14, of which 5 were waited for; matrix products, arithmetic and copies ran while one was open for 0% of the time, Pallas kernels for 18%

profile of v7, /device:TPU:0, one launch (start us, length us, event | category | flops | bytes accessed | tf_op | source)
XLA Modules:
  0.0 30.1 jit_solution(834216098897911829)
XLA Ops:
  0.6 1.9 %shard_map.67 = (bf16[256,640]{1,0:T(8,128)(2,1)S(1)}, bf16[256,640]{1,0:T(8,128)(2,1)S(1)}, bf16[256,640]{1,0:T(8,128)(2,1)S(1)}, bf16[64,640]{1,0:T(8,128)(2,1...) custom-call(bf16[256,640]{1,0:T(8,128)(2,1)} %q_ref.1, ...), custom_call_target="tpu_custom_call" | custom-call | bytes 1048576 | tf_op jit(solution)/shard_map/pallas_call | solution.py:523
  2.6 0.5 %collective-permute-start = (bf16[64,640]{1,0:T(8,128)(2,1)S(1)}, bf16[64,640]{1,0:T(8,128)(2,1)S(1)}, u32[]{:S(2)}, u32[]{:S(2)}) collective-permute-start(bf16[64,640]{1,0:T(8,128)(2,1)S(1)} %get-tuple-element.48.q_own), channel_id=1, source_target_pairs={{0,4},{4,0},{8,12},{12,8},{16,20},{20,16},{24,28},{28,24},{1,5},{5... | collective-permute-start | bytes 245768 | tf_op jit(solution)/shard_map/ppermute | solution.py:503
  3.1 4.7 %collective-permute-start.1 = (bf16[64,640]{1,0:T(8,128)(2,1)S(1)}, bf16[64,640]{1,0:T(8,128)(2,1)S(1)}, u32[]{:S(2)}, u32[]{:S(2)}) collective-permute-start(bf16[64,640]{1,0:T(8,128)(2,1)S(1)} %get-tuple-element.50), channel_id=1, source_target_pairs={{0,3},{1,2},{2,1},{3,0},{4,7},{5,6},{6,5},{7,4},{8,11},{9,10},{10,... | collective-permute-start | bytes 245768 | tf_op jit(solution)/shard_map/ppermute | solution.py:503
  7.8 0.0 collective-permute-start.2
  7.8 0.6 %collective-permute-start.3 = (bf16[64,640]{1,0:T(8,128)(2,1)S(1)}, bf16[64,640]{1,0:T(8,128)(2,1)S(1)}, u32[]{:S(2)}, u32[]{:S(2)}) collective-permute-start(bf16[64,640]{1,0:T(8,128)(2,1)S(1)} %get-tuple-element.52), channel_id=1, source_target_pairs={{0,1},{1,0},{2,3},{3,2},{4,5},{5,4},{6,7},{7,6},{8,9},{9,8},{10,11... | collective-permute-start | bytes 245768 | tf_op jit(solution)/shard_map/ppermute | solution.py:503
  8.4 1.6 %collective-permute-start.5 = (bf16[128,640]{1,0:T(8,128)(2,1)S(1)}, bf16[128,640]{1,0:T(8,128)(2,1)S(1)}, u32[]{:S(2)}, u32[]{:S(2)}) collective-permute-start(bf16[128,640]{1,0:T(8,128)(2,1)S(1)} %get-tuple-element.61.refs_0_), channel_id=1, source_target_pairs={{0,8},{4,12},{8,0},{12,4},{16,24},{20,28},{24,16},{28,20},{1,9},{5... | collective-permute-start | bytes 491528 | tf_op jit(solution)/shard_map/ppermute | solution.py:503
  10.0 0.0 collective-permute-done.after.q_other
  10.0 1.5 %collective-permute-start.7 = (bf16[64,640]{1,0:T(8,128)(2,1)S(1)}, bf16[64,640]{1,0:T(8,128)(2,1)S(1)}, u32[]{:S(2)}, u32[]{:S(2)}) collective-permute-start(bf16[64,640]{1,0:T(8,128)(2,1)S(1)} %get-tuple-element.63), channel_id=1, source_target_pairs={{0,24},{4,28},{8,16},{12,20},{16,8},{20,12},{24,0},{28,4},{1,25},{... | collective-permute-start | bytes 245768 | tf_op jit(solution)/shard_map/ppermute | solution.py:503
  11.5 0.9 %shard_map.68 = (f32[2048,256]{1,0:T(8,128)S(1)}, f32[8,256]{1,0:T(8,128)S(1)}, f32[8,128]{1,0:T(8,128)S(1)}) custom-call(bf16[256,640]{1,0:T(8,128)(2,1)S(1)} %get-tuple-element.46.qp, bf16[256,640]{1,0:T(8,128)(2,1)S(1)} %get-tuple-element.47.kp, bf16[64,640]{1,0:T(8,128)(2,1)S(1)} %collective-permute-done.after.q_other), custom_call_target="tpu_custom_call" | custom-call | bytes 1048576 | tf_op jit(solution)/shard_map/pallas_call | solution.py:538
  12.5 0.4 %collective-permute-start.6 = (bf16[64,640]{1,0:T(8,128)(2,1)S(1)}, bf16[64,640]{1,0:T(8,128)(2,1)S(1)}, u32[]{:S(2)}, u32[]{:S(2)}) collective-permute-start(bf16[64,640]{1,0:T(8,128)(2,1)S(1)} %get-tuple-element.63), channel_id=1, source_target_pairs={{0,16},{4,20},{8,24},{12,28},{16,0},{20,4},{24,8},{28,12},{1,17},{... | collective-permute-start | bytes 245768 | tf_op jit(solution)/shard_map/ppermute | solution.py:503
  12.9 2.3 %collective-permute-done.2.refs_1_ = bf16[64,640]{1,0:T(8,128)(2,1)S(1)} collective-permute-done((bf16[64,640]{1,0:T(8,128)(2,1)S(1)}, bf16[64,640]{1,0:T(8,128)(2,1)S(1)}, u32[]{:S(2)}, u32[]{:S(2)}) %collective-permute-start.2) | collective-permute-done | bytes 81952 | tf_op jit(solution)/shard_map/ppermute | solution.py:503
  15.2 0.3 %shard_map.69 = (bf16[256,640]{1,0:T(8,128)(2,1)S(1)}, bf16[64,640]{1,0:T(8,128)(2,1)S(1)}) custom-call(f32[8,128]{1,0:T(8,128)S(1)} %get-tuple-element.49.after.lse01, bf16[64,640]{1,0:T(8,128)(2,1)S(1)} %collective-permute-done.1.refs_0_, bf16[64,640]{1,0:T(8,128)(2,1)S(1)} %collective-permute-done.2.refs_1_, ...), custom_call_target="tpu_custom_call" | custom-call | bytes 1048576 | tf_op jit(solution)/shard_map/pallas_call | solution.py:549
  15.5 0.1 collective-permute-start.4
  15.6 0.6 %shard_map.70 = (f32[2048,256]{1,0:T(8,128)S(1)}, f32[8,256]{1,0:T(8,128)S(1)}, f32[8,128]{1,0:T(8,128)S(1)}) custom-call(bf16[256,640]{1,0:T(8,128)(2,1)S(1)} %get-tuple-element.56.vp, f32[2048,256]{1,0:T(8,128)S(1)} %get-tuple-element.55.weight, bf16[256,640]{1,0:T(8,128)(2,1)S(1)} %get-tuple-element.54.gp), custom_call_target="tpu_custom_call" | custom-call | bytes 1048576 | tf_op jit(solution)/shard_map/pallas_call | solution.py:553
  16.2 0.4 %shard_map.71 = (f32[128,1024]{1,0:T(8,128)S(1)}, f32[8,128]{1,0:T(8,128)S(1)}, f32[8,128]{1,0:T(8,128)S(1)}) custom-call(bf16[64,640]{1,0:T(8,128)(2,1)S(1)} %get-tuple-element.48.q_own, bf16[64,640]{1,0:T(8,128)(2,1)S(1)} %collective-permute-done.after.q_other, bf16[128,640]{1,0:T(8,128)(2,1)S(1)} %get-tuple-element.61.refs_0_, ...), custom_call_target="tpu_custom_call" | custom-call | bytes 1048576 | tf_op jit(solution)/shard_map/pallas_call | solution.py:543
  16.7 0.5 %collective-permute-done.7.refs_3_ = bf16[64,640]{1,0:T(8,128)(2,1)S(1)} collective-permute-done((bf16[64,640]{1,0:T(8,128)(2,1)S(1)}, bf16[64,640]{1,0:T(8,128)(2,1)S(1)}, u32[]{:S(2)}, u32[]{:S(2)}) %collective-permute-start.7) | collective-permute-done | bytes 81952 | tf_op jit(solution)/shard_map/ppermute | solution.py:503
  17.1 0.8 %collective-permute-done.6.refs_2_ = bf16[64,640]{1,0:T(8,128)(2,1)S(1)} collective-permute-done((bf16[64,640]{1,0:T(8,128)(2,1)S(1)}, bf16[64,640]{1,0:T(8,128)(2,1)S(1)}, u32[]{:S(2)}, u32[]{:S(2)}) %collective-permute-start.6) | collective-permute-done | bytes 81952 | tf_op jit(solution)/shard_map/ppermute | solution.py:503
  17.9 0.4 %shard_map.72 = (f32[128,1024]{1,0:T(8,128)S(1)}, f32[8,128]{1,0:T(8,128)S(1)}, f32[8,128]{1,0:T(8,128)S(1)}) custom-call(bf16[64,640]{1,0:T(8,128)(2,1)S(1)} %get-tuple-element.48.q_own, bf16[64,640]{1,0:T(8,128)(2,1)S(1)} %collective-permute-done.after.q_other, bf16[128,640]{1,0:T(8,128)(2,1)S(1)} %get-tuple-element.61.refs_0_, ...), custom_call_target="tpu_custom_call" | custom-call | bytes 1048576 | tf_op jit(solution)/shard_map/pallas_call | solution.py:546
  18.3 0.5 %shard_map.73 = (f32[128,1024]{1,0:T(8,128)S(1)}, f32[128,1024]{1,0:T(8,128)S(1)}, f32[16,128]{1,0:T(8,128)S(1)}) custom-call(bf16[64,640]{1,0:T(8,128)(2,1)S(1)} %get-tuple-element.60.g_own, bf16[64,640]{1,0:T(8,128)(2,1)S(1)} %collective-permute-done.4.g_other, f32[128,1024]{1,0:T(8,128)S(1)} %get-tuple-element.62.e1, ...), custom_call_target="tpu_custom_call" | custom-call | bytes 1048576 | tf_op jit(solution)/shard_map/pallas_call | solution.py:556
  18.8 0.1 collective-permute-start.8
  18.8 1.2 %collective-permute-done.8.theirs = f32[16,128]{1,0:T(8,128)S(1)} collective-permute-done((f32[16,128]{1,0:T(8,128)S(1)}, f32[16,128]{1,0:T(8,128)S(1)}, u32[]{:S(2)}, u32[]{:S(2)}) %collective-permute-start.8) | collective-permute-done | bytes 8224 | tf_op jit(solution)/shard_map/ppermute | solution.py:503
  20.0 0.7 %shard_map.74 = (bf16[128,1024]{1,0:T(8,128)(2,1)S(1)}, bf16[128,1024]{1,0:T(8,128)(2,1)S(1)}, f32[8,128]{1,0:T(8,128)S(1)}, f32[8,128]{1,0:T(8,128)S(1)}, f32[1...) custom-call(bf16[64,640]{1,0:T(8,128)(2,1)S(1)} %get-tuple-element.4, ...), custom_call_target="tpu_custom_call" | custom-call | bytes 1048576 | tf_op jit(solution)/shard_map/pallas_call | solution.py:561
  20.7 1.6 %collective-permute-start.11 = (bf16[128,640]{1,0:T(8,128)(2,1)S(1)}, bf16[128,640]{1,0:T(8,128)(2,1)S(1)}, u32[]{:S(2)}, u32[]{:S(2)}) collective-permute-start(bf16[128,640]{1,0:T(8,128)(2,1)S(1)} %get-tuple-element.84), channel_id=1, source_target_pairs={{0,8},{4,12},{8,0},{12,4},{16,24},{20,28},{24,16},{28,20},{1,9},{5... | collective-permute-start | bytes 491528 | tf_op jit(solution)/shard_map/ppermute | solution.py:503
  22.3 0.5 %collective-permute-start.12 = (bf16[64,640]{1,0:T(8,128)(2,1)S(1)}, bf16[64,640]{1,0:T(8,128)(2,1)S(1)}, u32[]{:S(2)}, u32[]{:S(2)}) collective-permute-start(bf16[64,640]{1,0:T(8,128)(2,1)S(1)} %get-tuple-element.85), channel_id=1, source_target_pairs={{0,16},{4,20},{8,24},{12,28},{16,0},{20,4},{24,8},{28,12},{1,17},{... | collective-permute-start | bytes 245768 | tf_op jit(solution)/shard_map/ppermute | solution.py:503
  22.8 1.5 %collective-permute-start.13 = (bf16[64,640]{1,0:T(8,128)(2,1)S(1)}, bf16[64,640]{1,0:T(8,128)(2,1)S(1)}, u32[]{:S(2)}, u32[]{:S(2)}) collective-permute-start(bf16[64,640]{1,0:T(8,128)(2,1)S(1)} %get-tuple-element.86), channel_id=1, source_target_pairs={{0,24},{4,28},{8,16},{12,20},{16,8},{20,12},{24,0},{28,4},{1,25},{... | collective-permute-start | bytes 245768 | tf_op jit(solution)/shard_map/ppermute | solution.py:503
  24.3 0.5 %shard_map.76 = (f32[64,640]{1,0:T(8,128)S(1)}, bf16[32,640]{1,0:T(8,128)(2,1)S(1)}, bf16[32,640]{1,0:T(8,128)(2,1)S(1)}) custom-call(bf16[128,1024]{1,0:T(8,128)(2,1)S(1)} %get-tuple-element.77.ds1, bf16[128,1024]{1,0:T(8,128)(2,1)S(1)} %get-tuple-element.78.ds2, bf16[128,640]{1,0:T(8,128)(2,1)S(1)} %get-tuple-element.61.refs_0_, ...), custom_call_target="tpu_custom_call" | custom-call | bytes 1048576 | tf_op jit(solution)/shard_map/pallas_call | solution.py:569
  24.8 0.1 collective-permute-start.9
  24.8 0.5 %collective-permute-start.10 = (bf16[32,640]{1,0:T(8,128)(2,1)S(1)}, bf16[32,640]{1,0:T(8,128)(2,1)S(1)}, u32[]{:S(2)}, u32[]{:S(2)}) collective-permute-start(bf16[32,640]{1,0:T(8,128)(2,1)S(1)} %get-tuple-element.81), channel_id=1, source_target_pairs={{0,4},{4,0},{8,12},{12,8},{16,20},{20,16},{24,28},{28,24},{1,5},{5... | collective-permute-start | bytes 122888 | tf_op jit(solution)/shard_map/ppermute | solution.py:503
  25.3 1.4 %shard_map.75 = (f32[256,640]{1,0:T(8,128)S(1)}, f32[256,640]{1,0:T(8,128)S(1)}, f32[256,640]{1,0:T(8,128)S(1)}) custom-call(bf16[256,640]{1,0:T(8,128)(2,1)S(1)} %get-tuple-element.46.qp, bf16[256,640]{1,0:T(8,128)(2,1)S(1)} %get-tuple-element.47.kp, bf16[256,640]{1,0:T(8,128)(2,1)S(1)} %get-tuple-element.54.gp, f32[2048,256]{1,0:T(8,128)S(1)} %get-tuple-element.55.weight, ...), custom_call_target="tpu_custom_call" | custom-call | bytes 1048576 | tf_op jit(solution)/shard_map/pallas_call | solution.py:575
  26.7 1.0 %shard_map.77 = bf16[256,640]{1,0:T(8,128)(2,1)} custom-call(f32[256,640]{1,0:T(8,128)S(1)} %get-tuple-element.76.dq, f32[64,640]{1,0:T(8,128)S(1)} %get-tuple-element.79.dq_own, bf16[32,640]{1,0:T(8,128)(2,1)S(1)} %collective-permute-done.9.dq_low, bf16[32,640]{1,0:T(8,128)(2,1)S(1)} %collective-permute-done.10.dq_high), custom_call_target="tpu_custom_call" | custom-call | bytes 1048576 | tf_op jit(solution)/shard_map/pallas_call | solution.py:578
  27.7 1.2 %collective-permute-done.13.refs_2_ = bf16[64,640]{1,0:T(8,128)(2,1)S(1)} collective-permute-done((bf16[64,640]{1,0:T(8,128)(2,1)S(1)}, bf16[64,640]{1,0:T(8,128)(2,1)S(1)}, u32[]{:S(2)}, u32[]{:S(2)}) %collective-permute-start.13) | collective-permute-done | bytes 81952 | tf_op jit(solution)/shard_map/ppermute | solution.py:503
  28.9 1.2 %shard_map.78 = (bf16[256,640]{1,0:T(8,128)(2,1)}, bf16[256,640]{1,0:T(8,128)(2,1)}) custom-call(f32[256,640]{1,0:T(8,128)S(1)} %get-tuple-element.82.dk0, f32[256,640]{1,0:T(8,128)S(1)} %get-tuple-element.83.dv0, bf16[128,640]{1,0:T(8,128)(2,1)S(1)} %collective-permute-done.11.refs_0_, bf16[64,640]{1,0:T(8,128)(2,1)S(1)} %collective-permute-done.12.refs_1_, ...), custom_call_target="tpu_custom_call" | custom-call | bytes 1048576 | tf_op jit(solution)/shard_map/pallas_call | solution.py:579
  (8 shorter events, 0.0 us)
Async XLA Ops:
  2.6 7.5 %collective-permute-start = (bf16[64,640]{1,0:T(8,128)(2,1)S(1)}, bf16[64,640]{1,0:T(8,128)(2,1)S(1)}, u32[]{:S(2)}, u32[]{:S(2)}) collective-permute-start(bf16[64,640]{1,0:T(8,128)(2,1)S(1)} %get-tuple-element.48.q_own), channel_id=1, source_target_pairs={{0,4},{4,0},{8,12},{12,8},{16,20},{20,16},{24,28},{28,24},{1,5},{5... | collective-permute-start | bytes 245768 | tf_op jit(solution)/shard_map/ppermute | solution.py:503
  3.1 9.4 %collective-permute-start.1 = (bf16[64,640]{1,0:T(8,128)(2,1)S(1)}, bf16[64,640]{1,0:T(8,128)(2,1)S(1)}, u32[]{:S(2)}, u32[]{:S(2)}) collective-permute-start(bf16[64,640]{1,0:T(8,128)(2,1)S(1)} %get-tuple-element.50), channel_id=1, source_target_pairs={{0,3},{1,2},{2,1},{3,0},{4,7},{5,6},{6,5},{7,4},{8,11},{9,10},{10,... | collective-permute-start | bytes 245768 | tf_op jit(solution)/shard_map/ppermute | solution.py:503
  7.8 7.5 %collective-permute-start.2 = (bf16[64,640]{1,0:T(8,128)(2,1)S(1)}, bf16[64,640]{1,0:T(8,128)(2,1)S(1)}, u32[]{:S(2)}, u32[]{:S(2)}) collective-permute-start(bf16[64,640]{1,0:T(8,128)(2,1)S(1)} %get-tuple-element.51), channel_id=1, source_target_pairs={{0,2},{1,3},{2,0},{3,1},{4,6},{5,7},{6,4},{7,5},{8,10},{9,11},{10,... | collective-permute-start | bytes 245768 | tf_op jit(solution)/shard_map/ppermute | solution.py:503
  7.8 7.5 %collective-permute-start.3 = (bf16[64,640]{1,0:T(8,128)(2,1)S(1)}, bf16[64,640]{1,0:T(8,128)(2,1)S(1)}, u32[]{:S(2)}, u32[]{:S(2)}) collective-permute-start(bf16[64,640]{1,0:T(8,128)(2,1)S(1)} %get-tuple-element.52), channel_id=1, source_target_pairs={{0,1},{1,0},{2,3},{3,2},{4,5},{5,4},{6,7},{7,6},{8,9},{9,8},{10,11... | collective-permute-start | bytes 245768 | tf_op jit(solution)/shard_map/ppermute | solution.py:503
  8.4 7.8 %collective-permute-start.5 = (bf16[128,640]{1,0:T(8,128)(2,1)S(1)}, bf16[128,640]{1,0:T(8,128)(2,1)S(1)}, u32[]{:S(2)}, u32[]{:S(2)}) collective-permute-start(bf16[128,640]{1,0:T(8,128)(2,1)S(1)} %get-tuple-element.61.refs_0_), channel_id=1, source_target_pairs={{0,8},{4,12},{8,0},{12,4},{16,24},{20,28},{24,16},{28,20},{1,9},{5... | collective-permute-start | bytes 491528 | tf_op jit(solution)/shard_map/ppermute | solution.py:503
  10.0 7.1 %collective-permute-start.7 = (bf16[64,640]{1,0:T(8,128)(2,1)S(1)}, bf16[64,640]{1,0:T(8,128)(2,1)S(1)}, u32[]{:S(2)}, u32[]{:S(2)}) collective-permute-start(bf16[64,640]{1,0:T(8,128)(2,1)S(1)} %get-tuple-element.63), channel_id=1, source_target_pairs={{0,24},{4,28},{8,16},{12,20},{16,8},{20,12},{24,0},{28,4},{1,25},{... | collective-permute-start | bytes 245768 | tf_op jit(solution)/shard_map/ppermute | solution.py:503
  12.5 5.4 %collective-permute-start.6 = (bf16[64,640]{1,0:T(8,128)(2,1)S(1)}, bf16[64,640]{1,0:T(8,128)(2,1)S(1)}, u32[]{:S(2)}, u32[]{:S(2)}) collective-permute-start(bf16[64,640]{1,0:T(8,128)(2,1)S(1)} %get-tuple-element.63), channel_id=1, source_target_pairs={{0,16},{4,20},{8,24},{12,28},{16,0},{20,4},{24,8},{28,12},{1,17},{... | collective-permute-start | bytes 245768 | tf_op jit(solution)/shard_map/ppermute | solution.py:503
  15.5 2.7 %collective-permute-start.4 = (bf16[64,640]{1,0:T(8,128)(2,1)S(1)}, bf16[64,640]{1,0:T(8,128)(2,1)S(1)}, u32[]{:S(2)}, u32[]{:S(2)}) collective-permute-start(bf16[64,640]{1,0:T(8,128)(2,1)S(1)} %get-tuple-element.60.g_own), channel_id=1, source_target_pairs={{0,4},{4,0},{8,12},{12,8},{16,20},{20,16},{24,28},{28,24},{1,5},{5... | collective-permute-start | bytes 245768 | tf_op jit(solution)/shard_map/ppermute | solution.py:503
  18.8 1.2 %collective-permute-start.8 = (f32[16,128]{1,0:T(8,128)S(1)}, f32[16,128]{1,0:T(8,128)S(1)}, u32[]{:S(2)}, u32[]{:S(2)}) collective-permute-start(f32[16,128]{1,0:T(8,128)S(1)} %get-tuple-element.72.mine), channel_id=1, source_target_pairs={{0,4},{4,0},{8,12},{12,8},{16,20},{20,16},{24,28},{28,24},{1,5},{5... | collective-permute-start | bytes 24584 | tf_op jit(solution)/shard_map/ppermute | solution.py:503
  20.7 8.2 %collective-permute-start.11 = (bf16[128,640]{1,0:T(8,128)(2,1)S(1)}, bf16[128,640]{1,0:T(8,128)(2,1)S(1)}, u32[]{:S(2)}, u32[]{:S(2)}) collective-permute-start(bf16[128,640]{1,0:T(8,128)(2,1)S(1)} %get-tuple-element.84), channel_id=1, source_target_pairs={{0,8},{4,12},{8,0},{12,4},{16,24},{20,28},{24,16},{28,20},{1,9},{5... | collective-permute-start | bytes 491528 | tf_op jit(solution)/shard_map/ppermute | solution.py:503
  22.3 5.5 %collective-permute-start.12 = (bf16[64,640]{1,0:T(8,128)(2,1)S(1)}, bf16[64,640]{1,0:T(8,128)(2,1)S(1)}, u32[]{:S(2)}, u32[]{:S(2)}) collective-permute-start(bf16[64,640]{1,0:T(8,128)(2,1)S(1)} %get-tuple-element.85), channel_id=1, source_target_pairs={{0,16},{4,20},{8,24},{12,28},{16,0},{20,4},{24,8},{28,12},{1,17},{... | collective-permute-start | bytes 245768 | tf_op jit(solution)/shard_map/ppermute | solution.py:503
  22.8 6.1 %collective-permute-start.13 = (bf16[64,640]{1,0:T(8,128)(2,1)S(1)}, bf16[64,640]{1,0:T(8,128)(2,1)S(1)}, u32[]{:S(2)}, u32[]{:S(2)}) collective-permute-start(bf16[64,640]{1,0:T(8,128)(2,1)S(1)} %get-tuple-element.86), channel_id=1, source_target_pairs={{0,24},{4,28},{8,16},{12,20},{16,8},{20,12},{24,0},{28,4},{1,25},{... | collective-permute-start | bytes 245768 | tf_op jit(solution)/shard_map/ppermute | solution.py:503
  24.8 1.9 %collective-permute-start.9 = (bf16[32,640]{1,0:T(8,128)(2,1)S(1)}, bf16[32,640]{1,0:T(8,128)(2,1)S(1)}, u32[]{:S(2)}, u32[]{:S(2)}) collective-permute-start(bf16[32,640]{1,0:T(8,128)(2,1)S(1)} %get-tuple-element.80), channel_id=1, source_target_pairs={{0,4},{4,0},{8,12},{12,8},{16,20},{20,16},{24,28},{28,24},{1,5},{5... | collective-permute-start | bytes 122888 | tf_op jit(solution)/shard_map/ppermute | solution.py:503
  24.8 1.9 %collective-permute-start.10 = (bf16[32,640]{1,0:T(8,128)(2,1)S(1)}, bf16[32,640]{1,0:T(8,128)(2,1)S(1)}, u32[]{:S(2)}, u32[]{:S(2)}) collective-permute-start(bf16[32,640]{1,0:T(8,128)(2,1)S(1)} %get-tuple-element.81), channel_id=1, source_target_pairs={{0,4},{4,0},{8,12},{12,8},{16,20},{20,16},{24,28},{28,24},{1,5},{5... | collective-permute-start | bytes 122888 | tf_op jit(solution)/shard_map/ppermute | solution.py:503

commit v8 on v7

--- a/solution.py
+++ b/solution.py
@@ -259,13 +259,18 @@
     lse01[...] = pick_stat(p, lse, LOWEST)
 
 
+def block_order(p):
+    half = p.zcount // 2
+    return [half, *range(1, half), *range(half + 1, p.zcount), 0]
+
+
 def gather_kernel(p, after, *refs):
     gz, (gp, g1, natural) = refs[: p.zcount], refs[p.zcount :]
     z = lax.axis_index("head")
     share = p.tokens // p.zcount
-    for b in range(p.zcount):
+    for b, ref in zip(block_order(p), gz):
         start = pl.multiple_of(jnp.bitwise_xor(z, b) * share, share)
-        natural[pl.ds(start, share), :] = gz[p.zcount - 1 - b][...]
+        natural[pl.ds(start, share), :] = ref[...]
     g = nn(phase_order(p), natural[...])
     gp[...] = g.astype(BF16)
     g1[...] = pick(p, g, column_class(p)).astype(BF16)
@@ -547,7 +552,7 @@
         q1, q_other, *kv
     )
     gp, g1 = call(run(gather_kernel), [(row, BF16), (kept, BF16)], [(row, BF16)])(
-        lse01, *gz[::-1]
+        lse01, *[gz[b] for b in block_order(p)]
     )
     g_other = swap(g1, "seq", 1)
     dprob, d0, d01 = call(

time: 30.2 us -> 30.1 us (level)
  waiting for transfers between devices: 5.87 us -> 5.13 us
  starting transfers between devices: 13.7 us -> 14.3 us
    ppermute x14, waiting for transfers between devices: 5.87 us -> 5.13 us  [swap(): return lax.ppermute(block, axis, [(i, i ^ bits) for i in range(count)])]
    ppermute x14, starting transfers between devices: 13.7 us -> 14.3 us  [swap(): return lax.ppermute(block, axis, [(i, i ^ bits) for i in range(count)])]
where the time goes in v8:
time: 30.1 us; the launch traced here: 30 us
  starting transfers between devices  14.3 us (48%)
  Pallas kernels  9.81 us (33%)
  waiting for transfers between devices  5.13 us (17%)
  between operations  0.76 us (3%)
    ppermute x14, starting transfers between devices, swap(): return lax.ppermute(block, axis, [(i, i ^ bits) for i in range(count)])  14.3 us
    ppermute x14, waiting for transfers between devices, swap(): return lax.ppermute(block, axis, [(i, i ^ bits) for i in range(count)])  5.13 us
    pallas_call x1, Pallas kernels, body(): call(run(pack_kernel), [(row, BF16)] * 3 + [(kept, BF16), ((2 * n1, width...  1.92 us
    pallas_call x1, Pallas kernels, body(): call(run(own_grad_kernel), [(row, F32)] * 3)  1.35 us
    pallas_call x1, Pallas kernels, body(): call(run(last_kernel), [(row, BF16)] * 2, [(row, BF16)] * 2 + [pltpu.Sema...  1.2 us
    pallas_call x1, Pallas kernels, body(): grad_q, = call(run(finish_kernel), [(row, BF16)])(dq, dq_own, *dq_came)  1.02 us
    pallas_call x1, Pallas kernels, body(): call(run(own_scores_kernel), [(flat(p.heads * tokens), F32), (stat, F32),...  0.95 us
    pallas_call x1, Pallas kernels, body(): call(run(levels_kernel), [(near, BF16), (wide, BF16), (stat1, F32), (stat...  0.71 us
  transfers between devices with their start and end apart: 14, of which 5 were waited for; matrix products, arithmetic and copies ran while one was open for 0% of the time, Pallas kernels for 18%

profile of v8, /device:TPU:0, one launch (start us, length us, event | category | flops | bytes accessed | tf_op | source)
XLA Modules:
  0.0 30.0 jit_solution(1517514399931661270)
XLA Ops:
  0.6 1.9 %shard_map.67 = (bf16[256,640]{1,0:T(8,128)(2,1)S(1)}, bf16[256,640]{1,0:T(8,128)(2,1)S(1)}, bf16[256,640]{1,0:T(8,128)(2,1)S(1)}, bf16[64,640]{1,0:T(8,128)(2,1...) custom-call(bf16[256,640]{1,0:T(8,128)(2,1)} %q_ref.1, ...), custom_call_target="tpu_custom_call" | custom-call | bytes 1048576 | tf_op jit(solution)/shard_map/pallas_call | solution.py:528
  2.6 0.5 %collective-permute-start = (bf16[64,640]{1,0:T(8,128)(2,1)S(1)}, bf16[64,640]{1,0:T(8,128)(2,1)S(1)}, u32[]{:S(2)}, u32[]{:S(2)}) collective-permute-start(bf16[64,640]{1,0:T(8,128)(2,1)S(1)} %get-tuple-element.48.q_own), channel_id=1, source_target_pairs={{0,4},{4,0},{8,12},{12,8},{16,20},{20,16},{24,28},{28,24},{1,5},{5... | collective-permute-start | bytes 245768 | tf_op jit(solution)/shard_map/ppermute | solution.py:508
  3.1 3.7 %collective-permute-start.1 = (bf16[64,640]{1,0:T(8,128)(2,1)S(1)}, bf16[64,640]{1,0:T(8,128)(2,1)S(1)}, u32[]{:S(2)}, u32[]{:S(2)}) collective-permute-start(bf16[64,640]{1,0:T(8,128)(2,1)S(1)} %get-tuple-element.50), channel_id=1, source_target_pairs={{0,2},{1,3},{2,0},{3,1},{4,6},{5,7},{6,4},{7,5},{8,10},{9,11},{10,... | collective-permute-start | bytes 245768 | tf_op jit(solution)/shard_map/ppermute | solution.py:508
  6.7 1.6 %collective-permute-start.2 = (bf16[64,640]{1,0:T(8,128)(2,1)S(1)}, bf16[64,640]{1,0:T(8,128)(2,1)S(1)}, u32[]{:S(2)}, u32[]{:S(2)}) collective-permute-start(bf16[64,640]{1,0:T(8,128)(2,1)S(1)} %get-tuple-element.51), channel_id=1, source_target_pairs={{0,1},{1,0},{2,3},{3,2},{4,5},{5,4},{6,7},{7,6},{8,9},{9,8},{10,11... | collective-permute-start | bytes 245768 | tf_op jit(solution)/shard_map/ppermute | solution.py:508
  8.3 0.0 collective-permute-start.3
  8.3 1.7 %collective-permute-start.5 = (bf16[128,640]{1,0:T(8,128)(2,1)S(1)}, bf16[128,640]{1,0:T(8,128)(2,1)S(1)}, u32[]{:S(2)}, u32[]{:S(2)}) collective-permute-start(bf16[128,640]{1,0:T(8,128)(2,1)S(1)} %get-tuple-element.61.refs_0_), channel_id=1, source_target_pairs={{0,8},{4,12},{8,0},{12,4},{16,24},{20,28},{24,16},{28,20},{1,9},{5... | collective-permute-start | bytes 491528 | tf_op jit(solution)/shard_map/ppermute | solution.py:508
  10.0 1.5 %collective-permute-start.7 = (bf16[64,640]{1,0:T(8,128)(2,1)S(1)}, bf16[64,640]{1,0:T(8,128)(2,1)S(1)}, u32[]{:S(2)}, u32[]{:S(2)}) collective-permute-start(bf16[64,640]{1,0:T(8,128)(2,1)S(1)} %get-tuple-element.63), channel_id=1, source_target_pairs={{0,24},{4,28},{8,16},{12,20},{16,8},{20,12},{24,0},{28,4},{1,25},{... | collective-permute-start | bytes 245768 | tf_op jit(solution)/shard_map/ppermute | solution.py:508
  11.5 0.9 %shard_map.68 = (f32[2048,256]{1,0:T(8,128)S(1)}, f32[8,256]{1,0:T(8,128)S(1)}, f32[8,128]{1,0:T(8,128)S(1)}) custom-call(bf16[256,640]{1,0:T(8,128)(2,1)S(1)} %get-tuple-element.46.qp, bf16[256,640]{1,0:T(8,128)(2,1)S(1)} %get-tuple-element.47.kp, bf16[64,640]{1,0:T(8,128)(2,1)S(1)} %collective-permute-done.after.q_other), custom_call_target="tpu_custom_call" | custom-call | bytes 1048576 | tf_op jit(solution)/shard_map/pallas_call | solution.py:543
  12.5 1.1 %collective-permute-start.6 = (bf16[64,640]{1,0:T(8,128)(2,1)S(1)}, bf16[64,640]{1,0:T(8,128)(2,1)S(1)}, u32[]{:S(2)}, u32[]{:S(2)}) collective-permute-start(bf16[64,640]{1,0:T(8,128)(2,1)S(1)} %get-tuple-element.63), channel_id=1, source_target_pairs={{0,16},{4,20},{8,24},{12,28},{16,0},{20,4},{24,8},{28,12},{1,17},{... | collective-permute-start | bytes 245768 | tf_op jit(solution)/shard_map/ppermute | solution.py:508
  13.6 1.0 %collective-permute-done.3.refs_2_ = bf16[64,640]{1,0:T(8,128)(2,1)S(1)} collective-permute-done((bf16[64,640]{1,0:T(8,128)(2,1)S(1)}, bf16[64,640]{1,0:T(8,128)(2,1)S(1)}, u32[]{:S(2)}, u32[]{:S(2)}) %collective-permute-start.3) | collective-permute-done | bytes 81952 | tf_op jit(solution)/shard_map/ppermute | solution.py:508
  14.6 0.3 %shard_map.69 = (bf16[256,640]{1,0:T(8,128)(2,1)S(1)}, bf16[64,640]{1,0:T(8,128)(2,1)S(1)}) custom-call(f32[8,128]{1,0:T(8,128)S(1)} %get-tuple-element.49.after.lse01, bf16[64,640]{1,0:T(8,128)(2,1)S(1)} %collective-permute-done.1.refs_0_, bf16[64,640]{1,0:T(8,128)(2,1)S(1)} %collective-permute-done.2.refs_1_, ...), custom_call_target="tpu_custom_call" | custom-call | bytes 1048576 | tf_op jit(solution)/shard_map/pallas_call | solution.py:554
  14.9 0.1 collective-permute-start.4
  15.0 0.6 %shard_map.70 = (f32[2048,256]{1,0:T(8,128)S(1)}, f32[8,256]{1,0:T(8,128)S(1)}, f32[8,128]{1,0:T(8,128)S(1)}) custom-call(bf16[256,640]{1,0:T(8,128)(2,1)S(1)} %get-tuple-element.56.vp, f32[2048,256]{1,0:T(8,128)S(1)} %get-tuple-element.55.weight, bf16[256,640]{1,0:T(8,128)(2,1)S(1)} %get-tuple-element.54.gp), custom_call_target="tpu_custom_call" | custom-call | bytes 1048576 | tf_op jit(solution)/shard_map/pallas_call | solution.py:558
  15.6 0.4 %shard_map.71 = (f32[128,1024]{1,0:T(8,128)S(1)}, f32[8,128]{1,0:T(8,128)S(1)}, f32[8,128]{1,0:T(8,128)S(1)}) custom-call(bf16[64,640]{1,0:T(8,128)(2,1)S(1)} %get-tuple-element.48.q_own, bf16[64,640]{1,0:T(8,128)(2,1)S(1)} %collective-permute-done.after.q_other, bf16[128,640]{1,0:T(8,128)(2,1)S(1)} %get-tuple-element.61.refs_0_, ...), custom_call_target="tpu_custom_call" | custom-call | bytes 1048576 | tf_op jit(solution)/shard_map/pallas_call | solution.py:548
  16.0 1.1 %collective-permute-done.7.refs_3_ = bf16[64,640]{1,0:T(8,128)(2,1)S(1)} collective-permute-done((bf16[64,640]{1,0:T(8,128)(2,1)S(1)}, bf16[64,640]{1,0:T(8,128)(2,1)S(1)}, u32[]{:S(2)}, u32[]{:S(2)}) %collective-permute-start.7) | collective-permute-done | bytes 81952 | tf_op jit(solution)/shard_map/ppermute | solution.py:508
  17.1 0.7 %collective-permute-done.6.refs_2_ = bf16[64,640]{1,0:T(8,128)(2,1)S(1)} collective-permute-done((bf16[64,640]{1,0:T(8,128)(2,1)S(1)}, bf16[64,640]{1,0:T(8,128)(2,1)S(1)}, u32[]{:S(2)}, u32[]{:S(2)}) %collective-permute-start.6) | collective-permute-done | bytes 81952 | tf_op jit(solution)/shard_map/ppermute | solution.py:508
  17.9 0.4 %shard_map.72 = (f32[128,1024]{1,0:T(8,128)S(1)}, f32[8,128]{1,0:T(8,128)S(1)}, f32[8,128]{1,0:T(8,128)S(1)}) custom-call(bf16[64,640]{1,0:T(8,128)(2,1)S(1)} %get-tuple-element.48.q_own, bf16[64,640]{1,0:T(8,128)(2,1)S(1)} %collective-permute-done.after.q_other, bf16[128,640]{1,0:T(8,128)(2,1)S(1)} %get-tuple-element.61.refs_0_, ...), custom_call_target="tpu_custom_call" | custom-call | bytes 1048576 | tf_op jit(solution)/shard_map/pallas_call | solution.py:551
  18.3 0.0 collective-permute-done.4.g_other
  18.3 0.5 %shard_map.73 = (f32[128,1024]{1,0:T(8,128)S(1)}, f32[128,1024]{1,0:T(8,128)S(1)}, f32[16,128]{1,0:T(8,128)S(1)}) custom-call(bf16[64,640]{1,0:T(8,128)(2,1)S(1)} %get-tuple-element.60.g_own, bf16[64,640]{1,0:T(8,128)(2,1)S(1)} %collective-permute-done.4.g_other, f32[128,1024]{1,0:T(8,128)S(1)} %get-tuple-element.62.e1, ...), custom_call_target="tpu_custom_call" | custom-call | bytes 1048576 | tf_op jit(solution)/shard_map/pallas_call | solution.py:561
  18.8 0.1 collective-permute-start.8
  18.8 1.2 %collective-permute-done.8.theirs = f32[16,128]{1,0:T(8,128)S(1)} collective-permute-done((f32[16,128]{1,0:T(8,128)S(1)}, f32[16,128]{1,0:T(8,128)S(1)}, u32[]{:S(2)}, u32[]{:S(2)}) %collective-permute-start.8) | collective-permute-done | bytes 8224 | tf_op jit(solution)/shard_map/ppermute | solution.py:508
  20.0 0.7 %shard_map.74 = (bf16[128,1024]{1,0:T(8,128)(2,1)S(1)}, bf16[128,1024]{1,0:T(8,128)(2,1)S(1)}, f32[8,128]{1,0:T(8,128)S(1)}, f32[8,128]{1,0:T(8,128)S(1)}, f32[1...) custom-call(bf16[64,640]{1,0:T(8,128)(2,1)S(1)} %get-tuple-element.4, ...), custom_call_target="tpu_custom_call" | custom-call | bytes 1048576 | tf_op jit(solution)/shard_map/pallas_call | solution.py:566
  20.7 1.6 %collective-permute-start.11 = (bf16[128,640]{1,0:T(8,128)(2,1)S(1)}, bf16[128,640]{1,0:T(8,128)(2,1)S(1)}, u32[]{:S(2)}, u32[]{:S(2)}) collective-permute-start(bf16[128,640]{1,0:T(8,128)(2,1)S(1)} %get-tuple-element.84), channel_id=1, source_target_pairs={{0,8},{4,12},{8,0},{12,4},{16,24},{20,28},{24,16},{28,20},{1,9},{5... | collective-permute-start | bytes 491528 | tf_op jit(solution)/shard_map/ppermute | solution.py:508
  22.3 0.5 %collective-permute-start.12 = (bf16[64,640]{1,0:T(8,128)(2,1)S(1)}, bf16[64,640]{1,0:T(8,128)(2,1)S(1)}, u32[]{:S(2)}, u32[]{:S(2)}) collective-permute-start(bf16[64,640]{1,0:T(8,128)(2,1)S(1)} %get-tuple-element.85), channel_id=1, source_target_pairs={{0,16},{4,20},{8,24},{12,28},{16,0},{20,4},{24,8},{28,12},{1,17},{... | collective-permute-start | bytes 245768 | tf_op jit(solution)/shard_map/ppermute | solution.py:508
  22.8 1.5 %collective-permute-start.13 = (bf16[64,640]{1,0:T(8,128)(2,1)S(1)}, bf16[64,640]{1,0:T(8,128)(2,1)S(1)}, u32[]{:S(2)}, u32[]{:S(2)}) collective-permute-start(bf16[64,640]{1,0:T(8,128)(2,1)S(1)} %get-tuple-element.86), channel_id=1, source_target_pairs={{0,24},{4,28},{8,16},{12,20},{16,8},{20,12},{24,0},{28,4},{1,25},{... | collective-permute-start | bytes 245768 | tf_op jit(solution)/shard_map/ppermute | solution.py:508
  24.3 0.5 %shard_map.76 = (f32[64,640]{1,0:T(8,128)S(1)}, bf16[32,640]{1,0:T(8,128)(2,1)S(1)}, bf16[32,640]{1,0:T(8,128)(2,1)S(1)}) custom-call(bf16[128,1024]{1,0:T(8,128)(2,1)S(1)} %get-tuple-element.77.ds1, bf16[128,1024]{1,0:T(8,128)(2,1)S(1)} %get-tuple-element.78.ds2, bf16[128,640]{1,0:T(8,128)(2,1)S(1)} %get-tuple-element.61.refs_0_, ...), custom_call_target="tpu_custom_call" | custom-call | bytes 1048576 | tf_op jit(solution)/shard_map/pallas_call | solution.py:574
  24.8 0.1 collective-permute-start.9
  24.8 0.5 %collective-permute-start.10 = (bf16[32,640]{1,0:T(8,128)(2,1)S(1)}, bf16[32,640]{1,0:T(8,128)(2,1)S(1)}, u32[]{:S(2)}, u32[]{:S(2)}) collective-permute-start(bf16[32,640]{1,0:T(8,128)(2,1)S(1)} %get-tuple-element.81), channel_id=1, source_target_pairs={{0,4},{4,0},{8,12},{12,8},{16,20},{20,16},{24,28},{28,24},{1,5},{5... | collective-permute-start | bytes 122888 | tf_op jit(solution)/shard_map/ppermute | solution.py:508
  25.3 1.4 %shard_map.75 = (f32[256,640]{1,0:T(8,128)S(1)}, f32[256,640]{1,0:T(8,128)S(1)}, f32[256,640]{1,0:T(8,128)S(1)}) custom-call(bf16[256,640]{1,0:T(8,128)(2,1)S(1)} %get-tuple-element.46.qp, bf16[256,640]{1,0:T(8,128)(2,1)S(1)} %get-tuple-element.47.kp, bf16[256,640]{1,0:T(8,128)(2,1)S(1)} %get-tuple-element.54.gp, f32[2048,256]{1,0:T(8,128)S(1)} %get-tuple-element.55.weight, ...), custom_call_target="tpu_custom_call" | custom-call | bytes 1048576 | tf_op jit(solution)/shard_map/pallas_call | solution.py:580
  26.7 1.0 %shard_map.77 = bf16[256,640]{1,0:T(8,128)(2,1)} custom-call(f32[256,640]{1,0:T(8,128)S(1)} %get-tuple-element.76.dq, f32[64,640]{1,0:T(8,128)S(1)} %get-tuple-element.79.dq_own, bf16[32,640]{1,0:T(8,128)(2,1)S(1)} %collective-permute-done.9.dq_low, bf16[32,640]{1,0:T(8,128)(2,1)S(1)} %collective-permute-done.10.dq_high), custom_call_target="tpu_custom_call" | custom-call | bytes 1048576 | tf_op jit(solution)/shard_map/pallas_call | solution.py:583
  27.7 1.1 %collective-permute-done.13.refs_2_ = bf16[64,640]{1,0:T(8,128)(2,1)S(1)} collective-permute-done((bf16[64,640]{1,0:T(8,128)(2,1)S(1)}, bf16[64,640]{1,0:T(8,128)(2,1)S(1)}, u32[]{:S(2)}, u32[]{:S(2)}) %collective-permute-start.13) | collective-permute-done | bytes 81952 | tf_op jit(solution)/shard_map/ppermute | solution.py:508
  28.8 1.2 %shard_map.78 = (bf16[256,640]{1,0:T(8,128)(2,1)}, bf16[256,640]{1,0:T(8,128)(2,1)}) custom-call(f32[256,640]{1,0:T(8,128)S(1)} %get-tuple-element.82.dk0, f32[256,640]{1,0:T(8,128)S(1)} %get-tuple-element.83.dv0, bf16[128,640]{1,0:T(8,128)(2,1)S(1)} %collective-permute-done.11.refs_0_, bf16[64,640]{1,0:T(8,128)(2,1)S(1)} %collective-permute-done.12.refs_1_, ...), custom_call_target="tpu_custom_call" | custom-call | bytes 1048576 | tf_op jit(solution)/shard_map/pallas_call | solution.py:584
  (8 shorter events, 0.0 us)
Async XLA Ops:
  2.6 7.5 %collective-permute-start = (bf16[64,640]{1,0:T(8,128)(2,1)S(1)}, bf16[64,640]{1,0:T(8,128)(2,1)S(1)}, u32[]{:S(2)}, u32[]{:S(2)}) collective-permute-start(bf16[64,640]{1,0:T(8,128)(2,1)S(1)} %get-tuple-element.48.q_own), channel_id=1, source_target_pairs={{0,4},{4,0},{8,12},{12,8},{16,20},{20,16},{24,28},{28,24},{1,5},{5... | collective-permute-start | bytes 245768 | tf_op jit(solution)/shard_map/ppermute | solution.py:508
  3.1 9.4 %collective-permute-start.1 = (bf16[64,640]{1,0:T(8,128)(2,1)S(1)}, bf16[64,640]{1,0:T(8,128)(2,1)S(1)}, u32[]{:S(2)}, u32[]{:S(2)}) collective-permute-start(bf16[64,640]{1,0:T(8,128)(2,1)S(1)} %get-tuple-element.50), channel_id=1, source_target_pairs={{0,2},{1,3},{2,0},{3,1},{4,6},{5,7},{6,4},{7,5},{8,10},{9,11},{10,... | collective-permute-start | bytes 245768 | tf_op jit(solution)/shard_map/ppermute | solution.py:508
  6.7 6.8 %collective-permute-start.2 = (bf16[64,640]{1,0:T(8,128)(2,1)S(1)}, bf16[64,640]{1,0:T(8,128)(2,1)S(1)}, u32[]{:S(2)}, u32[]{:S(2)}) collective-permute-start(bf16[64,640]{1,0:T(8,128)(2,1)S(1)} %get-tuple-element.51), channel_id=1, source_target_pairs={{0,1},{1,0},{2,3},{3,2},{4,5},{5,4},{6,7},{7,6},{8,9},{9,8},{10,11... | collective-permute-start | bytes 245768 | tf_op jit(solution)/shard_map/ppermute | solution.py:508
  8.3 6.3 %collective-permute-start.3 = (bf16[64,640]{1,0:T(8,128)(2,1)S(1)}, bf16[64,640]{1,0:T(8,128)(2,1)S(1)}, u32[]{:S(2)}, u32[]{:S(2)}) collective-permute-start(bf16[64,640]{1,0:T(8,128)(2,1)S(1)} %get-tuple-element.52), channel_id=1, source_target_pairs={{0,3},{1,2},{2,1},{3,0},{4,7},{5,6},{6,5},{7,4},{8,11},{9,10},{10,... | collective-permute-start | bytes 245768 | tf_op jit(solution)/shard_map/ppermute | solution.py:508
  8.3 7.3 %collective-permute-start.5 = (bf16[128,640]{1,0:T(8,128)(2,1)S(1)}, bf16[128,640]{1,0:T(8,128)(2,1)S(1)}, u32[]{:S(2)}, u32[]{:S(2)}) collective-permute-start(bf16[128,640]{1,0:T(8,128)(2,1)S(1)} %get-tuple-element.61.refs_0_), channel_id=1, source_target_pairs={{0,8},{4,12},{8,0},{12,4},{16,24},{20,28},{24,16},{28,20},{1,9},{5... | collective-permute-start | bytes 491528 | tf_op jit(solution)/shard_map/ppermute | solution.py:508
  10.0 7.1 %collective-permute-start.7 = (bf16[64,640]{1,0:T(8,128)(2,1)S(1)}, bf16[64,640]{1,0:T(8,128)(2,1)S(1)}, u32[]{:S(2)}, u32[]{:S(2)}) collective-permute-start(bf16[64,640]{1,0:T(8,128)(2,1)S(1)} %get-tuple-element.63), channel_id=1, source_target_pairs={{0,24},{4,28},{8,16},{12,20},{16,8},{20,12},{24,0},{28,4},{1,25},{... | collective-permute-start | bytes 245768 | tf_op jit(solution)/shard_map/ppermute | solution.py:508
  12.5 5.4 %collective-permute-start.6 = (bf16[64,640]{1,0:T(8,128)(2,1)S(1)}, bf16[64,640]{1,0:T(8,128)(2,1)S(1)}, u32[]{:S(2)}, u32[]{:S(2)}) collective-permute-start(bf16[64,640]{1,0:T(8,128)(2,1)S(1)} %get-tuple-element.63), channel_id=1, source_target_pairs={{0,16},{4,20},{8,24},{12,28},{16,0},{20,4},{24,8},{28,12},{1,17},{... | collective-permute-start | bytes 245768 | tf_op jit(solution)/shard_map/ppermute | solution.py:508
  14.9 3.3 %collective-permute-start.4 = (bf16[64,640]{1,0:T(8,128)(2,1)S(1)}, bf16[64,640]{1,0:T(8,128)(2,1)S(1)}, u32[]{:S(2)}, u32[]{:S(2)}) collective-permute-start(bf16[64,640]{1,0:T(8,128)(2,1)S(1)} %get-tuple-element.60.g_own), channel_id=1, source_target_pairs={{0,4},{4,0},{8,12},{12,8},{16,20},{20,16},{24,28},{28,24},{1,5},{5... | collective-permute-start | bytes 245768 | tf_op jit(solution)/shard_map/ppermute | solution.py:508
  18.8 1.2 %collective-permute-start.8 = (f32[16,128]{1,0:T(8,128)S(1)}, f32[16,128]{1,0:T(8,128)S(1)}, u32[]{:S(2)}, u32[]{:S(2)}) collective-permute-start(f32[16,128]{1,0:T(8,128)S(1)} %get-tuple-element.72.mine), channel_id=1, source_target_pairs={{0,4},{4,0},{8,12},{12,8},{16,20},{20,16},{24,28},{28,24},{1,5},{5... | collective-permute-start | bytes 24584 | tf_op jit(solution)/shard_map/ppermute | solution.py:508
  20.7 8.1 %collective-permute-start.11 = (bf16[128,640]{1,0:T(8,128)(2,1)S(1)}, bf16[128,640]{1,0:T(8,128)(2,1)S(1)}, u32[]{:S(2)}, u32[]{:S(2)}) collective-permute-start(bf16[128,640]{1,0:T(8,128)(2,1)S(1)} %get-tuple-element.84), channel_id=1, source_target_pairs={{0,8},{4,12},{8,0},{12,4},{16,24},{20,28},{24,16},{28,20},{1,9},{5... | collective-permute-start | bytes 491528 | tf_op jit(solution)/shard_map/ppermute | solution.py:508
  22.3 5.5 %collective-permute-start.12 = (bf16[64,640]{1,0:T(8,128)(2,1)S(1)}, bf16[64,640]{1,0:T(8,128)(2,1)S(1)}, u32[]{:S(2)}, u32[]{:S(2)}) collective-permute-start(bf16[64,640]{1,0:T(8,128)(2,1)S(1)} %get-tuple-element.85), channel_id=1, source_target_pairs={{0,16},{4,20},{8,24},{12,28},{16,0},{20,4},{24,8},{28,12},{1,17},{... | collective-permute-start | bytes 245768 | tf_op jit(solution)/shard_map/ppermute | solution.py:508
  22.8 6.0 %collective-permute-start.13 = (bf16[64,640]{1,0:T(8,128)(2,1)S(1)}, bf16[64,640]{1,0:T(8,128)(2,1)S(1)}, u32[]{:S(2)}, u32[]{:S(2)}) collective-permute-start(bf16[64,640]{1,0:T(8,128)(2,1)S(1)} %get-tuple-element.86), channel_id=1, source_target_pairs={{0,24},{4,28},{8,16},{12,20},{16,8},{20,12},{24,0},{28,4},{1,25},{... | collective-permute-start | bytes 245768 | tf_op jit(solution)/shard_map/ppermute | solution.py:508
  24.8 1.9 %collective-permute-start.9 = (bf16[32,640]{1,0:T(8,128)(2,1)S(1)}, bf16[32,640]{1,0:T(8,128)(2,1)S(1)}, u32[]{:S(2)}, u32[]{:S(2)}) collective-permute-start(bf16[32,640]{1,0:T(8,128)(2,1)S(1)} %get-tuple-element.80), channel_id=1, source_target_pairs={{0,4},{4,0},{8,12},{12,8},{16,20},{20,16},{24,28},{28,24},{1,5},{5... | collective-permute-start | bytes 122888 | tf_op jit(solution)/shard_map/ppermute | solution.py:508
  24.8 1.9 %collective-permute-start.10 = (bf16[32,640]{1,0:T(8,128)(2,1)S(1)}, bf16[32,640]{1,0:T(8,128)(2,1)S(1)}, u32[]{:S(2)}, u32[]{:S(2)}) collective-permute-start(bf16[32,640]{1,0:T(8,128)(2,1)S(1)} %get-tuple-element.81), channel_id=1, source_target_pairs={{0,4},{4,0},{8,12},{12,8},{16,20},{20,16},{24,28},{28,24},{1,5},{5... | collective-permute-start | bytes 122888 | tf_op jit(solution)/shard_map/ppermute | solution.py:508

commit v9 on v8

--- a/solution.py
+++ b/solution.py
@@ -242,21 +242,26 @@
         copy.wait()
 
 
-def own_scores_kernel(p, qp, kp, after, weight, lse0, lse01):
+def own_scores_kernel(p, first, end, qp, kp, after, weight, lse0):
     bias = own_bias(p)
     rows = []
-    for h in range(p.heads):
+    for h in range(first, end):
         low, high = window(h)
         mask = jnp.where(window_mask(h, low, high), 1.0, 0.0).astype(BF16)
         s = nt(kp[:, low:high], qp[:, low:high] * mask) * SCALE2 + bias
         top = jnp.max(s, axis=0, keepdims=True)
         e = jnp.exp2(s - top)
         denom = jnp.sum(e, axis=0, keepdims=True)
-        weight[h * p.tokens : (h + 1) * p.tokens, :] = e * (1.0 / denom)
+        at = (h - first) * p.tokens
+        weight[at : at + p.tokens, :] = e * (1.0 / denom)
         rows.append(top + jnp.log2(denom))
-    lse = jnp.concatenate(rows, axis=0)
-    lse0[...] = lse
-    lse01[...] = pick_stat(p, lse, LOWEST)
+    lse0[...] = jnp.concatenate(rows, axis=0)
+
+
+def own_weight(p, low, high, h):
+    half = p.heads // 2
+    ref, at = (low, h) if h < half else (high, h - half)
+    return ref[at * p.tokens : (at + 1) * p.tokens, :]
 
 
 def block_order(p):
@@ -276,7 +281,9 @@
     g1[...] = pick(p, g, column_class(p)).astype(BF16)
 
 
-def own_delta_kernel(p, vp, weight, gp, dprob, d0, d01):
+def own_delta_kernel(
+    p, vp, weight_a, weight_b, lse_a, lse_b, gp, dprob, d0, d01, lse0, lse01
+):
     sums = []
     for h in range(p.heads):
         low, high = window(h)
@@ -284,10 +291,14 @@
         mask = jnp.where(window_mask(h, low, high), 1.0, 0.0).astype(BF16)
         dp = nt(vp[:, low:high], gp[:, low:high] * mask)
         dprob[rows, :] = dp
-        sums.append(jnp.sum(weight[rows, :] * dp, axis=0, keepdims=True))
+        weight = own_weight(p, weight_a, weight_b, h)
+        sums.append(jnp.sum(weight * dp, axis=0, keepdims=True))
     d = jnp.concatenate(sums, axis=0)
     d0[...] = d
     d01[...] = pick_stat(p, d, 0.0)
+    lse = jnp.concatenate([lse_a[...], lse_b[...]], axis=0)
+    lse0[...] = lse
+    lse01[...] = pick_stat(p, lse, LOWEST)
 
 
 def cut(p, block, start, count):
@@ -452,7 +463,7 @@
 
 
 def own_grad_kernel(
-    p, qp, kp, gp, weight, dprob, lse0, d0, total1, delta1, own_part, dq, dk0, dv0
+    p, qp, kp, gp, weight_a, weight_b, dprob, lse0, d0, total1, delta1, own_part, dq, dk0, dv0
 ):
     lse = lse0[...]
     share = jnp.exp2(lse - spread_stat(p, total1[...], lse))
@@ -465,7 +476,7 @@
         rows = slice(h * p.tokens, (h + 1) * p.tokens)
         hit = window_mask(h, low, high)
         mask = jnp.where(hit, 1.0, 0.0).astype(BF16)
-        prob = weight[rows, :] * share[h : h + 1, :]
+        prob = own_weight(p, weight_a, weight_b, h) * share[h : h + 1, :]
         ds = (prob * (dprob[rows, :] - delta[h : h + 1, :]) * SCALE).astype(BF16)
         dq[:, low:high] = jnp.where(hit, tn(ds, kp[:, low:high]), dq[:, low:high])
         dk0[:, low:high] += nn(ds, qp[:, low:high] * mask)
@@ -540,9 +551,12 @@
     kv = [kv1] + [swap(kv1 if b < p.g1 else kv2, "seq", b) for b in even[1:]]
 
     q_other = swap(q1, "seq", 1)
-    weight, lse0, lse01 = call(
-        run(own_scores_kernel), [(flat(p.heads * tokens), F32), (stat, F32), (stat1, F32)]
-    )(qp, kp, q_other)
+    half = p.heads // 2
+    lows = [(flat(half * tokens), F32), ((half, tokens), F32)]
+    weight_a, lse_a = call(functools.partial(own_scores_kernel, p, 0, half), lows)(qp, kp, q_other)
+    weight_b, lse_b = call(functools.partial(own_scores_kernel, p, half, p.heads), lows)(
+        qp, kp, q_other
+    )
     near = (p.g1 // 2 * n1, 2 * p.heads * n1)
     wide = (p.g2 // 2 * n2, 2 * p.heads * n1)
     e1, top1, sum1 = call(run(near_kernel), [(near, F32)] + [(stat1, F32)] * 2)(
@@ -552,12 +566,13 @@
         q1, q_other, *kv
     )
     gp, g1 = call(run(gather_kernel), [(row, BF16), (kept, BF16)], [(row, BF16)])(
-        lse01, *[gz[b] for b in block_order(p)]
+        lse_a, *[gz[b] for b in block_order(p)]
     )
     g_other = swap(g1, "seq", 1)
-    dprob, d0, d01 = call(
-        run(own_delta_kernel), [(flat(p.heads * tokens), F32), (stat, F32), (stat1, F32)]
-    )(vp, weight, gp)
+    dprob, d0, d01, lse0, lse01 = call(
+        run(own_delta_kernel),
+        [(flat(p.heads * tokens), F32)] + [(stat, F32), (stat1, F32)] * 2,
+    )(vp, weight_a, weight_b, lse_a, lse_b, gp)
     dp1, dp2, mine = call(
         run(delta_kernel), [(near, F32), (wide, F32), ((2 * p.heads, 2 * n1), F32)]
     )(g1, g_other, e1, e2, top1, sum1, top2, sum2, lse01, d01, *kv)
@@ -578,7 +593,7 @@
     )(ds1, ds2, *kv)
     dq_came = [swap(half, "seq", 1) for half in dq_other]
     dq, dk0, dv0 = call(run(own_grad_kernel), [(row, F32)] * 3)(
-        qp, kp, gp, weight, dprob, lse0, d0, total1, delta1, own_part
+        qp, kp, gp, weight_a, weight_b, dprob, lse0, d0, total1, delta1, own_part
     )
     (grad_q,) = call(run(finish_kernel), [(row, BF16)])(dq, dq_own, *dq_came)
     grad_k, grad_v = call(

time: 30.1 us -> 30.1 us (level)
  waiting for transfers between devices: 5.13 us -> 4.61 us
  starting transfers between devices: 14.3 us -> 14.7 us
    ppermute x14, waiting for transfers between devices: 5.13 us -> 4.61 us  [swap(): return lax.ppermute(block, axis, [(i, i ^ bits) for i in range(count)])]
    ppermute x14, starting transfers between devices: 14.3 us -> 14.7 us  [swap(): return lax.ppermute(block, axis, [(i, i ^ bits) for i in range(count)])]
    pallas_call x2 -> x3, Pallas kernels: 1.54 us -> 1.63 us  [the longest x1 0.59 us: body(): call(run(own_delta_kernel), [(flat(p.heads * tokens), F32)] + [(stat, F32...]
  transfers between devices with their start and end apart: 14 -> 14, of which waited for: 5 -> 5; matrix products, arithmetic and copies ran while one was open for 0% -> 0% of each run, Pallas kernels for 18% -> 19%
where the time goes in v9:
time: 30.1 us; the launch traced here: 30 us
  starting transfers between devices  14.7 us (49%)
  Pallas kernels  9.88 us (33%)
  waiting for transfers between devices  4.61 us (15%)
  between operations  0.77 us (3%)
    ppermute x14, starting transfers between devices, swap(): return lax.ppermute(block, axis, [(i, i ^ bits) for i in range(count)])  14.7 us
    ppermute x14, waiting for transfers between devices, swap(): return lax.ppermute(block, axis, [(i, i ^ bits) for i in range(count)])  4.61 us
    pallas_call x1, Pallas kernels, body(): call(run(pack_kernel), [(row, BF16)] * 3 + [(kept, BF16), ((2 * n1, width...  1.92 us
    pallas_call x1, Pallas kernels, body(): call(run(own_grad_kernel), [(row, F32)] * 3)  1.35 us
    pallas_call x1, Pallas kernels, body(): call(run(last_kernel), [(row, BF16)] * 2, [(row, BF16)] * 2 + [pltpu.Sema...  1.2 us
    pallas_call x1, Pallas kernels, body(): grad_q, = call(run(finish_kernel), [(row, BF16)])(dq, dq_own, *dq_came)  1.02 us
    pallas_call x1, Pallas kernels, body(): call(run(levels_kernel), [(near, BF16), (wide, BF16), (stat1, F32), (stat...  0.69 us
  transfers between devices with their start and end apart: 14, of which 5 were waited for; matrix products, arithmetic and copies ran while one was open for 0% of the time, Pallas kernels for 19%

profile of v9, /device:TPU:0, one launch (start us, length us, event | category | flops | bytes accessed | tf_op | source)
XLA Modules:
  0.0 30.0 jit_solution(9459802202581782446)
XLA Ops:
  0.6 1.9 %shard_map.67 = (bf16[256,640]{1,0:T(8,128)(2,1)S(1)}, bf16[256,640]{1,0:T(8,128)(2,1)S(1)}, bf16[256,640]{1,0:T(8,128)(2,1)S(1)}, bf16[64,640]{1,0:T(8,128)(2,1...) custom-call(bf16[256,640]{1,0:T(8,128)(2,1)} %q_ref.1, ...), custom_call_target="tpu_custom_call" | custom-call | bytes 1048576 | tf_op jit(solution)/shard_map/pallas_call | solution.py:539
  2.6 0.5 %collective-permute-start = (bf16[64,640]{1,0:T(8,128)(2,1)S(1)}, bf16[64,640]{1,0:T(8,128)(2,1)S(1)}, u32[]{:S(2)}, u32[]{:S(2)}) collective-permute-start(bf16[64,640]{1,0:T(8,128)(2,1)S(1)} %get-tuple-element.51.q_own), channel_id=1, source_target_pairs={{0,4},{4,0},{8,12},{12,8},{16,20},{20,16},{24,28},{28,24},{1,5},{5... | collective-permute-start | bytes 245768 | tf_op jit(solution)/shard_map/ppermute | solution.py:519
  3.1 3.7 %collective-permute-start.1 = (bf16[64,640]{1,0:T(8,128)(2,1)S(1)}, bf16[64,640]{1,0:T(8,128)(2,1)S(1)}, u32[]{:S(2)}, u32[]{:S(2)}) collective-permute-start(bf16[64,640]{1,0:T(8,128)(2,1)S(1)} %get-tuple-element.53), channel_id=1, source_target_pairs={{0,2},{1,3},{2,0},{3,1},{4,6},{5,7},{6,4},{7,5},{8,10},{9,11},{10,... | collective-permute-start | bytes 245768 | tf_op jit(solution)/shard_map/ppermute | solution.py:519
  6.7 1.6 %collective-permute-start.2 = (bf16[64,640]{1,0:T(8,128)(2,1)S(1)}, bf16[64,640]{1,0:T(8,128)(2,1)S(1)}, u32[]{:S(2)}, u32[]{:S(2)}) collective-permute-start(bf16[64,640]{1,0:T(8,128)(2,1)S(1)} %get-tuple-element.54), channel_id=1, source_target_pairs={{0,1},{1,0},{2,3},{3,2},{4,5},{5,4},{6,7},{7,6},{8,9},{9,8},{10,11... | collective-permute-start | bytes 245768 | tf_op jit(solution)/shard_map/ppermute | solution.py:519
  8.3 1.7 %collective-permute-start.5 = (bf16[128,640]{1,0:T(8,128)(2,1)S(1)}, bf16[128,640]{1,0:T(8,128)(2,1)S(1)}, u32[]{:S(2)}, u32[]{:S(2)}) collective-permute-start(bf16[128,640]{1,0:T(8,128)(2,1)S(1)} %get-tuple-element.66.refs_0_), channel_id=1, source_target_pairs={{0,8},{4,12},{8,0},{12,4},{16,24},{20,28},{24,16},{28,20},{1,9},{5... | collective-permute-start | bytes 491528 | tf_op jit(solution)/shard_map/ppermute | solution.py:519
  10.0 0.0 collective-permute-done.after.q_other
  10.0 1.5 %collective-permute-start.7 = (bf16[64,640]{1,0:T(8,128)(2,1)S(1)}, bf16[64,640]{1,0:T(8,128)(2,1)S(1)}, u32[]{:S(2)}, u32[]{:S(2)}) collective-permute-start(bf16[64,640]{1,0:T(8,128)(2,1)S(1)} %get-tuple-element.68), channel_id=1, source_target_pairs={{0,24},{4,28},{8,16},{12,20},{16,8},{20,12},{24,0},{28,4},{1,25},{... | collective-permute-start | bytes 245768 | tf_op jit(solution)/shard_map/ppermute | solution.py:519
  11.5 0.5 %shard_map.68 = (f32[1024,256]{1,0:T(8,128)S(1)}, f32[4,256]{1,0:T(4,128)S(1)}) custom-call(bf16[256,640]{1,0:T(8,128)(2,1)S(1)} %get-tuple-element.49.qp, bf16[256,640]{1,0:T(8,128)(2,1)S(1)} %get-tuple-element.50.kp, bf16[64,640]{1,0:T(8,128)(2,1)S(1)} %collective-permute-done.after.q_other), custom_call_target="tpu_custom_call" | custom-call | bytes 1048576 | tf_op jit(solution)/shard_map/pallas_call | solution.py:556
  12.1 1.5 %collective-permute-start.6 = (bf16[64,640]{1,0:T(8,128)(2,1)S(1)}, bf16[64,640]{1,0:T(8,128)(2,1)S(1)}, u32[]{:S(2)}, u32[]{:S(2)}) collective-permute-start(bf16[64,640]{1,0:T(8,128)(2,1)S(1)} %get-tuple-element.68), channel_id=1, source_target_pairs={{0,16},{4,20},{8,24},{12,28},{16,0},{20,4},{24,8},{28,12},{1,17},{... | collective-permute-start | bytes 245768 | tf_op jit(solution)/shard_map/ppermute | solution.py:519
  13.6 1.0 %collective-permute-done.3.refs_2_ = bf16[64,640]{1,0:T(8,128)(2,1)S(1)} collective-permute-done((bf16[64,640]{1,0:T(8,128)(2,1)S(1)}, bf16[64,640]{1,0:T(8,128)(2,1)S(1)}, u32[]{:S(2)}, u32[]{:S(2)}) %collective-permute-start.3) | collective-permute-done | bytes 81952 | tf_op jit(solution)/shard_map/ppermute | solution.py:519
  14.6 0.3 %shard_map.69 = (bf16[256,640]{1,0:T(8,128)(2,1)S(1)}, bf16[64,640]{1,0:T(8,128)(2,1)S(1)}) custom-call(f32[4,256]{1,0:T(4,128)S(1)} %get-tuple-element.52.after.lse_a, bf16[64,640]{1,0:T(8,128)(2,1)S(1)} %collective-permute-done.1.refs_0_, bf16[64,640]{1,0:T(8,128)(2,1)S(1)} %collective-permute-done.2.refs_1_, ...), custom_call_target="tpu_custom_call" | custom-call | bytes 1048576 | tf_op jit(solution)/shard_map/pallas_call | solution.py:568
  14.9 0.1 collective-permute-start.4
  15.0 0.5 %shard_map.70 = (f32[1024,256]{1,0:T(8,128)S(1)}, f32[4,256]{1,0:T(4,128)S(1)}) custom-call(bf16[256,640]{1,0:T(8,128)(2,1)S(1)} %get-tuple-element.49.qp, bf16[256,640]{1,0:T(8,128)(2,1)S(1)} %get-tuple-element.50.kp, bf16[64,640]{1,0:T(8,128)(2,1)S(1)} %collective-permute-done.after.q_other), custom_call_target="tpu_custom_call" | custom-call | bytes 1048576 | tf_op jit(solution)/shard_map/pallas_call | solution.py:557
  15.5 0.6 %shard_map.71 = (f32[2048,256]{1,0:T(8,128)S(1)}, f32[8,256]{1,0:T(8,128)S(1)}, f32[8,128]{1,0:T(8,128)S(1)}, f32[8,256]{1,0:T(8,128)S(1)}, f32[8,128]{1,0:T(8,128)S(1)}) custom-call(bf16[256,640]{1,0:T(8,128)(2,1)S(1)} %get-tuple-element.60.vp, f32[1024,256]{1,0:T(8,128)S(1)} %get-tuple-element.58.weight_a, f32[1024,256]{1,0:T(8,128)S(1)} %get-tuple-element.59.weight_b, ...), custom_call_target="tpu_custom_call" | custom-call | bytes 1048576 | tf_op jit(solution)/shard_map/pallas_call | solution.py:572
  16.1 0.4 %shard_map.72 = (f32[128,1024]{1,0:T(8,128)S(1)}, f32[8,128]{1,0:T(8,128)S(1)}, f32[8,128]{1,0:T(8,128)S(1)}) custom-call(bf16[64,640]{1,0:T(8,128)(2,1)S(1)} %get-tuple-element.51.q_own, bf16[64,640]{1,0:T(8,128)(2,1)S(1)} %collective-permute-done.after.q_other, bf16[128,640]{1,0:T(8,128)(2,1)S(1)} %get-tuple-element.66.refs_0_, ...), custom_call_target="tpu_custom_call" | custom-call | bytes 1048576 | tf_op jit(solution)/shard_map/pallas_call | solution.py:562
  16.6 0.6 %collective-permute-done.7.refs_3_ = bf16[64,640]{1,0:T(8,128)(2,1)S(1)} collective-permute-done((bf16[64,640]{1,0:T(8,128)(2,1)S(1)}, bf16[64,640]{1,0:T(8,128)(2,1)S(1)}, u32[]{:S(2)}, u32[]{:S(2)}) %collective-permute-start.7) | collective-permute-done | bytes 81952 | tf_op jit(solution)/shard_map/ppermute | solution.py:519
  17.1 0.3 %collective-permute-done.6.refs_2_ = bf16[64,640]{1,0:T(8,128)(2,1)S(1)} collective-permute-done((bf16[64,640]{1,0:T(8,128)(2,1)S(1)}, bf16[64,640]{1,0:T(8,128)(2,1)S(1)}, u32[]{:S(2)}, u32[]{:S(2)}) %collective-permute-start.6) | collective-permute-done | bytes 81952 | tf_op jit(solution)/shard_map/ppermute | solution.py:519
  17.4 0.4 %shard_map.73 = (f32[128,1024]{1,0:T(8,128)S(1)}, f32[8,128]{1,0:T(8,128)S(1)}, f32[8,128]{1,0:T(8,128)S(1)}) custom-call(bf16[64,640]{1,0:T(8,128)(2,1)S(1)} %get-tuple-element.51.q_own, bf16[64,640]{1,0:T(8,128)(2,1)S(1)} %collective-permute-done.after.q_other, bf16[128,640]{1,0:T(8,128)(2,1)S(1)} %get-tuple-element.66.refs_0_, ...), custom_call_target="tpu_custom_call" | custom-call | bytes 1048576 | tf_op jit(solution)/shard_map/pallas_call | solution.py:565
  17.8 0.5 %shard_map.74 = (f32[128,1024]{1,0:T(8,128)S(1)}, f32[128,1024]{1,0:T(8,128)S(1)}, f32[16,128]{1,0:T(8,128)S(1)}) custom-call(bf16[64,640]{1,0:T(8,128)(2,1)S(1)} %get-tuple-element.65.g_own, bf16[64,640]{1,0:T(8,128)(2,1)S(1)} %collective-permute-done.4.g_other, f32[128,1024]{1,0:T(8,128)S(1)} %get-tuple-element.67.e1, ...), custom_call_target="tpu_custom_call" | custom-call | bytes 1048576 | tf_op jit(solution)/shard_map/pallas_call | solution.py:576
  18.3 0.1 collective-permute-start.8
  18.4 1.2 %collective-permute-done.8.theirs = f32[16,128]{1,0:T(8,128)S(1)} collective-permute-done((f32[16,128]{1,0:T(8,128)S(1)}, f32[16,128]{1,0:T(8,128)S(1)}, u32[]{:S(2)}, u32[]{:S(2)}) %collective-permute-start.8) | collective-permute-done | bytes 8224 | tf_op jit(solution)/shard_map/ppermute | solution.py:519
  19.6 0.7 %shard_map.75 = (bf16[128,1024]{1,0:T(8,128)(2,1)S(1)}, bf16[128,1024]{1,0:T(8,128)(2,1)S(1)}, f32[8,128]{1,0:T(8,128)S(1)}, f32[8,128]{1,0:T(8,128)S(1)}, f32[1...) custom-call(bf16[64,640]{1,0:T(8,128)(2,1)S(1)} %get-tuple-element.5, ...), custom_call_target="tpu_custom_call" | custom-call | bytes 1048576 | tf_op jit(solution)/shard_map/pallas_call | solution.py:581
  20.3 1.6 %collective-permute-start.11 = (bf16[128,640]{1,0:T(8,128)(2,1)S(1)}, bf16[128,640]{1,0:T(8,128)(2,1)S(1)}, u32[]{:S(2)}, u32[]{:S(2)}) collective-permute-start(bf16[128,640]{1,0:T(8,128)(2,1)S(1)} %get-tuple-element.90), channel_id=1, source_target_pairs={{0,8},{4,12},{8,0},{12,4},{16,24},{20,28},{24,16},{28,20},{1,9},{5... | collective-permute-start | bytes 491528 | tf_op jit(solution)/shard_map/ppermute | solution.py:519
  21.8 1.0 %collective-permute-start.12 = (bf16[64,640]{1,0:T(8,128)(2,1)S(1)}, bf16[64,640]{1,0:T(8,128)(2,1)S(1)}, u32[]{:S(2)}, u32[]{:S(2)}) collective-permute-start(bf16[64,640]{1,0:T(8,128)(2,1)S(1)} %get-tuple-element.91), channel_id=1, source_target_pairs={{0,16},{4,20},{8,24},{12,28},{16,0},{20,4},{24,8},{28,12},{1,17},{... | collective-permute-start | bytes 245768 | tf_op jit(solution)/shard_map/ppermute | solution.py:519
  22.8 1.0 %collective-permute-start.13 = (bf16[64,640]{1,0:T(8,128)(2,1)S(1)}, bf16[64,640]{1,0:T(8,128)(2,1)S(1)}, u32[]{:S(2)}, u32[]{:S(2)}) collective-permute-start(bf16[64,640]{1,0:T(8,128)(2,1)S(1)} %get-tuple-element.92), channel_id=1, source_target_pairs={{0,24},{4,28},{8,16},{12,20},{16,8},{20,12},{24,0},{28,4},{1,25},{... | collective-permute-start | bytes 245768 | tf_op jit(solution)/shard_map/ppermute | solution.py:519
  23.8 0.5 %shard_map.77 = (f32[64,640]{1,0:T(8,128)S(1)}, bf16[32,640]{1,0:T(8,128)(2,1)S(1)}, bf16[32,640]{1,0:T(8,128)(2,1)S(1)}) custom-call(bf16[128,1024]{1,0:T(8,128)(2,1)S(1)} %get-tuple-element.83.ds1, bf16[128,1024]{1,0:T(8,128)(2,1)S(1)} %get-tuple-element.84.ds2, bf16[128,640]{1,0:T(8,128)(2,1)S(1)} %get-tuple-element.66.refs_0_, ...), custom_call_target="tpu_custom_call" | custom-call | bytes 1048576 | tf_op jit(solution)/shard_map/pallas_call | solution.py:589
  24.3 0.1 collective-permute-start.9
  24.4 0.5 %collective-permute-start.10 = (bf16[32,640]{1,0:T(8,128)(2,1)S(1)}, bf16[32,640]{1,0:T(8,128)(2,1)S(1)}, u32[]{:S(2)}, u32[]{:S(2)}) collective-permute-start(bf16[32,640]{1,0:T(8,128)(2,1)S(1)} %get-tuple-element.87), channel_id=1, source_target_pairs={{0,4},{4,0},{8,12},{12,8},{16,20},{20,16},{24,28},{28,24},{1,5},{5... | collective-permute-start | bytes 122888 | tf_op jit(solution)/shard_map/ppermute | solution.py:519
  24.9 1.4 %shard_map.76 = (f32[256,640]{1,0:T(8,128)S(1)}, f32[256,640]{1,0:T(8,128)S(1)}, f32[256,640]{1,0:T(8,128)S(1)}) custom-call(bf16[256,640]{1,0:T(8,128)(2,1)S(1)} %get-tuple-element.49.qp, bf16[256,640]{1,0:T(8,128)(2,1)S(1)} %get-tuple-element.50.kp, bf16[256,640]{1,0:T(8,128)(2,1)S(1)} %get-tuple-element.57.gp, ...), custom_call_target="tpu_custom_call" | custom-call | bytes 1048576 | tf_op jit(solution)/shard_map/pallas_call | solution.py:595
  26.3 1.0 %shard_map.78 = bf16[256,640]{1,0:T(8,128)(2,1)} custom-call(f32[256,640]{1,0:T(8,128)S(1)} %get-tuple-element.82.dq, f32[64,640]{1,0:T(8,128)S(1)} %get-tuple-element.85.dq_own, bf16[32,640]{1,0:T(8,128)(2,1)S(1)} %collective-permute-done.9.dq_low, bf16[32,640]{1,0:T(8,128)(2,1)S(1)} %collective-permute-done.10.dq_high), custom_call_target="tpu_custom_call" | custom-call | bytes 1048576 | tf_op jit(solution)/shard_map/pallas_call | solution.py:598
  27.3 1.5 %collective-permute-done.13.refs_2_ = bf16[64,640]{1,0:T(8,128)(2,1)S(1)} collective-permute-done((bf16[64,640]{1,0:T(8,128)(2,1)S(1)}, bf16[64,640]{1,0:T(8,128)(2,1)S(1)}, u32[]{:S(2)}, u32[]{:S(2)}) %collective-permute-start.13) | collective-permute-done | bytes 81952 | tf_op jit(solution)/shard_map/ppermute | solution.py:519
  28.8 1.2 %shard_map.79 = (bf16[256,640]{1,0:T(8,128)(2,1)}, bf16[256,640]{1,0:T(8,128)(2,1)}) custom-call(f32[256,640]{1,0:T(8,128)S(1)} %get-tuple-element.88.dk0, f32[256,640]{1,0:T(8,128)S(1)} %get-tuple-element.89.dv0, bf16[128,640]{1,0:T(8,128)(2,1)S(1)} %collective-permute-done.11.refs_0_, bf16[64,640]{1,0:T(8,128)(2,1)S(1)} %collective-permute-done.12.refs_1_, ...), custom_call_target="tpu_custom_call" | custom-call | bytes 1048576 | tf_op jit(solution)/shard_map/pallas_call | solution.py:599
  (9 shorter events, 0.0 us)
Async XLA Ops:
  2.6 7.5 %collective-permute-start = (bf16[64,640]{1,0:T(8,128)(2,1)S(1)}, bf16[64,640]{1,0:T(8,128)(2,1)S(1)}, u32[]{:S(2)}, u32[]{:S(2)}) collective-permute-start(bf16[64,640]{1,0:T(8,128)(2,1)S(1)} %get-tuple-element.51.q_own), channel_id=1, source_target_pairs={{0,4},{4,0},{8,12},{12,8},{16,20},{20,16},{24,28},{28,24},{1,5},{5... | collective-permute-start | bytes 245768 | tf_op jit(solution)/shard_map/ppermute | solution.py:519
  3.1 9.0 %collective-permute-start.1 = (bf16[64,640]{1,0:T(8,128)(2,1)S(1)}, bf16[64,640]{1,0:T(8,128)(2,1)S(1)}, u32[]{:S(2)}, u32[]{:S(2)}) collective-permute-start(bf16[64,640]{1,0:T(8,128)(2,1)S(1)} %get-tuple-element.53), channel_id=1, source_target_pairs={{0,2},{1,3},{2,0},{3,1},{4,6},{5,7},{6,4},{7,5},{8,10},{9,11},{10,... | collective-permute-start | bytes 245768 | tf_op jit(solution)/shard_map/ppermute | solution.py:519
  6.7 6.8 %collective-permute-start.2 = (bf16[64,640]{1,0:T(8,128)(2,1)S(1)}, bf16[64,640]{1,0:T(8,128)(2,1)S(1)}, u32[]{:S(2)}, u32[]{:S(2)}) collective-permute-start(bf16[64,640]{1,0:T(8,128)(2,1)S(1)} %get-tuple-element.54), channel_id=1, source_target_pairs={{0,1},{1,0},{2,3},{3,2},{4,5},{5,4},{6,7},{7,6},{8,9},{9,8},{10,11... | collective-permute-start | bytes 245768 | tf_op jit(solution)/shard_map/ppermute | solution.py:519
  8.3 6.3 %collective-permute-start.3 = (bf16[64,640]{1,0:T(8,128)(2,1)S(1)}, bf16[64,640]{1,0:T(8,128)(2,1)S(1)}, u32[]{:S(2)}, u32[]{:S(2)}) collective-permute-start(bf16[64,640]{1,0:T(8,128)(2,1)S(1)} %get-tuple-element.55), channel_id=1, source_target_pairs={{0,3},{1,2},{2,1},{3,0},{4,7},{5,6},{6,5},{7,4},{8,11},{9,10},{10,... | collective-permute-start | bytes 245768 | tf_op jit(solution)/shard_map/ppermute | solution.py:519
  8.3 7.8 %collective-permute-start.5 = (bf16[128,640]{1,0:T(8,128)(2,1)S(1)}, bf16[128,640]{1,0:T(8,128)(2,1)S(1)}, u32[]{:S(2)}, u32[]{:S(2)}) collective-permute-start(bf16[128,640]{1,0:T(8,128)(2,1)S(1)} %get-tuple-element.66.refs_0_), channel_id=1, source_target_pairs={{0,8},{4,12},{8,0},{12,4},{16,24},{20,28},{24,16},{28,20},{1,9},{5... | collective-permute-start | bytes 491528 | tf_op jit(solution)/shard_map/ppermute | solution.py:519
  10.0 7.1 %collective-permute-start.7 = (bf16[64,640]{1,0:T(8,128)(2,1)S(1)}, bf16[64,640]{1,0:T(8,128)(2,1)S(1)}, u32[]{:S(2)}, u32[]{:S(2)}) collective-permute-start(bf16[64,640]{1,0:T(8,128)(2,1)S(1)} %get-tuple-element.68), channel_id=1, source_target_pairs={{0,24},{4,28},{8,16},{12,20},{16,8},{20,12},{24,0},{28,4},{1,25},{... | collective-permute-start | bytes 245768 | tf_op jit(solution)/shard_map/ppermute | solution.py:519
  12.1 5.4 %collective-permute-start.6 = (bf16[64,640]{1,0:T(8,128)(2,1)S(1)}, bf16[64,640]{1,0:T(8,128)(2,1)S(1)}, u32[]{:S(2)}, u32[]{:S(2)}) collective-permute-start(bf16[64,640]{1,0:T(8,128)(2,1)S(1)} %get-tuple-element.68), channel_id=1, source_target_pairs={{0,16},{4,20},{8,24},{12,28},{16,0},{20,4},{24,8},{28,12},{1,17},{... | collective-permute-start | bytes 245768 | tf_op jit(solution)/shard_map/ppermute | solution.py:519
  14.9 2.9 %collective-permute-start.4 = (bf16[64,640]{1,0:T(8,128)(2,1)S(1)}, bf16[64,640]{1,0:T(8,128)(2,1)S(1)}, u32[]{:S(2)}, u32[]{:S(2)}) collective-permute-start(bf16[64,640]{1,0:T(8,128)(2,1)S(1)} %get-tuple-element.65.g_own), channel_id=1, source_target_pairs={{0,4},{4,0},{8,12},{12,8},{16,20},{20,16},{24,28},{28,24},{1,5},{5... | collective-permute-start | bytes 245768 | tf_op jit(solution)/shard_map/ppermute | solution.py:519
  18.3 1.2 %collective-permute-start.8 = (f32[16,128]{1,0:T(8,128)S(1)}, f32[16,128]{1,0:T(8,128)S(1)}, u32[]{:S(2)}, u32[]{:S(2)}) collective-permute-start(f32[16,128]{1,0:T(8,128)S(1)} %get-tuple-element.78.mine), channel_id=1, source_target_pairs={{0,4},{4,0},{8,12},{12,8},{16,20},{20,16},{24,28},{28,24},{1,5},{5... | collective-permute-start | bytes 24584 | tf_op jit(solution)/shard_map/ppermute | solution.py:519
  20.3 8.5 %collective-permute-start.11 = (bf16[128,640]{1,0:T(8,128)(2,1)S(1)}, bf16[128,640]{1,0:T(8,128)(2,1)S(1)}, u32[]{:S(2)}, u32[]{:S(2)}) collective-permute-start(bf16[128,640]{1,0:T(8,128)(2,1)S(1)} %get-tuple-element.90), channel_id=1, source_target_pairs={{0,8},{4,12},{8,0},{12,4},{16,24},{20,28},{24,16},{28,20},{1,9},{5... | collective-permute-start | bytes 491528 | tf_op jit(solution)/shard_map/ppermute | solution.py:519
  21.8 5.5 %collective-permute-start.12 = (bf16[64,640]{1,0:T(8,128)(2,1)S(1)}, bf16[64,640]{1,0:T(8,128)(2,1)S(1)}, u32[]{:S(2)}, u32[]{:S(2)}) collective-permute-start(bf16[64,640]{1,0:T(8,128)(2,1)S(1)} %get-tuple-element.91), channel_id=1, source_target_pairs={{0,16},{4,20},{8,24},{12,28},{16,0},{20,4},{24,8},{28,12},{1,17},{... | collective-permute-start | bytes 245768 | tf_op jit(solution)/shard_map/ppermute | solution.py:519
  22.8 6.0 %collective-permute-start.13 = (bf16[64,640]{1,0:T(8,128)(2,1)S(1)}, bf16[64,640]{1,0:T(8,128)(2,1)S(1)}, u32[]{:S(2)}, u32[]{:S(2)}) collective-permute-start(bf16[64,640]{1,0:T(8,128)(2,1)S(1)} %get-tuple-element.92), channel_id=1, source_target_pairs={{0,24},{4,28},{8,16},{12,20},{16,8},{20,12},{24,0},{28,4},{1,25},{... | collective-permute-start | bytes 245768 | tf_op jit(solution)/shard_map/ppermute | solution.py:519
  24.3 1.9 %collective-permute-start.9 = (bf16[32,640]{1,0:T(8,128)(2,1)S(1)}, bf16[32,640]{1,0:T(8,128)(2,1)S(1)}, u32[]{:S(2)}, u32[]{:S(2)}) collective-permute-start(bf16[32,640]{1,0:T(8,128)(2,1)S(1)} %get-tuple-element.86), channel_id=1, source_target_pairs={{0,4},{4,0},{8,12},{12,8},{16,20},{20,16},{24,28},{28,24},{1,5},{5... | collective-permute-start | bytes 122888 | tf_op jit(solution)/shard_map/ppermute | solution.py:519
  24.4 1.9 %collective-permute-start.10 = (bf16[32,640]{1,0:T(8,128)(2,1)S(1)}, bf16[32,640]{1,0:T(8,128)(2,1)S(1)}, u32[]{:S(2)}, u32[]{:S(2)}) collective-permute-start(bf16[32,640]{1,0:T(8,128)(2,1)S(1)} %get-tuple-element.87), channel_id=1, source_target_pairs={{0,4},{4,0},{8,12},{12,8},{16,20},{20,16},{24,28},{28,24},{1,5},{5... | collective-permute-start | bytes 122888 | tf_op jit(solution)/shard_map/ppermute | solution.py:519
